TPU v7x, 32 devices: a whole 2x2x4 slice. The times are simulated.
32 devices in a mesh: expert: 8 (over z, x), tensor: 4 (over y, core).
Axes of the slice: x: 2, y: 2, z: 4, core: 2. Of those that a mesh axis runs over, the one named last changes fastest.
Arguments:
- activations: bfloat16 [8192, 1536], P('expert'), may hold values from -6 to 6
- cotangent: bfloat16 [8192, 1536], P('expert'), may hold values from -6 to 6
- block_ids: int32 [8, 1024], P('expert'), may hold values from 0 to 7, never falling along the last dimension, each value on 1 to 256 neighbouring positions
- expert_ids: int32 [8192, 8], P('expert'), may hold values from 0 to 15, as said below
- route_ranks: int32 [8192, 8], P('expert'), may hold values from 0 to 1023, as said below
- attention_gain: bfloat16 [1536], replicated, may hold values from 0.25 to 1.75
- query_weight: bfloat16 [1536, 1536], P(None, 'tensor'), may hold values from -0.15625 to 0.15625
- key_matrix: bfloat16 [1536, 512], P(None, 'tensor'), may hold values from -0.15625 to 0.15625
- value_matrix: bfloat16 [1536, 512], P(None, 'tensor'), may hold values from -0.15625 to 0.15625
- output_weight: bfloat16 [1536, 1536], P('tensor'), may hold values from -1.25 to 1.25
- mixture_gain: bfloat16 [1536], replicated, may hold values from 0.25 to 1.75
- router_weight: bfloat16 [1536, 16], replicated, may hold values from -0.078125 to 0.078125
- expert_gate: bfloat16 [16, 1536, 512], P('expert', None, 'tensor'), may hold values from -0.15625 to 0.15625
- expert_up: bfloat16 [16, 1536, 512], P('expert', None, 'tensor'), may hold values from -0.15625 to 0.15625
- expert_down: bfloat16 [16, 512, 1536], P('expert', 'tensor'), may hold values from -1.5 to 1.5
Outputs:
- output: bfloat16 [8192, 1536], P('expert')
- input_gradient: float32 [8192, 1536], P('expert')
- attention_gain_gradient: float32 [1536], replicated
- query_weight_gradient: float32 [1536, 1536], P(None, 'tensor')
- key_weight_gradient: float32 [1536, 512], P(None, 'tensor')
- value_weight_gradient: float32 [1536, 512], P(None, 'tensor')
- output_weight_gradient: float32 [1536, 1536], P('tensor')
- mixture_gain_gradient: float32 [1536], replicated
- router_weight_gradient: float32 [1536, 16], replicated
- expert_gate_gradient: float32 [16, 1536, 512], P('expert', None, 'tensor')
- expert_up_gradient: float32 [16, 1536, 512], P('expert', None, 'tensor')
- expert_down_gradient: float32 [16, 512, 1536], P('expert', 'tensor')
Inputs may be any that keep to these rules, and one draw needn't show every extreme that they name: `expert_ids`: each row names 8 different experts. route_ranks[t, k] is the place of pair (t, k) among the pairs of the same 1024 tokens of one index of the expert axis that name the same expert, in a route order drawn from the seed: for each such index and expert the places are 0, 1, 2, ... without gaps. `block_ids`: each row numbers the blocks of one sequence from 0 upward, never falling; every number occurs, on at most 256 positions.
All inputs are finite; a program needn't handle non-finite values.
Results may differ from a plain program's by a relative error of at most 0.024.
Values may be sent and summed in bfloat16 or wider, within the bound.
No kernel may reach another device: no remote copies, remote signals or barrier semaphores. Data moves between devices by JAX's collectives and lax.ppermute only.
A program may use at most 192 MiB of HBM per device.

v0:
```python
import math

import jax
import jax.numpy as jnp
from jax import lax
from jax.sharding import PartitionSpec as P

HEAD_WIDTH = 64


EPSILON = 1e-05
NEGATIVE = -1e30


def normalize(values, gain_vector):
    inverse = lax.rsqrt(jnp.mean(values * values, axis=-1, keepdims=True) + EPSILON)
    return (values * inverse * gain_vector, inverse)


def normalize_back(values, inverse, gain_vector, gradient):
    normed = values * inverse
    scaled = gradient * gain_vector
    d_values = inverse * (scaled - normed * jnp.mean(scaled * normed, axis=-1, keepdims=True))
    return (d_values, gradient * normed)


def rope_tables(sequence_length, head_size):
    half_width = head_size // 2
    frequency = jnp.exp(
        jnp.arange(half_width, dtype=jnp.float32) * (-2.0 * math.log(10000.0) / head_size)
    )
    angles = jnp.arange(sequence_length, dtype=jnp.float32)[:, None] * frequency[None, :]
    return (jnp.cos(angles), jnp.sin(angles))


def apply_rotation(values, cosine_table, sine_lookup):
    half_width = values.shape[-1] // 2
    first_half = values[..., :half_width]
    second_half = values[..., half_width:]
    cosine_rows = cosine_table[:, None, :]
    sine_rows = sine_lookup[:, None, :]
    return jnp.concatenate(
        [
            first_half * cosine_rows - second_half * sine_rows,
            second_half * cosine_rows + first_half * sine_rows,
        ],
        axis=-1,
    )


def rotate_back(values, cosine_table, sine_lookup):
    half_width = values.shape[-1] // 2
    first_half = values[..., :half_width]
    second_half = values[..., half_width:]
    cosine_rows = cosine_table[:, None, :]
    sine_rows = sine_lookup[:, None, :]
    return jnp.concatenate(
        [
            first_half * cosine_rows + second_half * sine_rows,
            second_half * cosine_rows - first_half * sine_rows,
        ],
        axis=-1,
    )


def block_scores(part_queries, keys_rot, blocks, part_blocks, scale):
    scores = (
        jnp.einsum("qkgd,skd->kgqs", part_queries, keys_rot, preferred_element_type=jnp.float32)
        * scale
    )
    visible = blocks[None, :] <= part_blocks[:, None]
    return jnp.where(visible, scores, NEGATIVE)


def attention_forward(queries_rot, keys_rot, values_low, blocks, block_rows, scale):
    block_count = queries_rot.shape[0] // block_rows

    def one_block(block_index):
        offset = block_index * block_rows
        part_queries = lax.dynamic_slice_in_dim(queries_rot, offset, block_rows, 0)
        part_blocks = lax.dynamic_slice_in_dim(blocks, offset, block_rows, 0)
        scores = block_scores(part_queries, keys_rot, blocks, part_blocks, scale)
        row_peak = jnp.max(scores, axis=-1, keepdims=True)
        exponent = jnp.exp(scores - row_peak)
        summed = jnp.sum(exponent, axis=-1, keepdims=True)
        weights = (exponent / summed).astype(jnp.bfloat16)
        mixture = jnp.einsum(
            "kgqs,skd->qkgd", weights, values_low, preferred_element_type=jnp.float32
        )
        return (mixture.astype(jnp.bfloat16), row_peak + jnp.log(summed))

    mixture, log_sums = lax.map(one_block, jnp.arange(block_count, dtype=jnp.int32))
    return (mixture.reshape(queries_rot.shape), log_sums)


def attention_backward(
    queries_rot, keys_rot, values_low, blocks, log_sums, d_mixture, block_rows, scale
):
    block_count = queries_rot.shape[0] // block_rows

    def one_block(running, pieces):
        d_keys, d_values = running
        block_index, log_sum = pieces
        offset = block_index * block_rows
        part_queries = lax.dynamic_slice_in_dim(queries_rot, offset, block_rows, 0)
        part_blocks = lax.dynamic_slice_in_dim(blocks, offset, block_rows, 0)
        part_grads = lax.dynamic_slice_in_dim(d_mixture, offset, block_rows, 0)
        scores = block_scores(part_queries, keys_rot, blocks, part_blocks, scale)
        weights = jnp.exp(scores - log_sum)
        weights_low = weights.astype(jnp.bfloat16)
        d_weights = jnp.einsum(
            "qkgd,skd->kgqs", part_grads, values_low, preferred_element_type=jnp.float32
        )
        row_delta = jnp.sum(weights * d_weights, axis=-1, keepdims=True)
        d_scores = (weights * (d_weights - row_delta)).astype(jnp.bfloat16)
        d_queries = (
            jnp.einsum("kgqs,skd->qkgd", d_scores, keys_rot, preferred_element_type=jnp.float32)
            * scale
        )
        d_keys = (
            d_keys
            + jnp.einsum(
                "kgqs,qkgd->skd", d_scores, part_queries, preferred_element_type=jnp.float32
            )
            * scale
        )
        d_values = d_values + jnp.einsum(
            "kgqs,qkgd->skd", weights_low, part_grads, preferred_element_type=jnp.float32
        )
        return ((d_keys, d_values), d_queries)

    zeros_kv = jnp.zeros(keys_rot.shape, jnp.float32)
    (d_keys, d_values), d_queries = lax.scan(
        one_block, (zeros_kv, zeros_kv), (jnp.arange(block_count, dtype=jnp.int32), log_sums)
    )
    return (d_queries.reshape(queries_rot.shape), d_keys, d_values)


def router_back(gates_now, d_gates_now, mask_now, d_moe_now, router_weight):
    d_chosen = gates_now * (d_gates_now - jnp.sum(gates_now * d_gates_now, axis=-1, keepdims=True))
    d_logits = jnp.sum(jnp.where(mask_now, d_chosen[:, :, None], 0.0), axis=1).astype(jnp.bfloat16)
    d_hidden = d_moe_now + jnp.einsum(
        "te,de->td", d_logits, router_weight, preferred_element_type=jnp.float32
    )
    return (d_logits, d_hidden)


def shards(
    activations,
    cotangent,
    block_ids,
    expert_ids,
    route_ranks,
    attention_gain,
    query_weight,
    key_matrix,
    value_matrix,
    output_weight,
    mixture_gain,
    router_weight,
    expert_gate,
    expert_up,
    expert_down,
):
    sequence_length = activations.shape[0]
    width = activations.shape[1]
    query_heads = query_weight.shape[1] // HEAD_WIDTH
    group_heads = key_matrix.shape[1] // HEAD_WIDTH
    group_size = query_heads // group_heads
    tensor_count = lax.axis_size("tensor")
    owner_count = lax.axis_size("expert")
    tensor_index = lax.axis_index("tensor")
    num_experts = router_weight.shape[1]
    local_experts = expert_gate.shape[0]
    picks = expert_ids.shape[1]
    capacity = sequence_length * picks // num_experts
    share = capacity // tensor_count
    slot_count = share * num_experts
    rows_share = sequence_length // tensor_count
    row_offset = tensor_index * rows_share
    block_rows = min(512, sequence_length)
    scale = HEAD_WIDTH ** (-0.5)
    blocks = block_ids[0]
    cosine_table, sine_lookup = rope_tables(sequence_length, HEAD_WIDTH)
    residual_in = activations.astype(jnp.float32)
    gain_first = attention_gain.astype(jnp.float32)
    normed_first, inverse_first = normalize(residual_in, gain_first)
    hidden_first = normed_first.astype(jnp.bfloat16)
    query_rows = jnp.dot(hidden_first, query_weight, preferred_element_type=jnp.float32).reshape(
        sequence_length, query_heads, HEAD_WIDTH
    )
    keys_unrotated = jnp.dot(hidden_first, key_matrix, preferred_element_type=jnp.float32).reshape(
        sequence_length, group_heads, HEAD_WIDTH
    )
    values_low = (
        jnp.dot(hidden_first, value_matrix, preferred_element_type=jnp.float32)
        .astype(jnp.bfloat16)
        .reshape(sequence_length, group_heads, HEAD_WIDTH)
    )
    queries_rot = (
        apply_rotation(query_rows, cosine_table, sine_lookup)
        .astype(jnp.bfloat16)
        .reshape(sequence_length, group_heads, group_size, HEAD_WIDTH)
    )
    keys_rot = apply_rotation(keys_unrotated, cosine_table, sine_lookup).astype(jnp.bfloat16)
    mixture, log_sums = attention_forward(
        queries_rot, keys_rot, values_low, blocks, block_rows, scale
    )
    mixture_flat = mixture.reshape(sequence_length, query_heads * HEAD_WIDTH)
    partial_out = jnp.dot(mixture_flat, output_weight, preferred_element_type=jnp.float32)
    gain_second = mixture_gain.astype(jnp.float32)
    attention_out = lax.psum(partial_out, "tensor")
    residual_mid = residual_in + attention_out
    normed_second, inverse_second = normalize(residual_mid, gain_second)
    hidden_second = normed_second.astype(jnp.bfloat16)
    logits = jnp.dot(hidden_second, router_weight, preferred_element_type=jnp.float32)
    expert_range = jnp.arange(num_experts, dtype=jnp.int32)
    picked_mask = expert_ids[:, :, None] == expert_range[None, None, :]
    chosen = jnp.sum(jnp.where(picked_mask, logits[:, None, :], 0.0), axis=-1)
    gate_values = jax.nn.softmax(chosen, axis=-1)
    gates_low = gate_values.astype(jnp.bfloat16)
    local_rank = route_ranks - tensor_index * share
    in_share = (local_rank >= 0) & (local_rank < share)
    slot_index = jnp.where(in_share, local_rank * num_experts + expert_ids, slot_count)
    slot_range = jnp.arange(slot_count, dtype=jnp.int32)
    matches = [
        slot_index[:, pick_index, None] == slot_range[None, :] for pick_index in range(picks)
    ]
    selector = jnp.zeros((sequence_length, slot_count), jnp.float32)
    gate_table = jnp.zeros((sequence_length, slot_count), jnp.float32)
    for pick_index in range(picks):
        selector = selector + matches[pick_index]
        gate_table = gate_table + jnp.where(
            matches[pick_index], gates_low[:, pick_index, None].astype(jnp.float32), 0.0
        )
    selector = selector.astype(jnp.bfloat16)
    gate_table = gate_table.astype(jnp.bfloat16)
    send_rows = jnp.einsum(
        "ts,td->sd", selector, hidden_second, preferred_element_type=jnp.float32
    ).astype(jnp.bfloat16)
    send_rows = send_rows.reshape(share, owner_count, local_experts, width)
    arrived = lax.all_to_all(send_rows, "expert", split_axis=1, concat_axis=1, tiled=True)
    gate_full, up_full, down_full = (
        lax.all_gather(expert_gate, "tensor", axis=2, tiled=True),
        lax.all_gather(expert_up, "tensor", axis=2, tiled=True),
        lax.all_gather(expert_down, "tensor", axis=1, tiled=True),
    )
    gate_pre = jnp.einsum("csad,adf->csaf", arrived, gate_full, preferred_element_type=jnp.float32)
    up_pre = jnp.einsum("csad,adf->csaf", arrived, up_full, preferred_element_type=jnp.float32)
    activated = (jax.nn.silu(gate_pre) * up_pre).astype(jnp.bfloat16)
    expert_out = jnp.einsum(
        "csaf,afd->csad", activated, down_full, preferred_element_type=jnp.float32
    ).astype(jnp.bfloat16)
    returned = lax.all_to_all(
        expert_out, "expert", split_axis=1, concat_axis=1, tiled=True
    ).reshape(slot_count, width)
    mixture_part = jnp.dot(gate_table, returned, preferred_element_type=jnp.float32)
    mixture_out = lax.psum(mixture_part.astype(jnp.bfloat16), "tensor").astype(jnp.float32)
    output = (residual_mid + mixture_out).astype(jnp.bfloat16)
    d_returned = jnp.einsum(
        "ts,td->sd", gate_table, cotangent, preferred_element_type=jnp.float32
    ).astype(jnp.bfloat16)
    products = jnp.einsum("td,sd->ts", cotangent, returned, preferred_element_type=jnp.float32)
    d_gates_part = jnp.stack(
        [
            jnp.sum(jnp.where(matches[pick_index], products, 0.0), axis=-1)
            for pick_index in range(picks)
        ],
        axis=1,
    )
    d_expert_out = lax.all_to_all(
        d_returned.reshape(share, owner_count, local_experts, width),
        "expert",
        split_axis=1,
        concat_axis=1,
        tiled=True,
    )
    sigmoid_gate = jax.nn.sigmoid(gate_pre)
    silu_gate = gate_pre * sigmoid_gate
    d_act = jnp.einsum(
        "csad,afd->csaf", d_expert_out, down_full, preferred_element_type=jnp.float32
    )
    d_gate_pre = (d_act * up_pre * sigmoid_gate * (1.0 + gate_pre * (1.0 - sigmoid_gate))).astype(
        jnp.bfloat16
    )
    d_up_pre = (d_act * silu_gate).astype(jnp.bfloat16)
    grad_down = jnp.einsum(
        "csaf,csad->afd", activated, d_expert_out, preferred_element_type=jnp.float32
    )
    grad_gate = jnp.einsum(
        "csad,csaf->adf", arrived, d_gate_pre, preferred_element_type=jnp.float32
    )
    grad_up = jnp.einsum("csad,csaf->adf", arrived, d_up_pre, preferred_element_type=jnp.float32)
    d_rows = (
        jnp.einsum("csaf,adf->csad", d_gate_pre, gate_full, preferred_element_type=jnp.float32)
        + jnp.einsum("csaf,adf->csad", d_up_pre, up_full, preferred_element_type=jnp.float32)
    ).astype(jnp.bfloat16)
    grad_gate, grad_up, grad_down = (
        lax.psum_scatter(
            grad_gate.astype(jnp.bfloat16), "tensor", scatter_dimension=2, tiled=True
        ).astype(jnp.float32),
        lax.psum_scatter(
            grad_up.astype(jnp.bfloat16), "tensor", scatter_dimension=2, tiled=True
        ).astype(jnp.float32),
        lax.psum_scatter(
            grad_down.astype(jnp.bfloat16), "tensor", scatter_dimension=1, tiled=True
        ).astype(jnp.float32),
    )
    d_sent = lax.all_to_all(d_rows, "expert", split_axis=1, concat_axis=1, tiled=True).reshape(
        slot_count, width
    )
    d_hidden_part = jnp.einsum("ts,sd->td", selector, d_sent, preferred_element_type=jnp.float32)
    d_hidden_moe, d_gates = lax.psum((d_hidden_part, d_gates_part), "tensor")
    d_logits, d_hidden_second = router_back(
        gate_values, d_gates, picked_mask, d_hidden_moe, router_weight
    )
    d_mid_norm, gain_terms = normalize_back(
        residual_mid, inverse_second, gain_second, d_hidden_second
    )
    d_mid = cotangent.astype(jnp.float32) + d_mid_norm
    grad_gain_second = jnp.sum(
        lax.dynamic_slice_in_dim(gain_terms, row_offset, rows_share, 0), axis=0
    )
    grad_router = jnp.einsum(
        "td,te->de",
        lax.dynamic_slice_in_dim(hidden_second, row_offset, rows_share, 0),
        lax.dynamic_slice_in_dim(d_logits, row_offset, rows_share, 0),
        preferred_element_type=jnp.float32,
    )
    d_attention = d_mid.astype(jnp.bfloat16)
    grad_output = jnp.einsum(
        "tq,td->qd", mixture_flat, d_attention, preferred_element_type=jnp.float32
    )
    d_mixture = (
        jnp.einsum("td,qd->tq", d_attention, output_weight, preferred_element_type=jnp.float32)
        .astype(jnp.bfloat16)
        .reshape(sequence_length, group_heads, group_size, HEAD_WIDTH)
    )
    d_queries, d_keys, d_values = attention_backward(
        queries_rot, keys_rot, values_low, blocks, log_sums, d_mixture, block_rows, scale
    )
    d_queries_low = (
        rotate_back(
            d_queries.reshape(sequence_length, query_heads, HEAD_WIDTH), cosine_table, sine_lookup
        )
        .astype(jnp.bfloat16)
        .reshape(sequence_length, query_heads * HEAD_WIDTH)
    )
    d_keys_low = (
        rotate_back(d_keys, cosine_table, sine_lookup)
        .astype(jnp.bfloat16)
        .reshape(sequence_length, group_heads * HEAD_WIDTH)
    )
    d_values_low = d_values.astype(jnp.bfloat16).reshape(sequence_length, group_heads * HEAD_WIDTH)
    grad_query = jnp.einsum(
        "td,tq->dq", hidden_first, d_queries_low, preferred_element_type=jnp.float32
    )
    grad_key = jnp.einsum("td,tq->dq", hidden_first, d_keys_low, preferred_element_type=jnp.float32)
    grad_value = jnp.einsum(
        "td,tq->dq", hidden_first, d_values_low, preferred_element_type=jnp.float32
    )
    d_first_part = jnp.einsum(
        "tq,dq->td", d_queries_low, query_weight, preferred_element_type=jnp.float32
    )
    d_first_part = d_first_part + jnp.einsum(
        "tq,dq->td", d_keys_low, key_matrix, preferred_element_type=jnp.float32
    )
    d_first_part = d_first_part + jnp.einsum(
        "tq,dq->td", d_values_low, value_matrix, preferred_element_type=jnp.float32
    )
    d_first, grad_gain_second, grad_router = (
        lax.psum(d_first_part.astype(jnp.bfloat16), "tensor").astype(jnp.float32),
        lax.psum(grad_gain_second.astype(jnp.bfloat16), "tensor").astype(jnp.float32),
        lax.psum(grad_router.astype(jnp.bfloat16), "tensor").astype(jnp.float32),
    )
    d_in_norm, first_terms = normalize_back(residual_in, inverse_first, gain_first, d_first)
    grad_gain_first = jnp.sum(first_terms, axis=0)
    input_gradient = d_mid + d_in_norm
    (
        sums_gain_first,
        sums_query,
        sums_key,
        sums_value,
        sums_output,
        sums_gain_second,
        sums_router,
    ) = (
        lax.psum(grad_gain_first.astype(jnp.bfloat16), "expert").astype(jnp.float32),
        lax.psum(grad_query.astype(jnp.bfloat16), "expert").astype(jnp.float32),
        lax.psum(grad_key.astype(jnp.bfloat16), "expert").astype(jnp.float32),
        lax.psum(grad_value.astype(jnp.bfloat16), "expert").astype(jnp.float32),
        lax.psum(grad_output.astype(jnp.bfloat16), "expert").astype(jnp.float32),
        lax.psum(grad_gain_second.astype(jnp.bfloat16), "expert").astype(jnp.float32),
        lax.psum(grad_router.astype(jnp.bfloat16), "expert").astype(jnp.float32),
    )
    return (
        output,
        input_gradient,
        sums_gain_first,
        sums_query,
        sums_key,
        sums_value,
        sums_output,
        sums_gain_second,
        sums_router,
        grad_gate,
        grad_up,
        grad_down,
    )


def solution(mesh):
    in_specs = (
        P("expert", None),
        P("expert", None),
        P("expert", None),
        P("expert", None),
        P("expert", None),
        P(),
        P(None, "tensor"),
        P(None, "tensor"),
        P(None, "tensor"),
        P("tensor", None),
        P(),
        P(),
        P("expert", None, "tensor"),
        P("expert", None, "tensor"),
        P("expert", "tensor", None),
    )
    out_specs = (
        P("expert", None),
        P("expert", None),
        P(),
        P(None, "tensor"),
        P(None, "tensor"),
        P(None, "tensor"),
        P("tensor", None),
        P(),
        P(),
        P("expert", None, "tensor"),
        P("expert", None, "tensor"),
        P("expert", "tensor", None),
    )
    return jax.shard_map(shards, mesh=mesh, in_specs=in_specs, out_specs=out_specs, check_vma=False)
```

profile of v0, /device:TPU:0, one launch (start us, length us, event | category | flops | bytes accessed | tf_op | source)
XLA Modules:
  0.0 1393.6 jit_solution(6454074672442217357)
XLA Ops:
  19.1 26.5 %while.27 = (s32[]{:T(128)}, bf16[2,512,2,3,64]{1,4,3,2,0:T(8,128)(2,1)S(1)}, f32[2,2,3,512,1]{3,2,1,4,0:T(4,128)}, s32[1,1024]{1,0:T(1,128)S(1)}, s32[2]{0:T(12...) while((s32[]{:T(128)}, ...), condition=%wide.region_4.5_spmd, body=%wide.region_1.4_spmd.sunk | while | flops 843772928 | bytes 41277644 | solution.py:92
  52.2 122.2 %all-reduce.9.cloned.1.call-done = f32[1024,1536]{1,0:T(8,128)} async-done(((f32[1024,1536]{1,0:T(8,128)}), f32[1024,1536]{1,0:T(8,128)}) %all-reduce.9.cloned.1.call-update) | async-done | bytes 6291472 | tf_op jit(solution)/shard_map/psum | solution.py:212
  186.3 15.4 %convolution_convert_fusion.1 = bf16[2048,1536]{1,0:T(8,128)(2,1)} fusion(bf16[1024,1536]{1,0:T(8,128)(2,1)S(1)} %get-tuple-element.231, s32[1024]{0:T(1024)S(1)} %bitcast.372, s32[1024]{0:T(1024)S(1)} %bitcast.377, s32[1024]{0:T(1024)S(1)} %bitcast.382, s32[1024]{0:T(1024)S(1)} %bitcast.387, s32[1024]{0:T(1024)S(1)} %bitcast.392, s32[1024]{0:T(1024)S(1)} %bitcast.397, ...), kind=kOutput, calls=%fused_computation.90 | convolution fusion | flops 6495928320 | bytes 9469952 | tf_op jit(solution)/shard_map/ts,td->sd/dot_general | solution.py:238
  201.7 13.1 reshape.166
  233.8 16.9 %convolution_convert_fusion = bf16[2048,1536]{1,0:T(8,128)(2,1)} fusion(bf16[1024,1536]{1,0:T(8,128)(2,1)} %param.20, f32[1024]{0:T(1024)S(1)} %bitcast.409, s32[1024]{0:T(1024)S(1)} %bitcast.373, f32[1024]{0:T(1024)S(1)} %bitcast.411, s32[1024]{0:T(1024)S(1)} %bitcast.378, f32[1024]{0:T(1024)S(1)} %bitcast.413, s32[1024]{0:T(1024)S(1)} %bitcast.383, ...), kind=kOutput, calls=%fused_computation.89 | convolution fusion | flops 6495928320 | bytes 9502720 | tf_op jit(solution)/shard_map/ts,td->sd/dot_general | solution.py:260
  250.8 13.1 reshape.168
  272.9 94.6 %all-to-all-done = bf16[128,8,2,1536]{3,0,2,1:T(8,128)(2,1)} async-done(((bf16[128,8,2,1536]{3,0,2,1:T(8,128)(2,1)}), bf16[128,8,2,1536]{3,0,2,1:T(8,128)(2,1)}, u32[]{:S(2)}, u32[]{:S(2)}) %all-to-all-start) | async-done | bytes 6291488 | tf_op jit(solution)/shard_map/all_to_all | solution.py:242
  382.9 21.7 %all-gather.4.cloned.1.call-done = bf16[2,1536,512]{2,1,0:T(8,128)(2,1)} async-done(((bf16[2,1536,128]{2,1,0:T(8,128)(2,1)}), bf16[2,1536,512]{2,1,0:T(8,128)(2,1)}) %all-gather.4.cloned.1.call-update) | async-done | bytes 3145744 | tf_op jit(solution)/shard_map/all_gather | solution.py:244
  404.6 9.2 fusion.72
  413.8 20.8 %all-gather.8.cloned.1.call-done = bf16[2,512,1536]{2,1,0:T(8,128)(2,1)} async-done(((bf16[2,128,1536]{2,1,0:T(8,128)(2,1)}), bf16[2,512,1536]{2,1,0:T(8,128)(2,1)}) %all-gather.8.cloned.1.call-update) | async-done | bytes 3145744 | tf_op jit(solution)/shard_map/all_gather | solution.py:246
  434.6 74.9 %all-to-all-done.2 = bf16[128,8,2,1536]{3,0,2,1:T(8,128)(2,1)} async-done(((bf16[128,8,2,1536]{3,0,2,1:T(8,128)(2,1)}), bf16[128,8,2,1536]{3,0,2,1:T(8,128)(2,1)}, u32[]{:S(2)}, u32[]{:S(2)}) %all-to-all-start.2) | async-done | bytes 6291488 | tf_op jit(solution)/shard_map/all_to_all | solution.py:271
  509.5 14.0 %fusion.77 = (bf16[128,8,2,512]{3,0,1,2:T(8,128)(2,1)}, bf16[128,8,2,512]{3,0,1,2:T(8,128)(2,1)}, bf16[128,8,2,512]{3,0,1,2:T(8,128)(2,1)}) fusion(f32[2,128,8,512]{3,1,2,0:T(8,128)} %fusion.72, f32[2,128,8,512]{3,1,2,0:T(8,128)} %fusion.70, bf16[2,512,1536]{2,1,0:T(8,128)(2,1)} %all-gather.8.cloned.1.call-done, bf16[128,8,2,1536]{3,0,2,1:T(8,128)(2,1)} %all-to-all-done.2), kind=kOutput, calls=%fused_computation.123 | convolution fusion | flops 3236954112 | bytes 24117248 | tf_op jit(solution)/shard_map/csad,afd->csaf/dot_general | solution.py:280
  539.2 142.1 %all_to_all.20 = bf16[128,8,2,1536]{3,0,2,1:T(8,128)(2,1)S(1)} all-to-all(bf16[128,8,2,1536]{3,0,2,1:T(8,128)(2,1)S(1)} %copy.72), channel_id=1, replica_groups=mesh['expert'=8,'tensor'=4] {'expert'}, dimensions={1} | all-to-all | bytes 12582912 | tf_op jit(solution)/shard_map/all_to_all | solution.py:309
  681.3 18.0 %copy.73 = bf16[128,8,2,1536]{3,2,1,0:T(2,128)(2,1)} copy(bf16[128,8,2,1536]{3,0,2,1:T(8,128)(2,1)S(1)} %all_to_all.20) | data formatting | bytes 12582912 | tf_op jit(solution)/shard_map/all_to_all | solution.py:309
  699.3 13.6 reshape.169
  712.9 17.4 %fusion.94 = f32[1024,1536]{1,0:T(8,128)} fusion(bf16[2048,1536]{1,0:T(8,128)(2,1)} %reshape.169, s32[1024]{0:T(1024)S(1)} %bitcast.374, s32[1024]{0:T(1024)S(1)} %bitcast.379, s32[1024]{0:T(1024)S(1)} %bitcast.384, s32[1024]{0:T(1024)S(1)} %bitcast.389, s32[1024]{0:T(1024)S(1)} %bitcast.394, s32[1024]{0:T(1024)S(1)} %bitcast.399, s32[1024]{0:T(1024)S(1)} %bitcast.404, ...), kind=kOutput, calls=%fused_computation.149 | convolution fusion | flops 6492782592 | bytes 12615680 | tf_op jit(solution)/shard_map/ts,sd->td/dot_general | solution.py:312
  731.8 9.1 bitcast_convert_fusion.1
  768.2 9.3 bitcast_convert_fusion.2
  799.8 105.5 %all-to-all-done.1 = bf16[128,8,2,1536]{3,0,2,1:T(8,128)(2,1)} async-done(((bf16[128,8,2,1536]{3,0,2,1:T(8,128)(2,1)}), bf16[128,8,2,1536]{3,0,2,1:T(8,128)(2,1)}, u32[]{:S(2)}, u32[]{:S(2)}) %all-to-all-start.1) | async-done | bytes 6291488 | tf_op jit(solution)/shard_map/all_to_all | solution.py:254
  905.3 12.7 copy.69
  918.0 13.6 reshape.167
  931.7 18.6 %fusion.57 = (f32[1024]{0:T(1024)S(1)}, f32[1024]{0:T(1024)S(1)}, f32[1024]{0:T(1024)S(1)}, f32[1024]{0:T(1024)S(1)}, f32[1024]{0:T(1024)S(1)}, /*index=5*/f32[1024]{0:T(1024)S(1)}, f32[1024]{0:T(1024)S(1)}, f32[1024]{0:T(1024)S(1)}) fusion(s32[1024]{0:T(1024)S(1)} %bitcast.375, s32[1024]{0:T(1024)S(1)} %bitcast.405, s32[1024]{0:T(1024)S(1)} %bitcast.400, ...), kind=kOutput, calls=%fused_computation.77 | convolution fusion | flops 6492774400 | bytes 9502720 | tf_op jit(solution)/shard_map/td,sd->ts/dot_general | solution.py:263
  950.4 11.6 psum.101
  977.5 86.7 %while.28 = (s32[]{:T(128)}, f32[1024,2,64]{0,2,1:T(8,128)S(1)}, f32[1024,2,64]{0,2,1:T(8,128)}, f32[2,512,2,3,64]{1,0,4,3,2:T(2,128)}, s32[2]{0:T(128)S(1)}, /*...) while((s32[]{:T(128)}, f32[1024,2,64]{0,2,1:T(8,128)S(1)}, ...), condition=%wide.region_26.27_spmd.clone, body=%wide.region_24.26_spmd.clone.sunk | while | flops 2061825024 | bytes 104954120 | solution.py:133
  1005.9 15.0 %dynamic_update_slice.20 = f32[2,512,2,3,64]{1,0,4,3,2:T(2,128)} dynamic-update-slice(f32[2,512,2,3,64]{1,0,4,3,2:T(2,128)} %get-tuple-element.464, f32[1,512,2,3,64]{1,0,4,3,2:T(1,128)S(1)} %copy.138, s32[]{:T(128)S(6)} %copy.157, s32[]{:T(128)} %constant.48.clone.1..sunk.1, s32[]{:T(128)} %constant.48.clone.1..sunk.1, s32[]{:T(128)} %constant.48.clone.1..sunk.1, s32[]{:T(128)} %constant.48.clone.1..sunk.1) | dynamic-update-slice | bytes 1572868 | tf_op jit(solution)/shard_map/while/body/jit(dynamic_update_index_in_dim)/dynamic_update_slice | solution.py:133
  1049.3 15.0 %dynamic_update_slice.20 = f32[2,512,2,3,64]{1,0,4,3,2:T(2,128)} dynamic-update-slice(f32[2,512,2,3,64]{1,0,4,3,2:T(2,128)} %get-tuple-element.464, f32[1,512,2,3,64]{1,0,4,3,2:T(1,128)S(1)} %copy.138, s32[]{:T(128)S(6)} %copy.157, s32[]{:T(128)} %constant.48.clone.1..sunk.1, s32[]{:T(128)} %constant.48.clone.1..sunk.1, s32[]{:T(128)} %constant.48.clone.1..sunk.1, s32[]{:T(128)} %constant.48.clone.1..sunk.1) | dynamic-update-slice | bytes 1572868 | tf_op jit(solution)/shard_map/while/body/jit(dynamic_update_index_in_dim)/dynamic_update_slice | solution.py:133
  1080.1 18.0 %convolution_convert_fusion.2 = bf16[1024,1536]{1,0:T(8,128)(2,1)} fusion(bf16[2048,1536]{1,0:T(8,128)(2,1)} %reshape.167, f32[1024]{0:T(1024)S(1)} %bitcast.410, s32[1024]{0:T(1024)S(1)} %bitcast.376, f32[1024]{0:T(1024)S(1)} %bitcast.412, s32[1024]{0:T(1024)S(1)} %bitcast.381, f32[1024]{0:T(1024)S(1)} %bitcast.414, s32[1024]{0:T(1024)S(1)} %bitcast.386, ...), kind=kOutput, calls=%fused_computation.133 | convolution fusion | flops 6494355456 | bytes 9502720 | tf_op jit(solution)/shard_map/dot_general | solution.py:257
  1119.4 10.9 all-reduce.2
  1130.3 79.2 %all-reduce.13.cloned.1.call-done = (bf16[1536,384]{1,0:T(8,128)(2,1)}, bf16[1536,128]{1,0:T(8,128)(2,1)}, bf16[1536,128]{1,0:T(8,128)(2,1)}, bf16[384,1536]{1,0:T(8,128)(2,1)}) async-done(((bf16[1536,384]{1,0:T(8,128)(2,1)}, bf16[1536,128]{1,0:T(8,128)(2,1)}, bf16[1536,128]{1,0:T(8,128)(2,1)}, bf16[384,1536]{1,0:T(8,128)(2,1)}), (bf16[1536,384]{1,0:T(8,128)(2,1)}, bf16[1536,128]{1,0:T(8,128)(2,1)}, ...) | async-done | bytes 3145744 | tf_op jit(solution)/shard_map/psum | solution.py:389
  1218.0 112.5 %all-reduce.15.cloned.1.call-done = (bf16[1024,1536]{1,0:T(8,128)(2,1)}, bf16[1024,1536]{1,0:T(8,128)(2,1)}) async-done(((bf16[1024,1536]{1,0:T(8,128)(2,1)}, bf16[1024,1536]{1,0:T(8,128)(2,1)}), (bf16[1024,1536]{1,0:T(8,128)(2,1)}, bf16[1024,1536]{1,0:T(8,128)(2,1)})) %all-reduce.15.cloned.1.call-update) | async-done | bytes 6291472 | tf_op jit(solution)/shard_map/psum | solution.py:258
  1334.6 37.6 %all-reduce = (bf16[1536]{0:T(1024)(128)(2,1)S(1)}, bf16[1536]{0:T(1024)(128)(2,1)S(1)}, bf16[1536,16]{0,1:T(8,128)(2,1)S(1)}) all-reduce(bf16[1536]{0:T(1024)(128)(2,1)S(1)} %get-tuple-element.176, bf16[1536]{0:T(1024)(128)(2,1)S(1)} %get-tuple-element.227, ...), channel_id=1, replica_groups=mesh['expert'=8,'tensor'=4] {'expert'}, use_global_device_ids=true, to_apply=%region_30.31 | all-reduce | flops 27648 | bytes 110592 | tf_op jit(solution)/shard_map/psum | solution.py:388
  1374.1 12.5 fusion.60
  (328 shorter events, 286.5 us)
Async XLA Ops:
  7.2 40.3 %copy-start = (bf16[384,1536]{1,0:T(8,128)(2,1)S(1)}, bf16[384,1536]{1,0:T(8,128)(2,1)}, u32[]{:S(2)}) copy-start(bf16[384,1536]{1,0:T(8,128)(2,1)} %param.28) | copy-start | bytes 3538948
  7.2 167.3 %all-reduce.9.cloned.1.call-start = ((), (), s32[]{:S(2)}) async-start(), calls=%async_computation.7 | async-start | bytes 12582912 | tf_op jit(solution)/shard_map/psum | solution.py:212
  52.1 132.5 %copy-start.39 = (f32[1536]{0:T(1024)}, f32[1536]{0:T(1024)S(1)}, u32[]{:S(2)}) copy-start(f32[1536]{0:T(1024)S(1)} %convert_element_type.212) | copy-start | bytes 18436
  52.2 879.4 %copy-start.51 = (s32[1024,1]{0,1:T(1,128)}, s32[1024,1]{0,1:T(1,128)S(1)}, u32[]{:S(2)}) copy-start(s32[1024,1]{0,1:T(1,128)S(1)} %get-tuple-element.250) | copy-start | bytes 12292
  52.2 879.4 %copy-start.53 = (s32[1024,1]{0,1:T(1,128)}, s32[1024,1]{0,1:T(1,128)S(1)}, u32[]{:S(2)}) copy-start(s32[1024,1]{0,1:T(1,128)S(1)} %get-tuple-element.251) | copy-start | bytes 12292
  52.2 879.4 %copy-start.55 = (s32[1024,1]{0,1:T(1,128)}, s32[1024,1]{0,1:T(1,128)S(1)}, u32[]{:S(2)}) copy-start(s32[1024,1]{0,1:T(1,128)S(1)} %get-tuple-element.252) | copy-start | bytes 12292
  52.2 879.4 %copy-start.57 = (s32[1024,1]{0,1:T(1,128)}, s32[1024,1]{0,1:T(1,128)S(1)}, u32[]{:S(2)}) copy-start(s32[1024,1]{0,1:T(1,128)S(1)} %get-tuple-element.253) | copy-start | bytes 12292
  52.2 879.4 %copy-start.59 = (s32[1024,1]{0,1:T(1,128)}, s32[1024,1]{0,1:T(1,128)S(1)}, u32[]{:S(2)}) copy-start(s32[1024,1]{0,1:T(1,128)S(1)} %get-tuple-element.254) | copy-start | bytes 12292
  52.2 879.4 %copy-start.61 = (s32[1024,1]{0,1:T(1,128)}, s32[1024,1]{0,1:T(1,128)S(1)}, u32[]{:S(2)}) copy-start(s32[1024,1]{0,1:T(1,128)S(1)} %get-tuple-element.255) | copy-start | bytes 12292
  52.2 879.4 %copy-start.63 = (s32[1024,1]{0,1:T(1,128)}, s32[1024,1]{0,1:T(1,128)S(1)}, u32[]{:S(2)}) copy-start(s32[1024,1]{0,1:T(1,128)S(1)} %get-tuple-element.256) | copy-start | bytes 12292
  52.2 879.4 %copy-start.65 = (s32[1024,1]{0,1:T(1,128)}, s32[1024,1]{0,1:T(1,128)S(1)}, u32[]{:S(2)}) copy-start(s32[1024,1]{0,1:T(1,128)S(1)} %get-tuple-element.257) | copy-start | bytes 12292
  223.8 143.6 %all-to-all-start = ((bf16[128,8,2,1536]{3,0,2,1:T(8,128)(2,1)}), bf16[128,8,2,1536]{3,0,2,1:T(8,128)(2,1)}, u32[]{:S(2)}, u32[]{:S(2)}) async-start(bf16[128,8,2,1536]{3,0,2,1:T(8,128)(2,1)} %copy.65), calls=%async_computation | async-start | bytes 12582912 | tf_op jit(solution)/shard_map/all_to_all | solution.py:242
  229.4 144.3 %all-gather.6.cloned.1.call-start = ((), (), s32[]{:S(2)}) async-start(), calls=%async_computation.9 | async-start | bytes 3932160 | tf_op jit(solution)/shard_map/all_gather | solution.py:245
  367.4 142.1 %all-to-all-start.2 = ((bf16[128,8,2,1536]{3,0,2,1:T(8,128)(2,1)}), bf16[128,8,2,1536]{3,0,2,1:T(8,128)(2,1)}, u32[]{:S(2)}, u32[]{:S(2)}) async-start(bf16[128,8,2,1536]{3,0,2,1:T(8,128)(2,1)} %copy.70), calls=%async_computation.2 | async-start | bytes 12582912 | tf_op jit(solution)/shard_map/all_to_all | solution.py:271
  372.2 32.4 %all-gather.4.cloned.1.call-start = ((), (), s32[]{:S(2)}) async-start(), calls=%async_computation.8 | async-start | bytes 3932160 | tf_op jit(solution)/shard_map/all_gather | solution.py:244
  372.9 61.6 %all-gather.8.cloned.1.call-start = ((), (), s32[]{:S(2)}) async-start(), calls=%async_computation.10 | async-start | bytes 3932160 | tf_op jit(solution)/shard_map/all_gather | solution.py:246
  373.5 588.6 %all-reduce.11.cloned.1.call-start = ((), (), s32[]{:S(2)}) async-start(), calls=%async_computation.11 | async-start | bytes 12582912 | tf_op jit(solution)/shard_map/psum | solution.py:313
  730.3 373.8 %reduce-scatter.12.cloned.1.call-start = ((), (), s32[]{:S(2)}) async-start(), calls=%async_computation.14 | async-start | bytes 3932160
  763.3 142.0 %all-to-all-start.1 = ((bf16[128,8,2,1536]{3,0,2,1:T(8,128)(2,1)}), bf16[128,8,2,1536]{3,0,2,1:T(8,128)(2,1)}, u32[]{:S(2)}, u32[]{:S(2)}) async-start(bf16[128,8,2,1536]{3,0,2,1:T(8,128)(2,1)} %copy.68), calls=%async_computation.1 | async-start | bytes 12582912 | tf_op jit(solution)/shard_map/all_to_all | solution.py:254
  768.2 339.2 %reduce-scatter.10.cloned.1.call-start = ((), (), s32[]{:S(2)}) async-start(), calls=%async_computation.13 | async-start | bytes 3932160
  790.7 322.8 %reduce-scatter.8.cloned.1.call-start = ((), (), s32[]{:S(2)}) async-start(), calls=%async_computation.12 | async-start | bytes 3932160 | tf_op jit(solution)/shard_map/reduce_scatter | solution.py:305
  799.3 410.2 %all-reduce.13.cloned.1.call-start = ((), (), s32[]{:S(2)}) async-start(), calls=%async_computation.15 | async-start | bytes 6291456 | tf_op jit(solution)/shard_map/psum | solution.py:389
  931.7 30.3 %copy-start.29 = (f32[1024,8]{0,1:T(8,128)S(1)}, f32[1024,8]{0,1:T(8,128)}, u32[]{:S(2)}) copy-start(f32[1024,8]{0,1:T(8,128)} %copy-done.28) | copy-start | bytes 98308
  931.7 30.3 %copy-start.42 = (f32[1024]{0:T(1024)S(1)}, f32[1024]{0:T(1024)}, u32[]{:S(2)}) copy-start(f32[1024]{0:T(1024)} %copy-done.41) | copy-start | bytes 12292
  931.7 30.3 %copy-start.44 = (f32[1024]{0:T(1024)S(1)}, f32[1024]{0:T(1024)}, u32[]{:S(2)}) copy-start(f32[1024]{0:T(1024)} %copy-done.43) | copy-start | bytes 12292
  931.7 30.3 %copy-start.33 = (s32[1024,8]{0,1:T(8,128)S(1)}, s32[1024,8]{0,1:T(8,128)}, u32[]{:S(2)}) copy-start(s32[1024,8]{0,1:T(8,128)} %param.22) | copy-start | bytes 98308
  931.7 30.4 %copy-start.35 = (bf16[1536,16]{0,1:T(8,128)(2,1)S(1)}, bf16[1536,16]{0,1:T(8,128)(2,1)}, u32[]{:S(2)}) copy-start(bf16[1536,16]{0,1:T(8,128)(2,1)} %param.30) | copy-start | bytes 147460
  931.7 30.4 %copy-start.40 = (f32[1536]{0:T(1024)S(1)}, f32[1536]{0:T(1024)}, u32[]{:S(2)}) copy-start(f32[1536]{0:T(1024)} %copy-done.39) | copy-start | bytes 18436
  1079.9 18.2 %copy-start.22 = (bf16[1536,128]{1,0:T(8,128)(2,1)S(1)}, bf16[1536,128]{1,0:T(8,128)(2,1)}, u32[]{:S(2)}) copy-start(bf16[1536,128]{1,0:T(8,128)(2,1)} %param.26) | copy-start | bytes 1179652
  1079.9 250.6 %all-reduce.15.cloned.1.call-start = ((), (), s32[]{:S(2)}) async-start(), calls=%async_computation.16 | async-start | bytes 12582912 | tf_op jit(solution)/shard_map/psum | solution.py:258
  1117.3 213.2 %copy-start.38 = (f32[1536]{0:T(1024)S(1)}, f32[1536]{0:T(1024)}, u32[]{:S(2)}) copy-start(f32[1536]{0:T(1024)} %copy-done.37) | copy-start | bytes 18436
  1117.3 213.2 %copy-start.46 = (f32[1024]{0:T(1024)S(1)}, f32[1024]{0:T(1024)}, u32[]{:S(2)}) copy-start(f32[1024]{0:T(1024)} %copy-done.45) | copy-start | bytes 12292
  (69 other events, 423.8 us)
Sparse Core Ops, SparseCore 0:
  52.1 122.2 all-reduce.8
  231.8 29.6 all-gather.5
  374.6 29.9 all-gather.3
  406.0 28.5 all-gather.7
  730.4 118.6 all-reduce.10
  851.4 38.1 reduce-scatter.11
  892.3 37.9 reduce-scatter.9
  932.8 38.4 reduce-scatter.7
  1080.0 129.4 all-reduce.12
  1211.7 118.6 all-reduce.14
where the time goes:
time: 1400 us; the launch traced here: 1390 us
  waiting for transfers between devices  634 us (45%)
  matrix products  254 us (18%)
  blocking collectives  202 us (14%)
  local copies, waits for them, and re-layouts  185 us (13%)
  other arithmetic  83.4 us (6%)
  starting transfers between devices  16.5 us (1%)
  between operations  15.8 us (1%)
    all_to_all x1, blocking collectives, shards(): lax.all_to_all(d_rows, 'expert', split_axis=1, concat_axis=1, tiled=True)  142 us
    psum x1, waiting for transfers between devices, shards(): attention_out = lax.psum(partial_out, 'tensor')  122 us
    psum x1, waiting for transfers between devices, shards(): lax.psum(mixture_part.astype(jnp.bfloat16), 'tensor').astype(jnp.float32)  112 us
    all_to_all x1, waiting for transfers between devices, shards(): lax.all_to_all(expert_out, 'expert', split_axis=1, concat_axis=1, tiled=T...  105 us
    all_to_all x1, waiting for transfers between devices, shards(): lax.all_to_all(send_rows, 'expert', split_axis=1, concat_axis=1, tiled=True)  94.6 us
    psum x1, waiting for transfers between devices, shards(): lax.psum(grad_query.astype(jnp.bfloat16), 'expert').astype(jnp.float32)  79.2 us
    all_to_all x1, waiting for transfers between devices, shards(): lax.all_to_all(d_returned.reshape(share, owner_count, local_experts, widt...  74.9 us
    unnamed x185, local copies, waits for them, and re-layouts  40.3 us
  transfers between devices with their start and end apart: 13, of which 8 were waited for; matrix products, arithmetic and copies ran while one was open for 24% of the time, Pallas kernels for 0%

commit v1 on v0

v1 whole, which is shorter than its diff:
```python
import functools
import math

import jax
import jax.numpy as jnp
from jax import lax
from jax.experimental import pallas as pl
from jax.experimental.pallas import tpu as pltpu
from jax.sharding import PartitionSpec as P

HEAD_WIDTH = 64
EPSILON = 1e-05
NEGATIVE = -1e30
LANES = 128
LOW = jnp.bfloat16
FULL = jnp.float32
NN = (((1,), (0,)), ((), ()))
NT = (((1,), (1,)), ((), ()))
TN = (((0,), (0,)), ((), ()))


def mul(left, right, dims=NN):
    return lax.dot_general(left, right, dims, preferred_element_type=FULL)


def rope_tables(sequence_length, head_size):
    half_width = head_size // 2
    frequency = jnp.exp(
        jnp.arange(half_width, dtype=FULL) * (-2.0 * math.log(10000.0) / head_size)
    )
    angles = jnp.arange(sequence_length, dtype=FULL)[:, None] * frequency[None, :]
    return (jnp.cos(angles), jnp.sin(angles))


def apply_rotation(values, cosine_table, sine_lookup, sign=1.0):
    half_width = values.shape[-1] // 2
    first_half = values[..., :half_width]
    second_half = values[..., half_width:]
    cosine_rows = cosine_table[:, None, :]
    sine_rows = sine_lookup[:, None, :] * sign
    return jnp.concatenate(
        [
            first_half * cosine_rows - second_half * sine_rows,
            second_half * cosine_rows + first_half * sine_rows,
        ],
        axis=-1,
    )


def block_scores(part_queries, keys_rot, blocks, part_blocks, scale):
    scores = (
        jnp.einsum("qkgd,skd->kgqs", part_queries, keys_rot, preferred_element_type=FULL) * scale
    )
    visible = blocks[None, :] <= part_blocks[:, None]
    return jnp.where(visible, scores, NEGATIVE)


def attention_forward(queries_rot, keys_rot, values_low, blocks, block_rows, scale):
    block_count = queries_rot.shape[0] // block_rows

    def one_block(block_index):
        offset = block_index * block_rows
        part_queries = lax.dynamic_slice_in_dim(queries_rot, offset, block_rows, 0)
        part_blocks = lax.dynamic_slice_in_dim(blocks, offset, block_rows, 0)
        scores = block_scores(part_queries, keys_rot, blocks, part_blocks, scale)
        row_peak = jnp.max(scores, axis=-1, keepdims=True)
        exponent = jnp.exp(scores - row_peak)
        summed = jnp.sum(exponent, axis=-1, keepdims=True)
        weights = (exponent / summed).astype(LOW)
        mixture = jnp.einsum("kgqs,skd->qkgd", weights, values_low, preferred_element_type=FULL)
        return (mixture.astype(LOW), row_peak + jnp.log(summed))

    mixture, log_sums = lax.map(one_block, jnp.arange(block_count, dtype=jnp.int32))
    return (mixture.reshape(queries_rot.shape), log_sums)


def attention_backward(
    queries_rot, keys_rot, values_low, blocks, log_sums, d_mixture, block_rows, scale
):
    block_count = queries_rot.shape[0] // block_rows

    def one_block(running, pieces):
        d_keys, d_values = running
        block_index, log_sum = pieces
        offset = block_index * block_rows
        part_queries = lax.dynamic_slice_in_dim(queries_rot, offset, block_rows, 0)
        part_blocks = lax.dynamic_slice_in_dim(blocks, offset, block_rows, 0)
        part_grads = lax.dynamic_slice_in_dim(d_mixture, offset, block_rows, 0)
        scores = block_scores(part_queries, keys_rot, blocks, part_blocks, scale)
        weights = jnp.exp(scores - log_sum)
        weights_low = weights.astype(LOW)
        d_weights = jnp.einsum("qkgd,skd->kgqs", part_grads, values_low, preferred_element_type=FULL)
        row_delta = jnp.sum(weights * d_weights, axis=-1, keepdims=True)
        d_scores = (weights * (d_weights - row_delta)).astype(LOW)
        d_queries = (
            jnp.einsum("kgqs,skd->qkgd", d_scores, keys_rot, preferred_element_type=FULL) * scale
        )
        d_keys = (
            d_keys
            + jnp.einsum("kgqs,qkgd->skd", d_scores, part_queries, preferred_element_type=FULL)
            * scale
        )
        d_values = d_values + jnp.einsum(
            "kgqs,qkgd->skd", weights_low, part_grads, preferred_element_type=FULL
        )
        return ((d_keys, d_values), d_queries)

    zeros_kv = jnp.zeros(keys_rot.shape, FULL)
    (d_keys, d_values), d_queries = lax.scan(
        one_block, (zeros_kv, zeros_kv), (jnp.arange(block_count, dtype=jnp.int32), log_sums)
    )
    return (d_queries.reshape(queries_rot.shape), d_keys, d_values)


def expert_body(shard_count, local, hidden, row_tile, column_tile, columns_ref, h_ref, g_ref,
                code_ref, router_ref, *rest):
    w_refs = rest[:shard_count]
    y_ref, dh_ref, hid_ref, dgb_ref, first_buffer, second_buffer, arrived, kept_ref = rest[shard_count:]
    wide = local * hidden
    first = 2 * wide
    copies = []
    for s in range(shard_count):
        a = pltpu.make_async_copy(
            w_refs[s].at[pl.ds(0, first)], first_buffer.at[pl.ds(s * first, first)], arrived.at[s, 0]
        )
        b = pltpu.make_async_copy(
            w_refs[s].at[pl.ds(first, wide)], second_buffer.at[pl.ds(s * wide, wide)], arrived.at[s, 1]
        )
        a.start()
        b.start()
        copies.append((a, b))
    rows, width = h_ref.shape
    logits = mul(h_ref[...], router_ref[...])
    code = code_ref[...].astype(FULL)
    picked = code > 0.5
    peak = jnp.max(jnp.where(picked, logits, NEGATIVE), axis=1, keepdims=True)
    exponent = jnp.where(picked, jnp.exp(logits - peak), 0.0)
    gates = exponent / jnp.sum(exponent, axis=1, keepdims=True)
    kept_ref[...] = jnp.where(code > 1.5, gates, 0.0).astype(LOW).astype(FULL)
    dgb_ref[...] = jnp.zeros(dgb_ref.shape, FULL)
    lane = lax.broadcasted_iota(jnp.int32, (row_tile, LANES), 1)
    owner = lax.broadcasted_iota(jnp.int32, (row_tile, wide), 1) // hidden
    for s in range(shard_count):
        copies[s][0].wait()
        copies[s][1].wait()
        place = local * (s // (shard_count // 2))

        @pl.loop(0, rows // row_tile)
        def _(i, s=s, place=place):
            at = pl.ds(pl.multiple_of(i * row_tile, row_tile), row_tile)
            z = mul(h_ref[at, :], first_buffer[s * first : (s + 1) * first, :], NT)
            q = mul(g_ref[at, :], second_buffer[s * wide : (s + 1) * wide, :], NT)
            kept = kept_ref[at, :]
            hits = [lane == columns_ref[place + e] for e in range(local)]
            gate_of = jnp.zeros((row_tile, wide), FULL)
            for e in range(local):
                own = jnp.sum(jnp.where(hits[e], kept, 0.0), axis=1, keepdims=True)
                gate_of = jnp.where(owner == e, own, gate_of)
            gate, up = z[:, :wide], z[:, wide:]
            sigmoid = jax.nn.sigmoid(gate)
            silu = gate * sigmoid
            act = silu * up
            d_act = q * gate_of
            base = s * first
            hid_ref[at, base : base + wide] = (
                d_act * up * sigmoid * (1.0 + gate * (1.0 - sigmoid))
            ).astype(LOW)
            hid_ref[at, base + wide : base + first] = (d_act * silu).astype(LOW)
            base = shard_count * first + s * wide
            hid_ref[at, base : base + wide] = (act * gate_of).astype(LOW)
            product = act * q
            dgb = dgb_ref[at, :]
            for e in range(local):
                part = jnp.sum(jnp.where(owner == e, product, 0.0), axis=1, keepdims=True)
                dgb = dgb + jnp.where(hits[e], part, 0.0)
            dgb_ref[at, :] = dgb

    @pl.loop(0, rows // row_tile)
    def _(i):
        at = pl.ds(pl.multiple_of(i * row_tile, row_tile), row_tile)

        @pl.loop(0, width // column_tile)
        def _(j):
            cut = pl.ds(pl.multiple_of(j * column_tile, column_tile), column_tile)
            middle = shard_count * first
            dh_ref[at, cut] = mul(hid_ref[at, 0:middle], first_buffer[:, cut]).astype(LOW)
            y_ref[at, cut] = mul(hid_ref[at, middle:], second_buffer[:, cut]).astype(LOW)


def run_experts(columns, h, g, code, router, shards_of, local, hidden):
    count = len(shards_of)
    rows, width = h.shape
    depth = shards_of[0].shape[0]
    wide = local * hidden
    whole = pl.BlockSpec(memory_space=pltpu.VMEM)
    row_tile = min(512, rows)
    return pl.pallas_call(
        functools.partial(expert_body, count, local, hidden, row_tile, 256),
        out_shape=(
            jax.ShapeDtypeStruct((rows, width), LOW),
            jax.ShapeDtypeStruct((rows, width), LOW),
            jax.ShapeDtypeStruct((rows, count * depth), LOW),
            jax.ShapeDtypeStruct((rows, LANES), FULL),
        ),
        in_specs=[pl.BlockSpec(memory_space=pltpu.SMEM)]
        + [whole] * 4
        + [pl.BlockSpec(memory_space=pl.ANY)] * count,
        out_specs=(whole,) * 4,
        scratch_shapes=[
            pltpu.VMEM((count * 2 * wide, width), LOW),
            pltpu.VMEM((count * wide, width), LOW),
            pltpu.SemaphoreType.DMA((count, 2)),
            pltpu.VMEM((rows, LANES), FULL),
        ],
        compiler_params=pltpu.CompilerParams(vmem_limit_bytes=50 * 1024 * 1024),
        cost_estimate=pl.CostEstimate(
            flops=rows * width * depth * 4 * count,
            bytes_accessed=count * depth * width * 2 + rows * width * 8 + count * rows * depth * 2,
            transcendentals=0,
        ),
        name="experts",
    )(columns, h, g, code, router, *shards_of)


def swap(values, axis, bit):
    count = lax.axis_size(axis)
    return lax.ppermute(values, axis, [(i, i ^ bit) for i in range(count)])


def pair(values):
    return swap(values, "expert", 1)


def ring(values):
    count = lax.axis_size("expert")
    return lax.ppermute(values, "expert", [(i, (i + 2) % count) for i in range(count)])


def pick(values, index):
    return lax.dynamic_index_in_dim(values, index, 0, keepdims=False)


def ring_gather(block):
    blocks = [block]
    for _ in range(lax.axis_size("expert") // 2 - 1):
        blocks.append(ring(blocks[-1]))
    return blocks


def ring_sum(blocks):
    running = blocks[1 % len(blocks)].astype(FULL)
    for k in range(2, len(blocks) + 1):
        running = ring(running.astype(LOW)).astype(FULL) + blocks[k % len(blocks)].astype(FULL)
    return running


def bits_of(count):
    return [1 << i for i in range(count.bit_length() - 1)]


def tensor_sum(values):
    count = lax.axis_size("tensor")
    here = lax.axis_index("tensor")
    own = values
    for bit in bits_of(count):
        split = own.reshape((own.shape[0] // 2, 2) + own.shape[1:])
        mine = (here // bit) % 2
        send = lax.dynamic_index_in_dim(split, 1 - mine, 1, keepdims=False).astype(LOW)
        keep = lax.dynamic_index_in_dim(split, mine, 1, keepdims=False)
        own = keep.astype(FULL) + swap(send, "tensor", bit).astype(FULL)
    return own[0]


def tensor_gather(values):
    count = lax.axis_size("tensor")
    here = lax.axis_index("tensor")
    own = values[None]
    for bit in reversed(bits_of(count)):
        other = swap(own, "tensor", bit)
        low = (here // bit) % 2 == 0
        own = jnp.stack([jnp.where(low, own, other), jnp.where(low, other, own)], axis=1)
        own = own.reshape((-1,) + values.shape)
    return own.reshape((-1,) + values.shape[1:])


def expert_sum(values):
    size = lax.axis_size("expert") // 2
    here = lax.axis_index("expert")
    place, side = here // 2, here % 2
    n, m = values.shape
    halves = values.reshape(2, n // 2, m)
    half = pick(halves, side) + pair(pick(halves, 1 - side).astype(LOW)).astype(FULL)
    cuts = half.reshape(size, n // 2 // size, m)
    own = ring_sum([pick(cuts, (place - k) % size) for k in range(size)]).astype(LOW)
    gathered = ring_gather(own)
    half = jnp.zeros((size,) + own.shape, LOW)
    for k in range(size):
        half = lax.dynamic_update_index_in_dim(half, gathered[k], (place - k) % size, 0)
    half = half.reshape(n // 2, m)
    other = pair(half)
    low = side == 0
    return jnp.concatenate([jnp.where(low, half, other), jnp.where(low, other, half)]).astype(FULL)


def gather_weights(own):
    cut = own.shape[0] // 2
    near, far = [own], [pair(own)]
    for bit in bits_of(lax.axis_size("tensor"))[1:]:
        for i in range(len(near)):
            near.append(swap(near[i], "tensor", bit))
            far.append(
                jnp.concatenate([pair(near[-1][:cut]), swap(far[i][cut:], "tensor", bit)])
            )
    shards_of = []
    for chip in near + far:
        shards_of += [chip, swap(chip, "tensor", 1)]
    return shards_of


def scatter_weights(parts):
    cut = parts[0].shape[0] // 2
    full = lambda v: v.astype(FULL)
    sums = [
        full(parts[i]) + full(swap(parts[i + 1], "tensor", 1)) for i in range(0, len(parts), 2)
    ]
    near, far = sums[: len(sums) // 2], sums[len(sums) // 2 :]
    for bit in reversed(bits_of(lax.axis_size("tensor"))[1:]):
        count = len(near) // 2
        for i in range(count):
            last_near, last_far = near[count + i], far[count + i]
            moved = full(pair(last_far[:cut].astype(LOW)))
            last_near = jnp.concatenate([last_near[:cut] + moved, last_near[cut:]])
            moved = full(swap(last_far[cut:].astype(LOW), "tensor", bit))
            far[i] = jnp.concatenate([far[i][:cut], far[i][cut:] + moved])
            near[i] = near[i] + full(swap(last_near.astype(LOW), "tensor", bit))
        near, far = near[:count], far[:count]
    return near[0] + full(pair(far[0].astype(LOW)))


def shards(
    activations,
    cotangent,
    block_ids,
    expert_ids,
    route_ranks,
    attention_gain,
    query_weight,
    key_matrix,
    value_matrix,
    output_weight,
    mixture_gain,
    router_weight,
    expert_gate,
    expert_up,
    expert_down,
):
    sequence_length, width = activations.shape
    query_heads = query_weight.shape[1] // HEAD_WIDTH
    group_heads = key_matrix.shape[1] // HEAD_WIDTH
    group_size = query_heads // group_heads
    tensor_count = lax.axis_size("tensor")
    expert_count = lax.axis_size("expert")
    tensor_index = lax.axis_index("tensor")
    expert_index = lax.axis_index("expert")
    num_experts = router_weight.shape[1]
    local, _, hidden = expert_gate.shape
    picks = expert_ids.shape[1]
    capacity = sequence_length * picks // num_experts
    rows = sequence_length // tensor_count
    ring_size = expert_count // 2
    place, side = expert_index // 2, expert_index % 2
    row_offset = tensor_index * rows
    own_rows = lambda v: lax.dynamic_slice_in_dim(v, row_offset, rows, 0)
    block_rows = min(512, sequence_length)
    scale = HEAD_WIDTH ** (-0.5)
    blocks = block_ids[0]
    wide = local * hidden

    packed = jnp.concatenate(
        [
            expert_gate.transpose(0, 2, 1).reshape(wide, width),
            expert_up.transpose(0, 2, 1).reshape(wide, width),
            expert_down.reshape(wide, width),
        ]
    )
    weight_shards = gather_weights(packed)
    cotangent_own = own_rows(cotangent)
    cotangent_blocks = ring_gather(cotangent_own)
    ids_own, ranks_own = own_rows(expert_ids), own_rows(route_ranks)
    expert_range = jnp.arange(LANES, dtype=jnp.int32)
    pair_code = jnp.where(ranks_own < capacity, 2.0, 1.0)
    code = jnp.zeros((rows, LANES), FULL)
    for j in range(picks):
        code = code + jnp.where(
            ids_own[:, j, None] == expert_range[None, :], pair_code[:, j, None], 0.0
        )
    code_blocks = ring_gather(code.astype(LOW))

    cosine_table, sine_lookup = rope_tables(sequence_length, HEAD_WIDTH)
    residual_in = activations.astype(FULL)
    gain_first = attention_gain.astype(FULL)
    inverse_first = lax.rsqrt(jnp.mean(residual_in * residual_in, axis=-1, keepdims=True) + EPSILON)
    hidden_first = (residual_in * inverse_first * gain_first).astype(LOW)
    weight_all = jnp.concatenate([query_weight, key_matrix, value_matrix], axis=1)
    cut_keys = query_heads * HEAD_WIDTH
    cut_values = cut_keys + group_heads * HEAD_WIDTH
    projected = mul(hidden_first, weight_all)
    values_low = (
        projected[:, cut_values:].astype(LOW).reshape(sequence_length, group_heads, HEAD_WIDTH)
    )
    queries_rot = (
        apply_rotation(
            projected[:, :cut_keys].reshape(sequence_length, query_heads, HEAD_WIDTH),
            cosine_table,
            sine_lookup,
        )
        .astype(LOW)
        .reshape(sequence_length, group_heads, group_size, HEAD_WIDTH)
    )
    keys_rot = apply_rotation(
        projected[:, cut_keys:cut_values].reshape(sequence_length, group_heads, HEAD_WIDTH),
        cosine_table,
        sine_lookup,
    ).astype(LOW)
    mixture, log_sums = attention_forward(
        queries_rot, keys_rot, values_low, blocks, block_rows, scale
    )
    mixture_flat = mixture.reshape(sequence_length, query_heads * HEAD_WIDTH)
    partial_out = mul(mixture_flat, output_weight)
    attention_out = tensor_sum(partial_out.reshape(tensor_count, rows, width))

    gain_second = mixture_gain.astype(FULL)
    residual_mid = own_rows(activations).astype(FULL) + attention_out
    inverse_second = lax.rsqrt(
        jnp.mean(residual_mid * residual_mid, axis=-1, keepdims=True) + EPSILON
    )
    normed_second = residual_mid * inverse_second
    hidden_second = (normed_second * gain_second).astype(LOW)
    hidden_blocks = ring_gather(hidden_second)

    router_wide = jnp.pad(router_weight, ((0, 0), (0, LANES - num_experts)))
    columns = jnp.concatenate(
        [
            expert_index * local + jnp.arange(local, dtype=jnp.int32),
            (expert_index ^ 1) * local + jnp.arange(local, dtype=jnp.int32),
        ]
    ).astype(jnp.int32)
    step = max(1, min(512, rows * ring_size) // rows)
    y_parts, dh_parts, dgb_parts, hids = [], [], [], []
    for k in range(0, ring_size, step):
        join = lambda v: v[k] if step == 1 else jnp.concatenate(v[k : k + step])
        y, dh, hid, dgb = run_experts(
            columns,
            join(hidden_blocks),
            join(cotangent_blocks),
            join(code_blocks),
            router_wide,
            weight_shards,
            local,
            hidden,
        )
        hids.append(hid)
        for i in range(step):
            cut = slice(i * rows, (i + 1) * rows)
            y_parts.append(y[cut])
            dh_parts.append(dh[cut])
            dgb_parts.append(dgb[cut, :num_experts])
    dgb_sends = jnp.zeros((ring_size, 2, rows, num_experts), FULL)
    for k in range(ring_size):
        dgb_sends = lax.dynamic_update_slice(
            dgb_sends, dgb_parts[k][None, None], ((place - k) % ring_size, side, 0, 0)
        )
    d_gates = jnp.sum(
        lax.all_to_all(
            dgb_sends.reshape(expert_count, rows, num_experts), "expert", 0, 0, tiled=True
        ),
        axis=0,
    )

    hid = jnp.concatenate(hids)
    h_all = jnp.concatenate(hidden_blocks)
    g_all = jnp.concatenate(cotangent_blocks)
    middle = len(weight_shards) * 2 * wide
    d_first_weights = mul(hid[:, :middle], h_all, TN).astype(LOW)
    d_second_weights = mul(hid[:, middle:], g_all, TN).astype(LOW)

    d_hidden_moe = ring_sum(dh_parts)
    logits = mul(hidden_second, router_weight)
    picked = code[:, :num_experts] > 0.5
    kept = code[:, :num_experts] > 1.5
    gates = jax.nn.softmax(jnp.where(picked, logits, NEGATIVE), axis=-1)
    d_gates = jnp.where(kept, d_gates, 0.0)
    d_logits = (
        gates * (d_gates - jnp.sum(gates * d_gates, axis=-1, keepdims=True))
    ).astype(LOW)
    d_hidden_second = d_hidden_moe + mul(d_logits, router_weight, NT)
    grad_router = mul(hidden_second, d_logits, TN)
    grad_gain_second = jnp.sum(d_hidden_second * normed_second, axis=0)
    scaled = d_hidden_second * gain_second
    d_mid = cotangent_own.astype(FULL) + inverse_second * (
        scaled - normed_second * jnp.mean(scaled * normed_second, axis=-1, keepdims=True)
    )
    d_attention = tensor_gather(d_mid.astype(LOW))
    d_mixture = (
        mul(d_attention, output_weight, NT)
        .astype(LOW)
        .reshape(sequence_length, group_heads, group_size, HEAD_WIDTH)
    )
    d_queries, d_keys, d_values = attention_backward(
        queries_rot, keys_rot, values_low, blocks, log_sums, d_mixture, block_rows, scale
    )
    d_queries_low = (
        apply_rotation(
            d_queries.reshape(sequence_length, query_heads, HEAD_WIDTH),
            cosine_table,
            sine_lookup,
            -1.0,
        )
        .astype(LOW)
        .reshape(sequence_length, query_heads * HEAD_WIDTH)
    )
    d_keys_low = (
        apply_rotation(d_keys, cosine_table, sine_lookup, -1.0)
        .astype(LOW)
        .reshape(sequence_length, group_heads * HEAD_WIDTH)
    )
    d_values_low = d_values.astype(LOW).reshape(sequence_length, group_heads * HEAD_WIDTH)
    d_projected = jnp.concatenate([d_queries_low, d_keys_low, d_values_low], axis=1)
    d_first_part = mul(d_projected, weight_all, NT)
    grad_gain_first = jnp.sum(d_first_part * (residual_in * inverse_first), axis=0)
    d_first = tensor_sum(d_first_part.reshape(tensor_count, rows, width))
    inverse_own = own_rows(inverse_first)
    normed_own = own_rows(activations).astype(FULL) * inverse_own
    scaled = d_first * gain_first
    d_in = d_mid + inverse_own * (
        scaled - normed_own * jnp.mean(scaled * normed_own, axis=-1, keepdims=True)
    )
    input_gradient = tensor_gather(d_in.astype(LOW)).astype(FULL)
    grad_projected = expert_sum(mul(hidden_first, d_projected, TN))
    grad_output = expert_sum(mul(mixture_flat, d_attention, TN))

    output = tensor_gather((residual_mid + ring_sum(y_parts)).astype(LOW))

    shard_count = len(weight_shards)
    grads = scatter_weights(
        [
            jnp.concatenate(
                [
                    d_first_weights[s * 2 * wide : (s + 1) * 2 * wide],
                    d_second_weights[s * wide : (s + 1) * wide],
                ]
            )
            for s in range(shard_count)
        ]
    )
    grad_gate = grads[:wide].reshape(local, hidden, width).transpose(0, 2, 1)
    grad_up = grads[wide : 2 * wide].reshape(local, hidden, width).transpose(0, 2, 1)
    grad_down = grads[2 * wide :].reshape(local, hidden, width)

    small = lax.psum(
        jnp.concatenate(
            [grad_gain_first[None], grad_gain_second[None], grad_router.T], axis=0
        ),
        ("expert", "tensor"),
    )
    return (
        output,
        input_gradient,
        small[0],
        grad_projected[:, :cut_keys],
        grad_projected[:, cut_keys:cut_values],
        grad_projected[:, cut_values:],
        grad_output,
        small[1],
        small[2:].T,
        grad_gate,
        grad_up,
        grad_down,
    )


def solution(mesh):
    in_specs = (
        P("expert", None),
        P("expert", None),
        P("expert", None),
        P("expert", None),
        P("expert", None),
        P(),
        P(None, "tensor"),
        P(None, "tensor"),
        P(None, "tensor"),
        P("tensor", None),
        P(),
        P(),
        P("expert", None, "tensor"),
        P("expert", None, "tensor"),
        P("expert", "tensor", None),
    )
    out_specs = (
        P("expert", None),
        P("expert", None),
        P(),
        P(None, "tensor"),
        P(None, "tensor"),
        P(None, "tensor"),
        P("tensor", None),
        P(),
        P(),
        P("expert", None, "tensor"),
        P("expert", None, "tensor"),
        P("expert", "tensor", None),
    )
    return jax.shard_map(shards, mesh=mesh, in_specs=in_specs, out_specs=out_specs, check_vma=False)
```

time: 1400 us -> 888 us (0.63)
  waiting for transfers between devices: 634 us -> 404 us
  blocking collectives: 202 us -> 0 us
  matrix products: 254 us -> 108 us
  Pallas kernels: 0 us -> 65.3 us
  local copies, waits for them, and re-layouts: 185 us -> 140 us
  starting transfers between devices: 16.5 us -> 45.3 us
  other arithmetic: 83.4 us -> 97.4 us
    ppermute x0 -> x57, waiting for transfers between devices: none -> 281 us  [the longest x27 172 us: ring(): lax.ppermute(values, 'expert', [(i, (i + 2) % count) for i in range(count)])]
    all_to_all x3 -> x1, waiting for transfers between devices: 275 us -> 24.9 us  [shards(): lax.all_to_all(dgb_sends.reshape(expert_count, rows, num_experts), 'exper...]
    psum x4 -> x1, waiting for transfers between devices: 314 us -> 97.8 us  [shards(): lax.psum(jnp.concatenate([grad_gain_first[None], grad_gain_second[None],...]
    dot_general x31 -> x13, matrix products: 207 us -> 55.5 us  [the longest x11 51.4 us: mul(): return lax.dot_general(left, right, dims, preferred_element_type=FULL)]
    all_to_all x1 -> x0, blocking collectives: 142 us -> none  [shards(): lax.all_to_all(d_rows, 'expert', split_axis=1, concat_axis=1, tiled=True)]
    pallas_call x0 -> x2, Pallas kernels: none -> 65.3 us  [run_experts(): pl.pallas_call(functools.partial(expert_body, count, local, hidden, row_t...]
    reshape x6 -> x2, local copies, waits for them, and re-layouts: 71.3 us -> 6.04 us  [the longest x1 3.02 us: shards(): grad_gate = grads[:wide].reshape(local, hidden, width).transpose(0, 2, 1)]
    psum x3 -> x0, blocking collectives: 60 us -> none  [the longest x1 37.6 us: shards(): lax.psum(grad_gain_first.astype(jnp.bfloat16), 'expert').astype(jnp.float32)]
  transfers between devices with their start and end apart: 13 -> 59, of which waited for: 8 -> 26; matrix products, arithmetic and copies ran while one was open for 24% -> 26% of each run, Pallas kernels for 0% -> 0%
where the time goes in v1:
time: 888 us; the launch traced here: 879 us
  waiting for transfers between devices  404 us (45%)
  local copies, waits for them, and re-layouts  140 us (16%)
  matrix products  108 us (12%)
  other arithmetic  97.4 us (11%)
  Pallas kernels  65.3 us (7%)
  starting transfers between devices  45.3 us (5%)
  between operations  16 us (2%)
    ppermute x27, waiting for transfers between devices, ring(): lax.ppermute(values, 'expert', [(i, (i + 2) % count) for i in range(count)])  172 us
    ppermute x30, waiting for transfers between devices, swap(): return lax.ppermute(values, axis, [(i, i ^ bit) for i in range(count)])  110 us
    psum x1, waiting for transfers between devices, shards(): lax.psum(jnp.concatenate([grad_gain_first[None], grad_gain_second[None],...  97.8 us
    pallas_call x2, Pallas kernels, run_experts(): pl.pallas_call(functools.partial(expert_body, count, local, hidden, row_t...  65.3 us
    dot_general x11, matrix products, mul(): return lax.dot_general(left, right, dims, preferred_element_type=FULL)  51.4 us
    dynamic_update_slice x4, local copies, waits for them, and re-layouts, attention_backward(): lax.scan(one_block, (zeros_kv, zeros_kv), (jnp.arange(block_count, dtype=...  31.4 us
    unnamed x170, local copies, waits for them, and re-layouts  28.2 us
    all_to_all x1, waiting for transfers between devices, shards(): lax.all_to_all(dgb_sends.reshape(expert_count, rows, num_experts), 'exper...  24.9 us
  transfers between devices with their start and end apart: 59, of which 26 were waited for; matrix products, arithmetic and copies ran while one was open for 26% of the time, Pallas kernels for 0%

profile of v1, /device:TPU:0, one launch (start us, length us, event | category | flops | bytes accessed | tf_op | source)
XLA Modules:
  0.0 879.1 jit_solution(3716651453011497602)
XLA Ops:
  18.8 24.4 %while.27 = (s32[]{:T(128)}, bf16[2,512,2,3,64]{1,4,3,2,0:T(8,128)(2,1)S(1)}, f32[2,2,3,512,1]{3,2,1,4,0:T(4,128)S(1)}, s32[1,1024]{1,0:T(1,128)S(1)}, s32[2]{0:...) while((s32[]{:T(128)}, ...), condition=%wide.region_4.5_spmd, body=%wide.region_1.4_spmd.sunk | while | flops 843772928 | bytes 41285828 | solution.py:73
  63.4 18.6 %collective-permute-done.3 = bf16[256,1536]{1,0:T(8,128)(2,1)} collective-permute-done((bf16[256,1536]{1,0:T(8,128)(2,1)S(1)}, bf16[256,1536]{1,0:T(8,128)(2,1)}, u32[]{:S(2)}, u32[]{:S(2)}) %collective-permute-start.3) | collective-permute-done | bytes 786464 | tf_op jit(solution)/shard_map/ppermute | solution.py:236
  89.0 22.5 %collective-permute-done.6.rest_2_ = bf16[768,1536]{1,0:T(8,128)(2,1)} collective-permute-done((bf16[768,1536]{1,0:T(8,128)(2,1)}, bf16[768,1536]{1,0:T(8,128)(2,1)}, u32[]{:S(2)}, u32[]{:S(2)}) %collective-permute-start.6) | collective-permute-done | bytes 2359328 | tf_op jit(solution)/shard_map/ppermute | solution.py:227
  145.8 14.4 %collective-permute-done.11 = bf16[384,1536]{1,0:T(8,128)(2,1)S(1)} collective-permute-done((bf16[384,1536]{1,0:T(8,128)(2,1)S(1)}, bf16[384,1536]{1,0:T(8,128)(2,1)S(1)}, u32[]{:S(2)}, u32[]{:S(2)}) %collective-permute-start.11) | collective-permute-done | bytes 1179680 | tf_op jit(solution)/shard_map/ppermute | solution.py:227
  161.9 8.7 collective-permute-done.2
  180.7 11.2 %collective-permute-done.14 = bf16[256,1536]{1,0:T(8,128)(2,1)} collective-permute-done((bf16[256,1536]{1,0:T(8,128)(2,1)}, bf16[256,1536]{1,0:T(8,128)(2,1)}, u32[]{:S(2)}, u32[]{:S(2)}) %collective-permute-start.14) | collective-permute-done | bytes 786464 | tf_op jit(solution)/shard_map/ppermute | solution.py:236
  198.5 14.3 %collective-permute-done.15 = bf16[256,1536]{1,0:T(8,128)(2,1)S(1)} collective-permute-done((bf16[256,1536]{1,0:T(8,128)(2,1)}, bf16[256,1536]{1,0:T(8,128)(2,1)S(1)}, u32[]{:S(2)}, u32[]{:S(2)}) %collective-permute-start.15) | collective-permute-done | bytes 786464 | tf_op jit(solution)/shard_map/ppermute | solution.py:236
  215.4 32.6 %experts.2 = (bf16[512,1536]{1,0:T(8,128)(2,1)S(1)}, bf16[512,1536]{1,0:T(8,128)(2,1)S(1)}, bf16[512,6144]{1,0:T(8,128)(2,1)}, f32[512,128]{1,0:T(8,128)S(1)}) custom-call(s32[4]{0:T(128)S(1)} %pad_add_fusion.columns_ref, bf16[512,1536]{1,0:T(8,128)(2,1)} %pad_maximum_fusion.9.h_ref, bf16[512,1536]{1,0:T(8,128)(2,1)} %pad_maximum_fusion.10.g_ref, ...), custom_call_target="tpu_custom_call" | custom-call | flops 19327352832 | bytes 31457280 | tf_op jit(solution)/shard_map/experts/pallas_call | solution.py:197
  248.1 6.7 constant_dynamic-update-slice_fusion.6
  254.8 32.7 %experts.3 = (bf16[512,1536]{1,0:T(8,128)(2,1)S(1)}, bf16[512,1536]{1,0:T(8,128)(2,1)S(1)}, bf16[512,6144]{1,0:T(8,128)(2,1)}, f32[512,128]{1,0:T(8,128)S(1)}) custom-call(s32[4]{0:T(128)S(1)} %pad_add_fusion.columns_ref, bf16[512,1536]{1,0:T(8,128)(2,1)} %pad_maximum_fusion.11.h_ref, bf16[512,1536]{1,0:T(8,128)(2,1)} %pad_maximum_fusion.12.g_ref, ...), custom_call_target="tpu_custom_call" | custom-call | flops 19327352832 | bytes 31457280 | tf_op jit(solution)/shard_map/experts/pallas_call | solution.py:197
  296.7 20.5 %convolution_convert_fusion = bf16[4096,1536]{1,0:T(8,128)(2,1)} fusion(bf16[1024,6144]{1,0:T(8,128)(2,1)} %constant_dynamic-update-slice_fusion.5, bf16[256,1536]{1,0:T(8,128)(2,1)} %copy-done.66, bf16[256,1536]{1,0:T(8,128)(2,1)} %collective-permute-done.14, bf16[256,1536]{1,0:T(8,128)(2,1)} %collective-permute-done.2, bf16[256,1536]{1,0:T(8,128)(2,1)} %copy-done.20), kind=kOutput, calls=%fused_computation.54 | convolution fusion | flops 12903776256 | bytes 24117248 | tf_op jit(solution)/shard_map/dot_general | solution.py:23
  317.2 8.1 fusion.111
  325.4 10.0 %convolution_convert_fusion.1 = bf16[2048,1536]{1,0:T(8,128)(2,1)S(1)} fusion(bf16[1024,6144]{1,0:T(8,128)(2,1)} %constant_dynamic-update-slice_fusion.5, bf16[256,1536]{1,0:T(8,128)(2,1)S(1)} %copy-done.65, bf16[256,1536]{1,0:T(8,128)(2,1)} %collective-permute-done.16, bf16[256,1536]{1,0:T(8,128)(2,1)} %collective-permute-done.3, ...), kind=kOutput, calls=%fused_computation.58 | convolution fusion | flops 6458179584 | bytes 13631488 | tf_op jit(solution)/shard_map/dot_general | solution.py:23
  360.3 24.9 %all-to-all-done = f32[8,256,16]{1,2,0:T(8,128)S(1)} async-done(((f32[8,256,16]{1,2,0:T(8,128)}), f32[8,256,16]{1,2,0:T(8,128)S(1)}, u32[]{:S(2)}, u32[]{:S(2)}) %all-to-all-start) | async-done | bytes 131104 | tf_op jit(solution)/shard_map/all_to_all | solution.py:474
  390.0 19.5 %collective-permute-done.20 = bf16[256,1536]{1,0:T(8,128)(2,1)S(1)} collective-permute-done((bf16[256,1536]{1,0:T(8,128)(2,1)S(1)}, bf16[256,1536]{1,0:T(8,128)(2,1)S(1)}, u32[]{:S(2)}, u32[]{:S(2)}) %collective-permute-start.20) | collective-permute-done | bytes 786464 | tf_op jit(solution)/shard_map/ppermute | solution.py:236
  409.8 15.7 %collective-permute-done.25 = bf16[256,1536]{1,0:T(8,128)(2,1)S(1)} collective-permute-done((bf16[256,1536]{1,0:T(8,128)(2,1)S(1)}, bf16[256,1536]{1,0:T(8,128)(2,1)S(1)}, u32[]{:S(2)}, u32[]{:S(2)}) %collective-permute-start.25) | collective-permute-done | bytes 786464 | tf_op jit(solution)/shard_map/ppermute | solution.py:236
  428.4 34.3 %collective-permute-done.26 = bf16[256,1536]{1,0:T(8,128)(2,1)S(1)} collective-permute-done((bf16[256,1536]{1,0:T(8,128)(2,1)S(1)}, bf16[256,1536]{1,0:T(8,128)(2,1)S(1)}, u32[]{:S(2)}, u32[]{:S(2)}) %collective-permute-start.26) | collective-permute-done | bytes 786464 | tf_op jit(solution)/shard_map/ppermute | solution.py:236
  475.7 12.9 %collective-permute-done.27 = bf16[1,256,1536]{2,1,0:T(8,128)(2,1)S(1)} collective-permute-done((bf16[1,256,1536]{2,1,0:T(8,128)(2,1)S(1)}, bf16[1,256,1536]{2,1,0:T(8,128)(2,1)S(1)}, u32[]{:S(2)}, u32[]{:S(2)}) %collective-permute-start.27) | collective-permute-done | bytes 786464 | tf_op jit(solution)/shard_map/ppermute | solution.py:227
  488.9 38.6 %collective-permute-done.22 = bf16[1,256,1536]{2,1,0:T(8,128)(2,1)S(1)} collective-permute-done((bf16[1,256,1536]{2,1,0:T(8,128)(2,1)S(1)}, bf16[1,256,1536]{2,1,0:T(8,128)(2,1)S(1)}, u32[]{:S(2)}, u32[]{:S(2)}) %collective-permute-start.22) | collective-permute-done | bytes 786464 | tf_op jit(solution)/shard_map/ppermute | solution.py:227
  543.6 100.6 %while.28 = (s32[]{:T(128)}, f32[1024,2,64]{0,2,1:T(8,128)S(1)}, f32[1024,2,64]{0,2,1:T(8,128)}, f32[2,512,2,3,64]{1,0,4,3,2:T(2,128)}, s32[2]{0:T(128)S(1)}, /*...) while((s32[]{:T(128)}, f32[1024,2,64]{0,2,1:T(8,128)S(1)}, ...), condition=%wide.region_13.14_spmd.clone, body=%wide.region_11.13_spmd.clone.sunk | while | flops 2061825024 | bytes 191994320 | solution.py:109
  548.1 7.1 fusion.162
  555.3 6.8 fusion.163
  567.6 14.9 %dynamic_update_slice.82 = f32[2,512,2,3,64]{1,0,4,3,2:T(2,128)} dynamic-update-slice(f32[2,512,2,3,64]{1,0,4,3,2:T(2,128)} %get-tuple-element.512, f32[1,512,2,3,64]{1,0,4,3,2:T(1,128)S(1)} %copy.107, s32[]{:T(128)} %get-tuple-element.509, s32[]{:T(128)} %constant.298.clone.1..sunk.1, s32[]{:T(128)} %constant.298.clone.1..sunk.1, s32[]{:T(128)} %constant.298.clone.1..sunk.1, ...) | dynamic-update-slice | bytes 1572868 | tf_op jit(solution)/shard_map/while/body/jit(dynamic_update_index_in_dim)/dynamic_update_slice | solution.py:109
  586.7 6.5 fusion.165
  598.3 7.1 fusion.162
  605.4 6.8 fusion.163
  617.8 14.9 %dynamic_update_slice.82 = f32[2,512,2,3,64]{1,0,4,3,2:T(2,128)} dynamic-update-slice(f32[2,512,2,3,64]{1,0,4,3,2:T(2,128)} %get-tuple-element.512, f32[1,512,2,3,64]{1,0,4,3,2:T(1,128)S(1)} %copy.107, s32[]{:T(128)} %get-tuple-element.509, s32[]{:T(128)} %constant.298.clone.1..sunk.1, s32[]{:T(128)} %constant.298.clone.1..sunk.1, s32[]{:T(128)} %constant.298.clone.1..sunk.1, ...) | dynamic-update-slice | bytes 1572868 | tf_op jit(solution)/shard_map/while/body/jit(dynamic_update_index_in_dim)/dynamic_update_slice | solution.py:109
  636.9 6.4 fusion.165
  678.5 97.8 %all-reduce.3.cloned.1.call-done = f32[18,1536]{1,0:T(8,128)} async-done(((f32[18,1536]{1,0:T(8,128)}), f32[18,1536]{1,0:T(8,128)}) %all-reduce.3.cloned.1.call-update) | async-done | bytes 110608 | tf_op jit(solution)/shard_map/psum | solution.py:560
  822.0 8.0 collective-permute-done.37
  838.5 7.9 collective-permute-done.39
  850.2 14.7 %collective-permute-done.40 = bf16[768,640]{1,0:T(8,128)(2,1)S(1)} collective-permute-done((bf16[768,640]{1,0:T(8,128)(2,1)S(1)}, bf16[768,640]{1,0:T(8,128)(2,1)S(1)}, u32[]{:S(2)}, u32[]{:S(2)}) %collective-permute-start.40) | collective-permute-done | bytes 983072 | tf_op jit(solution)/shard_map/ppermute | solution.py:227
  (488 shorter events, 314.4 us)
Async XLA Ops:
  50.6 31.4 %collective-permute-start = (bf16[2,256,1536]{2,1,0:T(8,128)(2,1)}, bf16[2,256,1536]{2,1,0:T(8,128)(2,1)}, u32[]{:S(2)}, u32[]{:S(2)}) collective-permute-start(bf16[2,256,1536]{2,1,0:T(8,128)(2,1)} %fusion.76), channel_id=1, source_target_pairs={{0,1},{1,0},{2,3},{3,2},{4,5},{5,4},{6,7},{7,6},{8,9},{9,8},{10,11... | collective-permute-start | bytes 4718600 | tf_op jit(solution)/shard_map/ppermute | solution.py:227
  56.6 54.9 %collective-permute-start.6 = (bf16[768,1536]{1,0:T(8,128)(2,1)}, bf16[768,1536]{1,0:T(8,128)(2,1)}, u32[]{:S(2)}, u32[]{:S(2)}) collective-permute-start(bf16[768,1536]{1,0:T(8,128)(2,1)} %pad_maximum_fusion.2.rest_0_), channel_id=1, source_target_pairs={{0,2},{1,3},{2,0},{3,1},{4,6},{5,7},{6,4},{7,5},{8,10},{9,11},{10,... | collective-permute-start | bytes 7077896 | tf_op jit(solution)/shard_map/ppermute | solution.py:227
  61.9 68.4 %collective-permute-start.8 = (bf16[768,1536]{1,0:T(8,128)(2,1)}, bf16[768,1536]{1,0:T(8,128)(2,1)}, u32[]{:S(2)}, u32[]{:S(2)}) collective-permute-start(bf16[768,1536]{1,0:T(8,128)(2,1)} %pad_maximum_fusion.2.rest_0_), channel_id=1, source_target_pairs={{0,4},{4,0},{8,12},{12,8},{16,20},{20,16},{24,28},{28,24},{1,5},{5... | collective-permute-start | bytes 7077896 | tf_op jit(solution)/shard_map/ppermute | solution.py:227
  82.0 48.3 %collective-permute-start.16 = (bf16[256,1536]{1,0:T(8,128)(2,1)}, bf16[256,1536]{1,0:T(8,128)(2,1)}, u32[]{:S(2)}, u32[]{:S(2)}) collective-permute-start(bf16[256,1536]{1,0:T(8,128)(2,1)} %collective-permute-done.3), channel_id=1, source_target_pairs={{0,8},{4,12},{8,16},{12,20},{16,24},{20,28},{24,0},{28,4},{1,9},{5... | collective-permute-start | bytes 2359304 | tf_op jit(solution)/shard_map/ppermute | solution.py:236
  86.6 45.1 %collective-permute-start.1 = (bf16[1,256,1536]{2,1,0:T(8,128)(2,1)S(1)}, bf16[1,256,1536]{2,1,0:T(8,128)(2,1)S(1)}, u32[]{:S(2)}, u32[]{:S(2)}) collective-permute-start(bf16[1,256,1536]{2,1,0:T(8,128)(2,1)S(1)} %dynamic-slice_convert_fusion.2), channel_id=1, source_target_pairs={{0,2},{1,3},{2,0},{3,1},{4,6},{5,7},{6,4},{7,5},{8,10},{9,11},{10,... | collective-permute-start | bytes 2359304 | tf_op jit(solution)/shard_map/ppermute | solution.py:227
  130.3 85.1 %collective-permute-start.5 = (bf16[768,1536]{1,0:T(8,128)(2,1)}, bf16[768,1536]{1,0:T(8,128)(2,1)}, u32[]{:S(2)}, u32[]{:S(2)}) collective-permute-start(bf16[768,1536]{1,0:T(8,128)(2,1)} %pad_maximum_fusion.2.rest_0_), channel_id=1, source_target_pairs={{0,1},{1,0},{2,3},{3,2},{4,5},{5,4},{6,7},{7,6},{8,9},{9,8},{10,11... | collective-permute-start | bytes 7077896 | tf_op jit(solution)/shard_map/ppermute | solution.py:227
  130.3 31.5 %collective-permute-start.17 = (bf16[256,1536]{1,0:T(8,128)(2,1)}, bf16[256,1536]{1,0:T(8,128)(2,1)S(1)}, u32[]{:S(2)}, u32[]{:S(2)}) collective-permute-start(bf16[256,1536]{1,0:T(8,128)(2,1)} %collective-permute-done.16), channel_id=1, source_target_pairs={{0,8},{4,12},{8,16},{12,20},{16,24},{20,28},{24,0},{28,4},{1,9},{5... | collective-permute-start | bytes 2359304 | tf_op jit(solution)/shard_map/ppermute | solution.py:236
  160.2 55.3 %collective-permute-start.7 = (bf16[768,1536]{1,0:T(8,128)(2,1)}, bf16[768,1536]{1,0:T(8,128)(2,1)}, u32[]{:S(2)}, u32[]{:S(2)}) collective-permute-start(bf16[768,1536]{1,0:T(8,128)(2,1)} %collective-permute-done.6.rest_2_), channel_id=1, source_target_pairs={{0,1},{1,0},{2,3},{3,2},{4,5},{5,4},{6,7},{7,6},{8,9},{9,8},{10,11... | collective-permute-start | bytes 7077896 | tf_op jit(solution)/shard_map/ppermute | solution.py:227
  161.3 54.2 %collective-permute-start.9 = (bf16[768,1536]{1,0:T(8,128)(2,1)}, bf16[768,1536]{1,0:T(8,128)(2,1)}, u32[]{:S(2)}, u32[]{:S(2)}) collective-permute-start(bf16[768,1536]{1,0:T(8,128)(2,1)} %collective-permute-done.8.rest_4_), channel_id=1, source_target_pairs={{0,1},{1,0},{2,3},{3,2},{4,5},{5,4},{6,7},{7,6},{8,9},{9,8},{10,11... | collective-permute-start | bytes 7077896 | tf_op jit(solution)/shard_map/ppermute | solution.py:227
  161.8 53.7 %collective-permute-start.12 = (bf16[768,1536]{1,0:T(8,128)(2,1)}, bf16[768,1536]{1,0:T(8,128)(2,1)}, u32[]{:S(2)}, u32[]{:S(2)}) collective-permute-start(bf16[768,1536]{1,0:T(8,128)(2,1)} %constant_dynamic-update-slice_fusion.3.rest_6_), channel_id=1, source_target_pairs={{0,1},{1,0},{2,3},{3,2},{4,5},{5,4},{6,7},{7,6},{8,9},{9,8},{10,11... | collective-permute-start | bytes 7077896 | tf_op jit(solution)/shard_map/ppermute | solution.py:227
  339.0 452.3 %collective-permute-start.49 = (bf16[768,1536]{1,0:T(8,128)(2,1)}, bf16[768,1536]{1,0:T(8,128)(2,1)}, u32[]{:S(2)}, u32[]{:S(2)}) collective-permute-start(bf16[768,1536]{1,0:T(8,128)(2,1)} %pad_maximum_fusion.3), channel_id=1, source_target_pairs={{0,1},{1,0},{2,3},{3,2},{4,5},{5,4},{6,7},{7,6},{8,9},{9,8},{10,11... | collective-permute-start | bytes 7077896 | tf_op jit(solution)/shard_map/ppermute | solution.py:227
  340.5 129.1 %collective-permute-start.50 = (bf16[768,1536]{1,0:T(8,128)(2,1)}, bf16[768,1536]{1,0:T(8,128)(2,1)}, u32[]{:S(2)}, u32[]{:S(2)}) collective-permute-start(bf16[768,1536]{1,0:T(8,128)(2,1)} %pad_maximum_fusion.4), channel_id=1, source_target_pairs={{0,1},{1,0},{2,3},{3,2},{4,5},{5,4},{6,7},{7,6},{8,9},{9,8},{10,11... | collective-permute-start | bytes 7077896 | tf_op jit(solution)/shard_map/ppermute | solution.py:227
  342.6 83.1 %collective-permute-start.51 = (bf16[768,1536]{1,0:T(8,128)(2,1)}, bf16[768,1536]{1,0:T(8,128)(2,1)}, u32[]{:S(2)}, u32[]{:S(2)}) collective-permute-start(bf16[768,1536]{1,0:T(8,128)(2,1)} %pad_maximum_fusion.5), channel_id=1, source_target_pairs={{0,1},{1,0},{2,3},{3,2},{4,5},{5,4},{6,7},{7,6},{8,9},{9,8},{10,11... | collective-permute-start | bytes 7077896 | tf_op jit(solution)/shard_map/ppermute | solution.py:227
  343.5 42.0 %collective-permute-start.13 = (bf16[256,1536]{1,0:T(8,128)(2,1)}, bf16[256,1536]{1,0:T(8,128)(2,1)}, u32[]{:S(2)}, u32[]{:S(2)}) collective-permute-start(bf16[256,1536]{1,0:T(8,128)(2,1)} %slice.256), channel_id=1, source_target_pairs={{0,8},{4,12},{8,16},{12,20},{16,24},{20,28},{24,0},{28,4},{1,9},{5... | collective-permute-start | bytes 2359304 | tf_op jit(solution)/shard_map/ppermute | solution.py:236
  349.5 35.6 %all-to-all-start = ((f32[8,256,16]{1,2,0:T(8,128)}), f32[8,256,16]{1,2,0:T(8,128)S(1)}, u32[]{:S(2)}, u32[]{:S(2)}) async-start(f32[8,256,16]{1,2,0:T(8,128)} %bitcast.53), calls=%async_computation | async-start | bytes 262144 | tf_op jit(solution)/shard_map/all_to_all | solution.py:474
  354.6 421.7 %all-reduce.3.cloned.1.call-start = ((), (), s32[]{:S(2)}) async-start(), calls=%async_computation.1 | async-start | bytes 294912 | tf_op jit(solution)/shard_map/psum | solution.py:560
  355.6 31.8 %collective-permute-start.24 = (bf16[256,1536]{1,0:T(8,128)(2,1)}, bf16[256,1536]{1,0:T(8,128)(2,1)}, u32[]{:S(2)}, u32[]{:S(2)}) collective-permute-start(bf16[256,1536]{1,0:T(8,128)(2,1)} %slice.260), channel_id=1, source_target_pairs={{0,8},{4,12},{8,16},{12,20},{16,24},{20,28},{24,0},{28,4},{1,9},{5... | collective-permute-start | bytes 2359304 | tf_op jit(solution)/shard_map/ppermute | solution.py:236
  388.9 36.6 %collective-permute-start.25 = (bf16[256,1536]{1,0:T(8,128)(2,1)S(1)}, bf16[256,1536]{1,0:T(8,128)(2,1)S(1)}, u32[]{:S(2)}, u32[]{:S(2)}) collective-permute-start(bf16[256,1536]{1,0:T(8,128)(2,1)S(1)} %add_convert_fusion.2), channel_id=1, source_target_pairs={{0,8},{4,12},{8,16},{12,20},{16,24},{20,28},{24,0},{28,4},{1,9},{5... | collective-permute-start | bytes 2359304 | tf_op jit(solution)/shard_map/ppermute | solution.py:236
  409.5 63.2 %collective-permute-start.54 = (bf16[768,1536]{1,0:T(8,128)(2,1)S(1)}, bf16[768,1536]{1,0:T(8,128)(2,1)S(1)}, u32[]{:S(2)}, u32[]{:S(2)}) collective-permute-start(bf16[768,1536]{1,0:T(8,128)(2,1)S(1)} %copy-done.51), channel_id=1, source_target_pairs={{0,1},{1,0},{2,3},{3,2},{4,5},{5,4},{6,7},{7,6},{8,9},{9,8},{10,11... | collective-permute-start | bytes 7077896 | tf_op jit(solution)/shard_map/ppermute | solution.py:227
  425.5 39.0 %collective-permute-start.21 = (bf16[256,1536]{1,0:T(8,128)(2,1)S(1)}, bf16[256,1536]{1,0:T(8,128)(2,1)S(1)}, u32[]{:S(2)}, u32[]{:S(2)}) collective-permute-start(bf16[256,1536]{1,0:T(8,128)(2,1)S(1)} %add_convert_fusion.4), channel_id=1, source_target_pairs={{0,8},{4,12},{8,16},{12,20},{16,24},{20,28},{24,0},{28,4},{1,9},{5... | collective-permute-start | bytes 2359304 | tf_op jit(solution)/shard_map/ppermute | solution.py:236
  425.7 37.1 %collective-permute-start.26 = (bf16[256,1536]{1,0:T(8,128)(2,1)S(1)}, bf16[256,1536]{1,0:T(8,128)(2,1)S(1)}, u32[]{:S(2)}, u32[]{:S(2)}) collective-permute-start(bf16[256,1536]{1,0:T(8,128)(2,1)S(1)} %add_convert_fusion.1), channel_id=1, source_target_pairs={{0,8},{4,12},{8,16},{12,20},{16,24},{20,28},{24,0},{28,4},{1,9},{5... | collective-permute-start | bytes 2359304 | tf_op jit(solution)/shard_map/ppermute | solution.py:236
  462.7 67.1 %collective-permute-start.52 = (bf16[384,1536]{1,0:T(8,128)(2,1)S(1)}, bf16[384,1536]{1,0:T(8,128)(2,1)S(1)}, u32[]{:S(2)}, u32[]{:S(2)}) collective-permute-start(bf16[384,1536]{1,0:T(8,128)(2,1)S(1)} %get-tuple-element.267), channel_id=1, source_target_pairs={{0,4},{4,0},{8,12},{12,8},{16,20},{20,16},{24,28},{28,24},{1,5},{5... | collective-permute-start | bytes 3538952 | tf_op jit(solution)/shard_map/ppermute | solution.py:227
  472.1 61.1 %collective-permute-start.55 = (bf16[384,1536]{1,0:T(8,128)(2,1)S(1)}, bf16[384,1536]{1,0:T(8,128)(2,1)S(1)}, u32[]{:S(2)}, u32[]{:S(2)}) collective-permute-start(bf16[384,1536]{1,0:T(8,128)(2,1)S(1)} %get-tuple-element.268), channel_id=1, source_target_pairs={{0,2},{1,3},{2,0},{3,1},{4,6},{5,7},{6,4},{7,5},{8,10},{9,11},{10,... | collective-permute-start | bytes 3538952 | tf_op jit(solution)/shard_map/ppermute | solution.py:227
  475.0 52.5 %collective-permute-start.22 = (bf16[1,256,1536]{2,1,0:T(8,128)(2,1)S(1)}, bf16[1,256,1536]{2,1,0:T(8,128)(2,1)S(1)}, u32[]{:S(2)}, u32[]{:S(2)}) collective-permute-start(bf16[1,256,1536]{2,1,0:T(8,128)(2,1)S(1)} %get-tuple-element.281), channel_id=1, source_target_pairs={{0,2},{1,3},{2,0},{3,1},{4,6},{5,7},{6,4},{7,5},{8,10},{9,11},{10,... | collective-permute-start | bytes 2359304 | tf_op jit(solution)/shard_map/ppermute | solution.py:227
  488.8 47.5 %collective-permute-start.28 = (bf16[2,256,1536]{2,1,0:T(8,128)(2,1)S(1)}, bf16[2,256,1536]{2,1,0:T(8,128)(2,1)S(1)}, u32[]{:S(2)}, u32[]{:S(2)}) collective-permute-start(bf16[2,256,1536]{2,1,0:T(8,128)(2,1)S(1)} %maximum_bitcast_fusion.1), channel_id=1, source_target_pairs={{0,1},{1,0},{2,3},{3,2},{4,5},{5,4},{6,7},{7,6},{8,9},{9,8},{10,11... | collective-permute-start | bytes 4718600 | tf_op jit(solution)/shard_map/ppermute | solution.py:227
  529.8 132.7 %collective-permute-start.23 = (bf16[2,256,1536]{2,1,0:T(8,128)(2,1)}, bf16[2,256,1536]{2,1,0:T(8,128)(2,1)}, u32[]{:S(2)}, u32[]{:S(2)}) collective-permute-start(bf16[2,256,1536]{2,1,0:T(8,128)(2,1)} %maximum_bitcast_fusion), channel_id=1, source_target_pairs={{0,1},{1,0},{2,3},{3,2},{4,5},{5,4},{6,7},{7,6},{8,9},{9,8},{10,11... | collective-permute-start | bytes 4718600 | tf_op jit(solution)/shard_map/ppermute | solution.py:227
  531.8 259.8 %collective-permute-start.53 = (bf16[768,1536]{1,0:T(8,128)(2,1)}, bf16[768,1536]{1,0:T(8,128)(2,1)}, u32[]{:S(2)}, u32[]{:S(2)}) collective-permute-start(bf16[768,1536]{1,0:T(8,128)(2,1)} %pad_maximum_fusion.6), channel_id=1, source_target_pairs={{0,2},{1,3},{2,0},{3,1},{4,6},{5,7},{6,4},{7,5},{8,10},{9,11},{10,... | collective-permute-start | bytes 7077896 | tf_op jit(solution)/shard_map/ppermute | solution.py:227
  535.2 256.4 %collective-permute-start.56 = (bf16[768,1536]{1,0:T(8,128)(2,1)}, bf16[768,1536]{1,0:T(8,128)(2,1)}, u32[]{:S(2)}, u32[]{:S(2)}) collective-permute-start(bf16[768,1536]{1,0:T(8,128)(2,1)} %pad_maximum_fusion.8), channel_id=1, source_target_pairs={{0,4},{4,0},{8,12},{12,8},{16,20},{20,16},{24,28},{28,24},{1,5},{5... | collective-permute-start | bytes 7077896 | tf_op jit(solution)/shard_map/ppermute | solution.py:227
  540.3 128.4 %collective-permute-start.41 = (bf16[192,1536]{1,0:T(8,128)(2,1)}, bf16[192,1536]{1,0:T(8,128)(2,1)}, u32[]{:S(2)}, u32[]{:S(2)}) collective-permute-start(bf16[192,1536]{1,0:T(8,128)(2,1)} %fusion.88), channel_id=1, source_target_pairs={{0,4},{4,0},{8,12},{12,8},{16,20},{20,16},{24,28},{28,24},{1,5},{5... | collective-permute-start | bytes 1769480 | tf_op jit(solution)/shard_map/ppermute | solution.py:227
  662.5 118.1 %collective-permute-start.33 = (bf16[768,640]{1,0:T(8,128)(2,1)S(1)}, bf16[768,640]{1,0:T(8,128)(2,1)S(1)}, u32[]{:S(2)}, u32[]{:S(2)}) collective-permute-start(bf16[768,640]{1,0:T(8,128)(2,1)S(1)} %fusion.80), channel_id=1, source_target_pairs={{0,4},{4,0},{8,12},{12,8},{16,20},{20,16},{24,28},{28,24},{1,5},{5... | collective-permute-start | bytes 2949128 | tf_op jit(solution)/shard_map/ppermute | solution.py:227
  678.5 100.9 %collective-permute-start.43 = (bf16[48,1536]{1,0:T(8,128)(2,1)S(1)}, bf16[48,1536]{1,0:T(8,128)(2,1)S(1)}, u32[]{:S(2)}, u32[]{:S(2)}) collective-permute-start(bf16[48,1536]{1,0:T(8,128)(2,1)S(1)} %fusion.95), channel_id=1, source_target_pairs={{0,8},{4,12},{8,16},{12,20},{16,24},{20,28},{24,0},{28,4},{1,9},{5... | collective-permute-start | bytes 442376 | tf_op jit(solution)/shard_map/ppermute | solution.py:236
  779.4 31.3 %collective-permute-start.29 = (bf16[2,256,1536]{2,1,0:T(8,128)(2,1)}, bf16[2,256,1536]{2,1,0:T(8,128)(2,1)}, u32[]{:S(2)}, u32[]{:S(2)}) collective-permute-start(bf16[2,256,1536]{2,1,0:T(8,128)(2,1)} %fusion.77), channel_id=1, source_target_pairs={{0,1},{1,0},{2,3},{3,2},{4,5},{5,4},{6,7},{7,6},{8,9},{9,8},{10,11... | collective-permute-start | bytes 4718600 | tf_op jit(solution)/shard_map/ppermute | solution.py:227
  (123 other events, 1504.9 us)
Sparse Core Ops, SparseCore 0:
  657.7 118.6 all-reduce.2

commit v2 on v1

v2 whole, which is shorter than its diff:
```python
import functools
import math

import jax
import jax.numpy as jnp
import numpy as np
from jax import lax
from jax.experimental import pallas as pl
from jax.experimental.pallas import tpu as pltpu
from jax.sharding import PartitionSpec as P

HEAD_WIDTH = 64
EPSILON = 1e-05
NEGATIVE = -1e30
LANES = 128
LOW = jnp.bfloat16
FULL = jnp.float32
NN = (((1,), (0,)), ((), ()))
NT = (((1,), (1,)), ((), ()))
TN = (((0,), (0,)), ((), ()))
BLOCK = 256
EXTRA = 32


def cost_of(flops, size):
    return pl.CostEstimate(flops=flops // 64, bytes_accessed=size // 64, transcendentals=0)


def tie(*values):
    return lax.optimization_barrier(values)


def mul(left, right, dims=NN):
    return lax.dot_general(left, right, dims, preferred_element_type=FULL)


def rope_tables(sequence_length):
    half_width = HEAD_WIDTH // 2
    frequency = np.exp(
        np.arange(half_width, dtype=np.float32) * np.float32(-2.0 * math.log(10000.0) / HEAD_WIDTH)
    )
    angles = np.arange(sequence_length, dtype=np.float32)[:, None] * frequency[None, :]
    cosine, sine = np.cos(angles), np.sin(angles)
    return (
        jnp.asarray(np.concatenate([cosine, cosine], axis=1)),
        jnp.asarray(np.concatenate([-sine, sine], axis=1)),
    )


def normalized(values):
    inverse = lax.rsqrt(jnp.mean(values * values, axis=-1, keepdims=True) + EPSILON)
    return inverse


def swapped(values):
    half = values.shape[1] // 2
    return jnp.concatenate([values[:, half:], values[:, :half]], axis=1)


def tiles_of(length, tile):
    return [(start, min(length, start + tile + BLOCK)) for start in range(0, length, tile)]


def front_body(heads, groups, x_ref, gain_ref, wq_ref, wk_ref, wv_ref, cos_ref, sin_ref,
               h_ref, q_ref, k_ref, v_ref):
    scale = HEAD_WIDTH ** (-0.5)
    x = x_ref[...].astype(FULL)
    h = (x * normalized(x) * gain_ref[...]).astype(LOW)
    h_ref[...] = h
    zq, zk, zv = mul(h, wq_ref[...]), mul(h, wk_ref[...]), mul(h, wv_ref[...])
    cosine, sine = cos_ref[...], sin_ref[...]
    for j in range(heads + groups):
        z, n = (zq, j) if j < heads else (zk, j - heads)
        part = z[:, n * HEAD_WIDTH : (n + 1) * HEAD_WIDTH]
        part = part * cosine + swapped(part) * sine
        if j < heads:
            q_ref[j] = (part.astype(LOW).astype(FULL) * scale).astype(LOW)
        else:
            k_ref[j - heads] = part.astype(LOW)
    for j in range(groups):
        v_ref[j] = zv[:, j * HEAD_WIDTH : (j + 1) * HEAD_WIDTH].astype(LOW)


def run_front(x, gain, weights, cosine, sine, heads, groups):
    length, width = x.shape
    tile = min(256, length)
    shape = jax.ShapeDtypeStruct
    fixed = lambda v: pl.BlockSpec(v.shape, lambda i: (0,) * v.ndim)
    strip = lambda columns: pl.BlockSpec((tile, columns), lambda i: (i, 0))
    of_heads = lambda n: pl.BlockSpec((n, tile, HEAD_WIDTH), lambda i: (0, i, 0))
    return pl.pallas_call(
        functools.partial(front_body, heads, groups),
        grid=(length // tile,),
        out_shape=[
            shape((length, width), LOW),
            shape((heads, length, HEAD_WIDTH), LOW),
            shape((groups, length, HEAD_WIDTH), LOW),
            shape((groups, length, HEAD_WIDTH), LOW),
        ],
        in_specs=[strip(width), fixed(gain)]
        + [fixed(w) for w in weights]
        + [strip(HEAD_WIDTH), strip(HEAD_WIDTH)],
        out_specs=[strip(width), of_heads(heads), of_heads(groups), of_heads(groups)],
        compiler_params=pltpu.CompilerParams(vmem_limit_bytes=32 * 1024 * 1024),
        cost_estimate=cost_of(8 * length * width * width, 12 * length * width),
        name="front",
    )(x, gain, *weights, cosine, sine)


def add_body(count, *refs):
    for i in range(count):
        total = refs[2 * i][...].astype(FULL) + refs[2 * i + 1][...].astype(FULL)
        refs[2 * count + i][...] = total.astype(LOW)


def run_adds(pairs):
    rows, width = pairs[0][0].shape
    tile = rows // 2
    count = len(pairs)
    block = pl.BlockSpec((tile, width), lambda i: (i, 0))
    specs, values = [], []
    for one in pairs:
        offset = one[2] // tile if len(one) > 2 else 0
        specs += [block, pl.BlockSpec((tile, width), lambda i, offset=offset: (i + offset, 0))]
        values += one[:2]
    return list(
        pl.pallas_call(
            functools.partial(add_body, count),
            grid=(rows // tile,),
            out_shape=[jax.ShapeDtypeStruct((rows, width), LOW)] * count,
            in_specs=specs,
            out_specs=[block] * count,
            compiler_params=pltpu.CompilerParams(vmem_limit_bytes=40 * 1024 * 1024),
            cost_estimate=cost_of(1000, 6 * count * rows * width),
            name="adds",
        )(*values)
    )


def attention_body(heads, groups, rows, tile, mine_ref, q_ref, k_ref, v_ref, wo_ref, column_ref,
                   row_ref, mix_ref, lse_ref, *rest):
    part_refs, (turned_ref, out_ref) = rest[:-2], rest[-2:]
    length = row_ref.shape[1]
    size = heads // groups
    for j in range(groups):
        turned_ref[j] = v_ref[j].astype(FULL).T.astype(LOW)

    for group in range(groups):
        for start, keys in tiles_of(length, tile):
            visible = column_ref[0:keys, :] <= row_ref[:, start : start + tile]

            @pl.loop(group * size, (group + 1) * size)
            def _(head, group=group, start=start, keys=keys, visible=visible):
                s = mul(k_ref[group, 0:keys, :], q_ref[head, start : start + tile, :], NT)
                s = jnp.where(visible, s, NEGATIVE)
                peak = jnp.max(s, axis=0, keepdims=True)
                p = jnp.exp(s - peak)
                total = jnp.sum(p, axis=0, keepdims=True)
                lse_ref[head, :, start : start + tile] = peak + jnp.log(total)
                o = mul(turned_ref[group, :, 0:keys], p.astype(LOW)) / total
                out_ref[head, start : start + tile, :] = o.T.astype(LOW)

    for head in range(heads):
        mix_ref[:, head * HEAD_WIDTH : (head + 1) * HEAD_WIDTH] = out_ref[head]
    for r, part_ref in enumerate(part_refs):
        at = pl.ds(pl.multiple_of((mine_ref[0] ^ r) * rows, rows), rows)
        part_ref[...] = mul(mix_ref[at, :], wo_ref[...]).astype(part_ref.dtype)


def run_attention(mine, q, k, v, output_weight, column, row, count):
    heads, length, _ = q.shape
    groups = k.shape[0]
    width = output_weight.shape[1]
    rows = length // count
    whole = pl.BlockSpec(memory_space=pltpu.VMEM)
    shape = jax.ShapeDtypeStruct
    results = pl.pallas_call(
        functools.partial(attention_body, heads, groups, rows, min(256, length)),
        out_shape=[
            shape((length, heads * HEAD_WIDTH), LOW),
            shape((heads, 1, length), FULL),
        ]
        + [shape((rows, width), LOW if r % 2 else FULL) for r in range(count)],
        in_specs=[pl.BlockSpec(memory_space=pltpu.SMEM)] + [whole] * 6,
        out_specs=[whole] * (2 + count),
        scratch_shapes=[
            pltpu.VMEM((groups, HEAD_WIDTH, length), LOW),
            pltpu.VMEM((heads, length, HEAD_WIDTH), LOW),
        ],
        compiler_params=pltpu.CompilerParams(vmem_limit_bytes=40 * 1024 * 1024),
        cost_estimate=cost_of(12 * length * width * width, 12 * length * width),
        name="attention",
    )(mine, q, k, v, output_weight, column, row)
    return results[0], results[1], list(results[2:])


def back_body(count, group, size, rows, tile, mine_ref, *rest):
    da_refs = rest[:count]
    (h_in, wo_ref, mix_ref, q_ref, k_ref, v_ref, lse_ref, column_ref, row_ref, cos_ref, sin_ref,
     d_ref, keep_ref, send_ref, da_ref, h_ref, do_ref, turned_ref, dk_ref, dv_ref, dq_ref,
     square_ref, landed) = rest[count:]
    length = row_ref.shape[1]
    scale = HEAD_WIDTH ** (-0.5)
    first = group * size
    loads = []
    for r in range(count):
        at = pl.ds(pl.multiple_of((mine_ref[0] ^ r) * rows, rows), rows)
        load = pltpu.make_async_copy(da_refs[r], da_ref.at[at], landed.at[r])
        load.start()
        loads.append(load)
    late = pltpu.make_async_copy(h_in, h_ref, landed.at[count])
    late.start()
    for load in loads:
        load.wait()
    turned_ref[...] = k_ref[group].astype(FULL).T.astype(LOW)
    dk_ref[...] = jnp.zeros(dk_ref.shape, FULL)
    dv_ref[...] = jnp.zeros(dv_ref.shape, FULL)
    span = slice(first * HEAD_WIDTH, (first + size) * HEAD_WIDTH)

    @pl.loop(0, length // tile)
    def _(i):
        at = pl.ds(pl.multiple_of(i * tile, tile), tile)
        z = mul(da_ref[at, :], wo_ref[span, :], NT).astype(LOW)
        for j in range(size):
            do_ref[j, at, :] = z[:, j * HEAD_WIDTH : (j + 1) * HEAD_WIDTH]

    for start, keys in tiles_of(length, tile):
        visible = column_ref[0:keys, :] <= row_ref[:, start : start + tile]
        cosine, sine = cos_ref[start : start + tile, :], sin_ref[start : start + tile, :]

        @pl.loop(0, size)
        def _(head, start=start, keys=keys, visible=visible, cosine=cosine, sine=sine):
            q = q_ref[first + head, start : start + tile, :]
            do = do_ref[head, start : start + tile, :]
            s = mul(k_ref[group, 0:keys, :], q, NT)
            p = jnp.where(visible, jnp.exp(s - lse_ref[first + head, :, start : start + tile]), 0.0)
            dp = mul(v_ref[group, 0:keys, :], do, NT)
            delta = jnp.sum(p * dp, axis=0, keepdims=True)
            ds = (p * (dp - delta)).astype(LOW)
            dv_ref[0:keys, :] += mul(p.astype(LOW), do)
            dk_ref[0:keys, :] += mul(ds, q)
            dq = mul(turned_ref[:, 0:keys], ds).T * scale
            dq = dq * cosine - swapped(dq) * sine
            dq_ref[head, start : start + tile, :] = dq.astype(LOW)

    for head in range(size):
        d_ref[:, head * HEAD_WIDTH : (head + 1) * HEAD_WIDTH] = dq_ref[head]
    dk = dk_ref[...]
    dk = dk * cos_ref[...] - swapped(dk) * sin_ref[...]
    d_ref[:, size * HEAD_WIDTH : (size + 1) * HEAD_WIDTH] = dk.astype(LOW)
    d_ref[:, (size + 1) * HEAD_WIDTH :] = dv_ref[...].astype(LOW)
    late.wait()
    depth = (size + 2) * HEAD_WIDTH
    square_ref[0:depth, :] = mul(d_ref[...], h_ref[...], TN)
    square_ref[depth:, :] = mul(mix_ref[:, span], da_ref[...], TN)
    half = keep_ref.shape[0]
    for side in range(2):

        @pl.when(mine_ref[1] == side)
        def _(side=side):
            keep_ref[...] = square_ref[side * half : (side + 1) * half, :]
            send_ref[...] = square_ref[(1 - side) * half : (2 - side) * half, :].astype(LOW)


def run_back(group, mine, da, hidden, output_weight, mixture, q, k, v, lse, column, row, cosine, sine):
    heads, length, _ = q.shape
    groups = k.shape[0]
    size = heads // groups
    rows, width = da[0].shape
    count = len(da)
    half = (size + 1) * HEAD_WIDTH
    whole = pl.BlockSpec(memory_space=pltpu.VMEM)
    shape = jax.ShapeDtypeStruct
    return pl.pallas_call(
        functools.partial(back_body, count, group, size, rows, min(256, length)),
        out_shape=(
            shape((length, (size + 2) * HEAD_WIDTH), LOW),
            shape((half, width), FULL),
            shape((half, width), LOW),
        ),
        in_specs=[pl.BlockSpec(memory_space=pltpu.SMEM)]
        + [pl.BlockSpec(memory_space=pltpu.HBM)] * (count + 1)
        + [whole] * 10,
        out_specs=(whole, whole, whole),
        scratch_shapes=[
            pltpu.VMEM((length, width), LOW),
            pltpu.VMEM((length, width), LOW),
            pltpu.VMEM((size, length, HEAD_WIDTH), LOW),
            pltpu.VMEM((HEAD_WIDTH, length), LOW),
            pltpu.VMEM((length, HEAD_WIDTH), FULL),
            pltpu.VMEM((length, HEAD_WIDTH), FULL),
            pltpu.VMEM((size, length, HEAD_WIDTH), LOW),
            pltpu.VMEM((2 * half, width), FULL),
            pltpu.SemaphoreType.DMA((count + 1,)),
        ],
        compiler_params=pltpu.CompilerParams(vmem_limit_bytes=44 * 1024 * 1024),
        cost_estimate=cost_of(8 * length * width * width, 12 * length * width),
        name="back",
    )(mine, *da, hidden, output_weight, mixture, q, k, v, lse, column, row, cosine, sine)


def place_body(rows, mine_ref, *refs):
    for r, ref in enumerate(refs[:-1]):
        at = pl.ds(pl.multiple_of((mine_ref[0] ^ r) * rows, rows), rows)
        refs[-1][at, :] = ref[...].astype(refs[-1].dtype)


def run_place(mine, blocks, kind):
    rows, width = blocks[0].shape
    whole = pl.BlockSpec(memory_space=pltpu.VMEM)
    return pl.pallas_call(
        functools.partial(place_body, rows),
        out_shape=jax.ShapeDtypeStruct((len(blocks) * rows, width), kind),
        in_specs=[pl.BlockSpec(memory_space=pltpu.SMEM)] + [whole] * len(blocks),
        out_specs=whole,
        compiler_params=pltpu.CompilerParams(vmem_limit_bytes=24 * 1024 * 1024),
        cost_estimate=cost_of(1000, 10 * len(blocks) * rows * width),
        name="place",
    )(mine, *blocks)


def gate_columns(num_experts):
    return -(-3 * num_experts // LANES) * LANES


def expert_body(places, block_count, local, hidden, row_tile, column_tile, num_experts, more,
                columns_ref, router_ref, *rest):
    rest = list(rest)
    take = lambda n: [rest.pop(0) for _ in range(n)]
    shard_count = len(places)
    h_refs, g_refs = take(block_count), take(block_count)
    w_refs = [take(3) for _ in range(shard_count)]
    before = take(3 * block_count) if more else None
    y_outs, dh_outs, sum_outs = take(block_count), take(block_count), take(block_count)
    (hid_out,) = take(1)
    (h_ref, g_ref, hid_ref, first_buffer, second_buffer, code_ref, kept_ref, y_ref, dh_ref,
     sum_ref) = take(10)
    arrived, landed, left = rest
    wide = local * hidden
    first = 2 * wide
    rows = h_refs[0].shape[0]
    total, width = h_ref.shape
    span = [pl.ds(i * rows, rows) for i in range(block_count)]

    def begin(source, target, flag):
        copy = pltpu.make_async_copy(source, target, flag)
        copy.start()
        return copy

    loads, olds = [], []
    for i in range(block_count):
        loads += [
            begin(h_refs[i], h_ref.at[span[i]], landed.at[i, 0]),
            begin(g_refs[i].at[:, pl.ds(0, width)], g_ref.at[span[i]], landed.at[i, 1]),
            begin(g_refs[i].at[:, pl.ds(width, LANES)], code_ref.at[span[i]], landed.at[i, 2]),
        ]
        if more:
            for j, target in enumerate((y_ref, dh_ref, sum_ref)):
                olds.append(
                    begin(before[j * block_count + i], target.at[span[i]], landed.at[i, 3 + j])
                )
    copies = []
    for s in range(shard_count):
        targets = (
            first_buffer.at[pl.ds(s * first, wide)],
            first_buffer.at[pl.ds(s * first + wide, wide)],
            second_buffer.at[pl.ds(s * wide, wide)],
        )
        copies.append([begin(w_refs[s][j], targets[j], arrived.at[s, j]) for j in range(3)])
    for load in loads:
        load.wait()
    code = code_ref[...].astype(FULL)
    logits = mul(h_ref[...], router_ref[...])
    picked = code > 0.5
    peak = jnp.max(jnp.where(picked, logits, NEGATIVE), axis=1, keepdims=True)
    exponent = jnp.where(picked, jnp.exp(logits - peak), 0.0)
    gates = exponent / jnp.sum(exponent, axis=1, keepdims=True)
    kept_ref[...] = jnp.where(code > 1.5, gates, 0.0).astype(LOW).astype(FULL)
    if more:
        for old in olds:
            old.wait()
    else:
        sum_ref[...] = jnp.zeros(sum_ref.shape, FULL)
    lane = lax.broadcasted_iota(jnp.int32, (row_tile, LANES), 1)
    owner = lax.broadcasted_iota(jnp.int32, (row_tile, wide), 1) // hidden
    for s in range(shard_count):
        for copy in copies[s]:
            copy.wait()
        place = local * places[s]

        @pl.loop(0, total // row_tile)
        def _(i, s=s, place=place):
            at = pl.ds(pl.multiple_of(i * row_tile, row_tile), row_tile)
            z = mul(h_ref[at, :], first_buffer[s * first : (s + 1) * first, :], NT)
            q = mul(g_ref[at, :], second_buffer[s * wide : (s + 1) * wide, :], NT)
            kept = kept_ref[at, :]
            hits = [lane == columns_ref[place + e] for e in range(local)]
            gate_of = jnp.zeros((row_tile, wide), FULL)
            for e in range(local):
                own = jnp.sum(jnp.where(hits[e], kept, 0.0), axis=1, keepdims=True)
                gate_of = jnp.where(owner == e, own, gate_of)
            gate, up = z[:, :wide], z[:, wide:]
            sigmoid = jax.nn.sigmoid(gate)
            silu = gate * sigmoid
            act = silu * up
            d_act = q * gate_of
            base = s * first
            hid_ref[at, base : base + wide] = (
                d_act * up * sigmoid * (1.0 + gate * (1.0 - sigmoid))
            ).astype(LOW)
            hid_ref[at, base + wide : base + first] = (d_act * silu).astype(LOW)
            base = shard_count * first + s * wide
            hid_ref[at, base : base + wide] = (act * gate_of).astype(LOW)
            product = act * q
            dgb = sum_ref[at, :]
            for e in range(local):
                part = jnp.sum(jnp.where(owner == e, product, 0.0), axis=1, keepdims=True)
                dgb = dgb + jnp.where(hits[e], part, 0.0)
            sum_ref[at, :] = dgb

    leaves = [begin(hid_ref, hid_out, left.at[0, 0])]
    rest_of = sum_ref[...]
    tiles = [jnp.zeros((total, LANES), FULL)] * (gate_columns(num_experts) // LANES)
    for n in range(3):
        piece = rest_of.astype(LOW).astype(FULL)
        rest_of = rest_of - piece
        tile, turn = divmod(n * num_experts, LANES)
        tiles[tile] = tiles[tile] + (pltpu.roll(piece, turn, 1) if turn else piece)
    for n, tile in enumerate(tiles):
        dh_ref[:, width + n * LANES : width + (n + 1) * LANES] = tile.astype(LOW)
    middle = shard_count * first
    for i in range(block_count):
        at = slice(i * rows, (i + 1) * rows)

        @pl.loop(0, width // column_tile)
        def _(j, i=i, at=at):
            cut = pl.ds(pl.multiple_of(j * column_tile, column_tile), column_tile)
            dh = mul(hid_ref[at, 0:middle], first_buffer[:, cut])
            y = mul(hid_ref[at, middle:], second_buffer[:, cut])
            if more:
                y = y + y_ref[at, cut].astype(FULL)
                dh = dh + dh_ref[at, cut].astype(FULL)
            dh_ref[at, cut] = dh.astype(LOW)
            y_ref[at, cut] = y.astype(LOW)

        leaves += [
            begin(y_ref.at[span[i]], y_outs[i], left.at[1 + i, 0]),
            begin(dh_ref.at[span[i]], dh_outs[i], left.at[1 + i, 1]),
            begin(sum_ref.at[span[i]], sum_outs[i], left.at[1 + i, 2]),
        ]
    for leave in leaves:
        leave.wait()


def run_experts(columns, router, h, g, weights, places, local, hidden, num_experts, before=None):
    count, blocks = len(weights), len(h)
    rows, width = h[0].shape
    wide = local * hidden
    depth = 3 * wide
    total = blocks * rows
    wider = width + gate_columns(num_experts)
    whole = pl.BlockSpec(memory_space=pltpu.VMEM)
    away = pl.BlockSpec(memory_space=pltpu.HBM)
    shape = jax.ShapeDtypeStruct
    extra = [] if before is None else before[0] + before[1] + before[2]
    results = pl.pallas_call(
        functools.partial(
            expert_body, tuple(places), blocks, local, hidden, total // -(-total // 512), 512,
            num_experts, bool(extra),
        ),
        out_shape=[shape((rows, width), LOW)] * blocks
        + [shape((rows, wider), LOW)] * blocks
        + [shape((rows, LANES), FULL)] * blocks
        + [shape((total, count * depth), LOW)],
        in_specs=[pl.BlockSpec(memory_space=pltpu.SMEM), whole]
        + [away] * (2 * blocks + 3 * count + len(extra)),
        out_specs=[away] * (3 * blocks + 1),
        scratch_shapes=[
            pltpu.VMEM((total, width), LOW),
            pltpu.VMEM((total, width), LOW),
            pltpu.VMEM((total, count * depth), LOW),
            pltpu.VMEM((count * 2 * wide, width), LOW),
            pltpu.VMEM((count * wide, width), LOW),
            pltpu.VMEM((total, LANES), LOW),
            pltpu.VMEM((total, LANES), FULL),
            pltpu.VMEM((total, width), LOW),
            pltpu.VMEM((total, wider), LOW),
            pltpu.VMEM((total, LANES), FULL),
            pltpu.SemaphoreType.DMA((count, 3)),
            pltpu.SemaphoreType.DMA((blocks, 6)),
            pltpu.SemaphoreType.DMA((blocks + 1, 3)),
        ],
        compiler_params=pltpu.CompilerParams(
            vmem_limit_bytes=min(56, 16 + total * count * 3 // 500 + count * 3) * 1024 * 1024
        ),
        cost_estimate=cost_of(4 * total * width * depth * count, depth * width * count * 2),
        name="experts",
    )(columns, router, *h, *g, *[piece for shard in weights for piece in shard], *extra)
    return (
        list(results[:blocks]),
        list(results[blocks : 2 * blocks]),
        list(results[2 * blocks : 3 * blocks]),
        results[-1],
    )


def weight_body(plan, rows, wide, *rest):
    rest = list(rest)
    take = lambda n: [rest.pop(0) for _ in range(n)]
    blocks = plan[0][1]
    shards_plan = plan[1]
    h_refs, g_refs = take(blocks), take(blocks)
    hid_refs = take(plan[0][0])
    stay = len(shards_plan) // 2
    out_refs = [take(3) for _ in range(stay)]
    (away_ref,) = take(1)
    h_ref, g_ref, first_ref, second_ref, landed, arrived = rest
    loads = []
    for i in range(blocks):
        at = pl.ds(i * rows, rows)
        sources = (h_refs[i], g_refs[i].at[:, pl.ds(0, h_ref.shape[1])])
        for j, (source, target) in enumerate(zip(sources, (h_ref, g_ref))):
            load = pltpu.make_async_copy(source, target.at[at], landed.at[i, j])
            load.start()
            loads.append(load)

    def fetch(s):
        slot = s % 2
        group = []
        for n, (hid, first, second, start, count) in enumerate(shards_plan[s]):
            at = pl.ds(start, count)
            group.append(
                pltpu.make_async_copy(
                    hid_refs[hid].at[:, pl.ds(first, 2 * wide)],
                    first_ref.at[slot, at],
                    arrived.at[slot, n, 0],
                )
            )
            group.append(
                pltpu.make_async_copy(
                    hid_refs[hid].at[:, pl.ds(second, wide)],
                    second_ref.at[slot, at],
                    arrived.at[slot, n, 1],
                )
            )
        for copy in group:
            copy.start()
        return group

    waiting = fetch(0)
    for load in loads:
        load.wait()
    for s in range(len(shards_plan)):
        following = fetch(s + 1) if s + 1 < len(shards_plan) else None
        for copy in waiting:
            copy.wait()
        slot = s % 2
        sums = (
            lambda: mul(first_ref[slot, :, 0:wide], h_ref[...], TN),
            lambda: mul(first_ref[slot, :, wide:], h_ref[...], TN),
            lambda: mul(second_ref[slot], g_ref[...], TN),
        )
        for j in range(3):
            if s < stay:
                out_refs[s][j][...] = sums[j]().astype(LOW)
            else:
                start = (3 * (s - stay) + j) * wide
                away_ref[start : start + wide, :] = sums[j]().astype(LOW)
        waiting = following


def run_weights(h, g, hids, shards_plan, wide):
    blocks = len(h)
    rows, width = h[0].shape
    total = blocks * rows
    stay = len(shards_plan) // 2
    pieces = max(len(p) for p in shards_plan)
    whole = pl.BlockSpec(memory_space=pltpu.VMEM)
    away = pl.BlockSpec(memory_space=pltpu.HBM)
    plan = ((len(hids), blocks), tuple(tuple(p) for p in shards_plan))
    results = pl.pallas_call(
        functools.partial(weight_body, plan, rows, wide),
        out_shape=[jax.ShapeDtypeStruct((wide, width), LOW)] * (3 * stay)
        + [jax.ShapeDtypeStruct((3 * stay * wide, width), LOW)],
        in_specs=[away] * (2 * blocks + len(hids)),
        out_specs=[whole] * (3 * stay + 1),
        scratch_shapes=[
            pltpu.VMEM((total, width), LOW),
            pltpu.VMEM((total, width), LOW),
            pltpu.VMEM((2, total, 2 * wide), LOW),
            pltpu.VMEM((2, total, wide), LOW),
            pltpu.SemaphoreType.DMA((blocks, 2)),
            pltpu.SemaphoreType.DMA((2, pieces, 2)),
        ],
        compiler_params=pltpu.CompilerParams(vmem_limit_bytes=44 * 1024 * 1024),
        cost_estimate=cost_of(12 * total * width * wide * stay, total * 6 * wide * stay * 2),
        name="weight_gradients",
    )(*h, *g, *hids)
    return list(results[:-1]), results[-1]


def swap(values, axis, bit):
    count = lax.axis_size(axis)
    return lax.ppermute(values, axis, [(i, i ^ bit) for i in range(count)])


def pair(values):
    return swap(values, "expert", 1)


def ring(values):
    count = lax.axis_size("expert")
    return lax.ppermute(values, "expert", [(i, (i + 2) % count) for i in range(count)])


def pick(values, index):
    return lax.dynamic_index_in_dim(values, index, 0, keepdims=False)


def ring_gather(block):
    blocks = [block]
    for _ in range(lax.axis_size("expert") // 2 - 1):
        blocks.append(ring(blocks[-1]))
    return blocks


def ring_sum(blocks, sent=LOW):
    running = blocks[1 % len(blocks)].astype(FULL)
    for k in range(2, len(blocks) + 1):
        running = ring(running.astype(sent)).astype(FULL) + blocks[k % len(blocks)].astype(FULL)
    return running


def bits_of(count):
    return [1 << i for i in range(count.bit_length() - 1)]


def parts_sum(parts):
    parts = list(parts)
    for bit in bits_of(len(parts)):
        for r in reversed(range(0, len(parts), 2 * bit)):
            other = swap(parts[r + bit].astype(LOW), "tensor", bit)
            parts[r] = parts[r].astype(FULL) + other.astype(FULL)
    return parts[0]


def tensor_blocks(own):
    count = lax.axis_size("tensor")
    blocks = [own] * count
    for bit in reversed(bits_of(count)):
        for r in range(0, count, 2 * bit):
            blocks[r + bit] = swap(blocks[r], "tensor", bit)
    return blocks


def sends_z(values):
    size = lax.axis_size("expert") // 2
    place = lax.axis_index("expert") // 2
    n, m = values.shape
    cuts = values.reshape(size, n // size, m)
    return [pick(cuts, place)] + [
        shift(pick(cuts, (place + k) % size).astype(LOW), k) for k in range(1, size)
    ]


def total_of(parts):
    return sum(part.astype(FULL) for part in parts)


def laid_z(blocks):
    size = len(blocks)
    place = lax.axis_index("expert") // 2
    whole = jnp.zeros((size,) + blocks[0].shape, blocks[0].dtype)
    for k, block in enumerate(blocks):
        whole = lax.dynamic_update_index_in_dim(whole, block, (place - k) % size, 0)
    return whole.reshape((-1,) + blocks[0].shape[1:])


def joined(half, other):
    low = lax.axis_index("expert") % 2 == 0
    return jnp.concatenate([jnp.where(low, half, other), jnp.where(low, other, half)])


def sum_everywhere(values):
    for axis in ("tensor", "expert"):
        for bit in bits_of(lax.axis_size(axis)):
            values = values + swap(values, axis, bit)
    return values


def shift(block, steps):
    count = lax.axis_size("expert")
    return lax.ppermute(block, "expert", [(i, (i + 2 * steps) % count) for i in range(count)])


def spread(block):
    return [block] + [shift(block, k) for k in range(1, lax.axis_size("expert") // 2)]


def with_cores(chips):
    shards_of = []
    for chip in chips:
        shards_of += [chip, [swap(piece, "tensor", 1) for piece in chip]]
    return shards_of


def gather_weights(own):
    near, far = [own], [[pair(piece) for piece in own]]
    for bit in bits_of(lax.axis_size("tensor"))[1:]:
        for i in range(len(near)):
            near.append([swap(piece, "tensor", bit) for piece in near[i]])
            far.append(
                [
                    pair(near[-1][0]),
                    swap(far[i][1], "tensor", bit),
                    pair(near[-1][2]),
                ]
            )
    return near, far


def scatter_weights(parts):
    full = lambda v: v.astype(FULL)
    sums = [[full(piece) for piece in chip] for chip in parts]
    near, far = sums[: len(sums) // 2], sums[len(sums) // 2 :]
    for bit in reversed(bits_of(lax.axis_size("tensor"))[1:]):
        count = len(near) // 2
        across = lambda v: full(swap(v.astype(LOW), "tensor", bit))
        beside = lambda v: full(pair(v.astype(LOW)))
        for i in range(count):
            last_near, last_far = near[count + i], far[count + i]
            last_near = [
                last_near[0] + beside(last_far[0]),
                last_near[1],
                last_near[2] + beside(last_far[2]),
            ]
            far[i] = [far[i][0], far[i][1] + across(last_far[1]), far[i][2]]
            near[i] = [one + across(two) for one, two in zip(near[i], last_near)]
        near, far = near[:count], far[:count]
    return [own + full(pair(other.astype(LOW))) for own, other in zip(near[0], far[0])]


def shards(
    activations,
    cotangent,
    block_ids,
    expert_ids,
    route_ranks,
    attention_gain,
    query_weight,
    key_matrix,
    value_matrix,
    output_weight,
    mixture_gain,
    router_weight,
    expert_gate,
    expert_up,
    expert_down,
):
    sequence_length, width = activations.shape
    heads = query_weight.shape[1] // HEAD_WIDTH
    groups = key_matrix.shape[1] // HEAD_WIDTH
    tensor_count = lax.axis_size("tensor")
    expert_count = lax.axis_size("expert")
    tensor_index = lax.axis_index("tensor")
    expert_index = lax.axis_index("expert")
    num_experts = router_weight.shape[1]
    local, _, hidden = expert_gate.shape
    picks = expert_ids.shape[1]
    capacity = sequence_length * picks // num_experts
    rows = sequence_length // tensor_count
    ring_size = expert_count // 2
    row_offset = tensor_index * rows
    own_rows = lambda v: lax.dynamic_slice_in_dim(v, row_offset, rows, 0)
    wide = local * hidden

    down = expert_down.reshape(wide, width)
    gate = expert_gate.transpose(0, 2, 1).reshape(wide, width)
    up = expert_up.transpose(0, 2, 1).reshape(wide, width)
    cotangent_own = own_rows(cotangent)
    ids_own, ranks_own = own_rows(expert_ids), own_rows(route_ranks)
    expert_range = jnp.arange(LANES, dtype=jnp.int32)
    pair_code = jnp.where(ranks_own < capacity, 2.0, 1.0)
    code = jnp.zeros((rows, LANES), FULL)
    for j in range(picks):
        code = code + jnp.where(
            ids_own[:, j, None] == expert_range[None, :], pair_code[:, j, None], 0.0
        )
    cosine, sine = rope_tables(sequence_length)
    gain_first = attention_gain.astype(FULL)[None]
    mine = jnp.stack([tensor_index, expert_index % 2]).astype(jnp.int32)
    row = block_ids
    column = block_ids.reshape(sequence_length, 1)
    fine = tensor_count == 4 and ring_size == 4
    x_in = activations
    across = lambda v: swap(v, "tensor", 2)
    sent = jnp.concatenate([cotangent_own, code.astype(LOW)], axis=1)
    x_own = own_rows(activations)
    core = lambda v: swap(v, "tensor", 1)
    if fine:
        x_in, gate, up, sent, x_own, column = tie(activations, gate, up, sent, x_own, column)
        moved = [pair(down), across(down), ring(sent), core(down), core(gate)]
    hidden_first, q, k, v = run_front(
        x_in, gain_first, (query_weight, key_matrix, value_matrix), cosine, sine, heads, groups
    )
    if fine:
        moved, hidden_first, q, k, v, gate, up = tie(moved, hidden_first, q, k, v, gate, up)
        down_x, down_y, g_1, down_c, gate_c = moved
        moved = [pair(gate), across(gate), ring(g_1), core(down_x), core(up)]
    mixture, lse, parts = run_attention(mine, q, k, v, output_weight, column, row, tensor_count)
    if fine:
        moved, mixture, lse, parts, up = tie(moved, mixture, lse, parts, up)
        gate_x, gate_y, g_2, down_xc, up_c = moved
        parts = tie(parts[0], parts[2], core(parts[3]), core(parts[1]))
        to_send = (parts[1] + parts[2].astype(FULL)).astype(LOW)
        attention_out = parts[0] + parts[3].astype(FULL)
        to_send, attention_out, up, g_2, gate_x, down_y = tie(
            to_send, attention_out, up, g_2, gate_x, down_y
        )
        moved = [across(to_send), pair(up), ring(g_2), core(gate_x), core(down_y)]
        moved, gate_y = tie(moved, gate_y)
        attention_out = attention_out + moved[0].astype(FULL)
        up_x, g_3, gate_xc, down_yc = moved[1:]
        g = [sent, g_1, g_2, g_3]
    else:
        attention_out = parts_sum(parts)

    gain_second = mixture_gain.astype(FULL)
    residual_mid = x_own.astype(FULL) + attention_out
    inverse_second = normalized(residual_mid)
    normed_second = residual_mid * inverse_second
    hidden_second = (normed_second * gain_second).astype(LOW)

    router_wide = jnp.pad(router_weight, ((0, 0), (0, LANES - num_experts)))
    columns = jnp.concatenate(
        [
            expert_index * local + jnp.arange(local, dtype=jnp.int32),
            (expert_index ^ 1) * local + jnp.arange(local, dtype=jnp.int32),
        ]
    ).astype(jnp.int32)
    experts = lambda h, g, weights, places, before=None: run_experts(
        columns, router_wide, h, g, weights, places, local, hidden, num_experts, before
    )
    first = 2 * wide
    low = lambda v: v.astype(LOW)
    full = lambda v: v.astype(FULL)

    def token_gradients(summed_rows):
        d_hidden_moe = summed_rows[:, :width]
        d_gates = sum(
            summed_rows[:, width + n * num_experts : width + (n + 1) * num_experts]
            for n in range(3)
        )
        logits = mul(hidden_second, router_weight)
        picked = code[:, :num_experts] > 0.5
        held = code[:, :num_experts] > 1.5
        gates = jax.nn.softmax(jnp.where(picked, logits, NEGATIVE), axis=-1)
        d_gates = jnp.where(held, d_gates, 0.0)
        d_logits = low(gates * (d_gates - jnp.sum(gates * d_gates, axis=-1, keepdims=True)))
        d_hidden_second = d_hidden_moe + mul(d_logits, router_weight, NT)
        grad_router = mul(hidden_second, d_logits, TN)
        grad_gain_second = jnp.sum(d_hidden_second * normed_second, axis=0)
        scaled = d_hidden_second * gain_second
        d_mid = full(cotangent_own) + inverse_second * (
            scaled - normed_second * jnp.mean(scaled * normed_second, axis=-1, keepdims=True)
        )
        return d_mid, jnp.concatenate([grad_gain_second[None], grad_router.T])

    back = lambda group, da: run_back(
        group, mine, da, hidden_first, output_weight, mixture, q, k, v, lse, column, row, cosine, sine
    )
    size = heads // groups
    cut = size * HEAD_WIDTH
    group_weights = [
        jnp.concatenate(
            [
                query_weight[:, i * cut : (i + 1) * cut],
                key_matrix[:, i * HEAD_WIDTH : (i + 1) * HEAD_WIDTH],
                value_matrix[:, i * HEAD_WIDTH : (i + 1) * HEAD_WIDTH],
            ],
            axis=1,
        )
        for i in range(groups)
    ]

    def first_gradients(d_projected):
        d_first = sum(mul(d, w, NT) for d, w in zip(d_projected, group_weights))
        inverse = normalized(full(activations))
        grad_gain = jnp.sum(d_first * (full(activations) * inverse), axis=0)
        parts = [
            lax.dynamic_slice_in_dim(d_first, (tensor_index ^ r) * rows, rows, 0)
            for r in range(tensor_count)
        ]
        return [low(p) if r % 2 else p for r, p in enumerate(parts)], grad_gain

    def input_rows(d_first, d_mid):
        values = full(x_own)
        inverse = normalized(values)
        normed = values * inverse
        scaled = d_first * gain_first
        return low(
            d_mid
            + inverse * (scaled - normed * jnp.mean(scaled * normed, axis=-1, keepdims=True))
        )

    if fine:
        hidden_second, up_xc, gate_yc = tie(hidden_second, core(up_x), core(gate_y))
        side = [
            [gate, up, down], [gate_c, up_c, down_c],
            [gate_x, up_x, down_x], [gate_xc, up_xc, down_xc],
        ]
        side_places = [0, 0, 1, 1]
        h = [hidden_second]
        moved = [ring(h[0]), across(up), pair(down_y)]
        start = experts(h[:1], g[:1], side, side_places)
        moved, start = tie(moved, start)
        y_0, dh_0, dgb_0, hid_0 = start
        h.append(moved[0])
        up_y, down_far = moved[1:]

        moved = [ring(h[1]), across(gate_x), pair(up_y)]
        up_yc, down_farc = core(up_y), core(down_far)
        y_1, dh_1, dgb_1, hid_1 = experts(h[1:2], g[1:2], side, side_places)
        beside = [[gate_y, up_y, down_y], [gate_yc, up_yc, down_yc]]
        second = experts(
            h[:2], g[:2], beside, [0, 0], (y_0 + y_1, dh_0 + dh_1, dgb_0 + dgb_1)
        )
        moved, second, hid_1, down_farc = tie(moved, second, hid_1, down_farc)
        y_1, dh_1, dgb_1, hid_y = second
        h.append(moved[0])
        gate_far, up_far = moved[1:]

        moved = [ring(h[2])]
        gate_farc, up_farc = core(gate_far), core(up_far)
        y_2, dh_2, dgb_2, hid_2 = experts(h[2:3], g[2:3], side + beside, side_places + [0, 0])
        distant = [[gate_far, up_far, down_far], [gate_farc, up_farc, down_farc]]
        third = experts(
            h[:3], g[:3], distant, [1, 1], (y_1 + y_2, dh_1 + dh_2, dgb_1 + dgb_2)
        )
        moved, third, hid_2, distant = tie(moved, third, hid_2, distant)
        y_parts, dh_parts, dgb_parts, hid_far = third
        h.append(moved[0])

        moved = ring(dh_parts[1])
        last = experts(h[3:], g[3:], side + beside + distant, side_places + [0, 0, 1, 1])
        moved, last = tie(moved, last)
        y, dh, _, hid_last = last
        y_parts, dh_parts = y_parts + y, dh_parts + dh

        (running,) = run_adds([(moved, dh_parts[2])])
        hids = [hid_0, hid_1, hid_y, hid_2, hid_far, hid_last]
        plan = []
        for s in range(8):
            place_of = lambda n, i: (i * first, n * first + i * wide)
            if s < 4:
                head = [(b, *place_of(4, s), b * rows, rows) for b in (0, 1)]
                head.append((3, *place_of(6, s), 2 * rows, rows))
            elif s < 6:
                head = [(2, *place_of(2, s - 4), 0, 2 * rows)]
                head.append((3, *place_of(6, s), 2 * rows, rows))
            else:
                head = [(4, *place_of(2, s - 6), 0, 3 * rows)]
            plan.append(head + [(5, *place_of(8, s), 3 * rows, rows)])
        weights_of = lambda which: run_weights(h, g, hids, [plan[s] for s in which], wide)
        running, hids = tie(running, hids)
        moved = ring(running)
        ready = weights_of([6, 4, 7, 5])
        moved, ready = tie(moved, ready)

        (running,) = run_adds([(moved, dh_parts[3])])
        running, h = tie(running, h)
        moved, others = ring(running), core(ready[1])
        later = weights_of([2, 0, 3, 1])
        moved, later, others = tie(moved, later, others)

        take_all = lambda kept, other, start: run_adds(
            [(piece, other, (start + i) * wide) for i, piece in enumerate(kept)]
        )
        far_sum = take_all(ready[0][:3], others, 0)
        d_mid, small = token_gradients(full(moved) + full(dh_parts[0]))
        d_a = low(d_mid)
        d_a, d_mid, far_sum, y_run, others, later = tie(
            d_a, d_mid, far_sum, y_parts[1], others, later
        )

        moved = [across(d_a), pair(far_sum[0]), ring(y_run), core(d_a), core(later[1])]
        y_sum = take_all(ready[0][3:], others, 3)
        moved, y_sum = tie(moved, y_sum)
        da = [d_a, moved[3], moved[0]]
        later_others = moved[4]
        da_3, y_sum[0], y_run = tie(
            core(da[2]), *run_adds([(y_sum[0], moved[1]), (moved[2], y_parts[2])])
        )
        da.append(da_3)

        moved = [across(far_sum[1]), pair(far_sum[2]), ring(y_run)]
        d_one, keep_one, send_one = back(0, da)
        kept, d_one = tie(later[0], d_one)
        sums = take_all(kept, later_others, 0)
        moved, d_one, keep_one, send_one, sums, da = tie(
            moved, d_one, keep_one, send_one, sums, da
        )
        x_sum, own_sum = sums[:3], sums[3:]
        y_sum[2], x_sum[1], y_run = run_adds(
            [(y_sum[2], moved[1]), (x_sum[1], moved[0]), (moved[2], y_parts[3])]
        )
        y_sum, x_sum, y_run = tie(y_sum, x_sum, y_run)

        moved = [across(y_sum[0]), pair(send_one), ring(y_run)]
        d_two, keep_two, send_two = back(1, da)
        moved, d_two, keep_two, send_two = tie(moved, d_two, keep_two, send_two)
        arrived_y, arrived_x = [moved[0]], []
        summed = moved[2]
        d_parts, grad_gain_first = first_gradients([d_one, d_two])
        half_one = keep_one + full(moved[1])
        extra = jnp.pad(
            jnp.concatenate([small, grad_gain_first[None]]),
            ((0, EXTRA - 2 - num_experts), (0, 0)),
        )
        send_two = jnp.concatenate([send_two, low(extra)])
        d_parts, half_one, extra, send_two = tie(d_parts, half_one, extra, send_two)
        d_others = tie(core(d_parts[3]), core(d_parts[1]))
        to_send = low(d_parts[2] + full(d_others[0]))
        d_first = d_parts[0] + full(d_others[1])

        place = expert_index // 2
        bits = [place % 2, place // 2]
        along = lambda v, bit: swap(v, "expert", 2 << bit)

        def halved(v, bit, more=None):
            parts = v.reshape(2, v.shape[0] // 2, v.shape[1])
            goes = low(pick(parts, 1 - bits[bit]))
            if more is not None:
                goes = jnp.concatenate([goes, low(more)])
            return pick(parts, bits[bit]), goes

        def doubled(v, other, bit):
            front = bits[bit] == 0
            return jnp.concatenate([jnp.where(front, v, other), jnp.where(front, other, v)])

        def apart(keep, came, more):
            n = keep.shape[0]
            return keep + full(came[:n]), more + full(came[n:])

        stay_one, go_one = halved(half_one, 0)
        to_send, d_first, stay_one, go_one = tie(to_send, d_first, stay_one, go_one)

        moved = tie(across(to_send), pair(send_two), along(go_one, 0))
        d_in = input_rows(d_first + full(moved[0]), d_mid)
        half_two, extra = apart(keep_two, moved[1], extra)
        stay_one, go_one = halved(stay_one + full(moved[2]), 1)
        stay_two, go_two = halved(half_two, 0, extra)
        d_in, stay_one, go_one, stay_two, go_two, extra = tie(
            d_in, stay_one, go_one, stay_two, go_two, extra
        )
        moved = [
            across(d_in), core(d_in), along(go_one, 1), along(go_two, 0), pair(x_sum[0]),
        ]
        out_own = low(residual_mid + full(summed) + full(y_parts[0]))
        moved, out_own = tie(moved, out_own)
        input_blocks = [d_in, moved[1], moved[0]]
        arrived_x.append(moved[4])
        one = low(stay_one + full(moved[2]))
        stay_two, extra = apart(stay_two, moved[3], extra)
        stay_two, go_two = halved(stay_two, 1, extra)
        one, stay_two, go_two, extra, input_blocks, arrived_x = tie(
            one, stay_two, go_two, extra, input_blocks, arrived_x
        )
        moved = [
            along(one, 1), along(go_two, 1), pair(x_sum[1]), across(y_sum[2]),
            core(input_blocks[2]),
        ]
        moved = tie(*moved)
        arrived_x.append(moved[2])
        arrived_y.append(moved[3])
        input_blocks.append(moved[4])
        one = doubled(one, moved[0], 1)
        two, extra = apart(stay_two, moved[1], extra)
        two = low(two)
        one, two, extra, input_blocks, arrived_x, arrived_y = tie(
            one, two, extra, input_blocks, arrived_x, arrived_y
        )
        input_gradient = run_place(mine, input_blocks, FULL)
        moved = tie(
            along(one, 0), along(two, 1), pair(x_sum[2]), across(y_sum[1]), core(extra),
            input_gradient,
        )
        input_gradient = moved[5]
        arrived_x.append(moved[2])
        arrived_y.append(moved[3])
        one = doubled(one, moved[0], 0)
        two = doubled(two, moved[1], 1)
        extra = extra + moved[4]
        out_more = jnp.concatenate([out_own, low(extra)])
        one, two, extra, out_more, out_own, arrived_x, arrived_y = tie(
            one, two, extra, out_more, out_own, arrived_x, arrived_y
        )
        grads = [
            total_of([own_sum[0], arrived_y[0], arrived_x[0]]),
            total_of([own_sum[1], arrived_y[2], arrived_x[1]]),
            total_of([own_sum[2], arrived_y[1], arrived_x[2]]),
        ]
        unturned = lambda v: v.reshape(local, hidden, width).transpose(0, 2, 1)
        grad_gate, grad_up, grad_down = unturned(grads[0]), unturned(grads[1]), grads[2]
        moved = tie(pair(one), along(two, 0), across(out_more), core(out_own), grad_gate, grad_up)
        grad_gate, grad_up = moved[4:]
        two = doubled(two, moved[1], 0)
        out_2 = moved[2][:rows]
        sums = extra + full(moved[2][rows:])
        sums = sums[: 2 + num_experts]
        two, out_2 = tie(two, out_2)
        whole_one = joined(one, moved[0])
        output_blocks = [out_own, moved[3], out_2, core(out_2)]
        wholes = [whole_one, joined(two, pair(two))]
    else:
        g = spread(sent)
        h = ring_gather(hidden_second)
        near, far = gather_weights([gate, up, down])
        places = [0] * (2 * len(near)) + [1] * (2 * len(far))
        weights = with_cores(near + far)
        step = max(1, min(ring_size, 1024 // rows))
        y_parts, dh_parts, dgb_parts, hids, plan = [], [], [], [], [[] for _ in weights]
        for i in range(0, ring_size, step):
            at = slice(i, i + step)
            y, dh, dgb, hid = experts(h[at], g[at], weights, places)
            y_parts, dh_parts, dgb_parts = y_parts + y, dh_parts + dh, dgb_parts + dgb
            for s in range(len(weights)):
                base = len(weights) * first + s * wide
                plan[s].append((len(hids), s * first, base, i * rows, step * rows))
            hids.append(hid)
        grad_parts = []
        for i in range(0, len(weights), 4):
            kept, other = run_weights(
                h, g, hids, [plan[i], plan[i + 2], plan[i + 1], plan[i + 3]], wide
            )
            other = core(other)
            sums = run_adds([(piece, other, j * wide) for j, piece in enumerate(kept)])
            grad_parts += [sums[:3], sums[3:]]
        grad_gate, grad_up, grad_down = scatter_weights(grad_parts)
        unturned = lambda v: v.reshape(local, hidden, width).transpose(0, 2, 1)
        grad_gate, grad_up = unturned(grad_gate), unturned(grad_up)
        d_mid, small = token_gradients(ring_sum(dh_parts))
        da = tensor_blocks(low(d_mid))
        backs = [back(i, da) for i in range(groups)]
        d_parts, grad_gain_first = first_gradients([d for d, _, _ in backs])
        d_first = parts_sum(d_parts)
        input_blocks = tensor_blocks(input_rows(d_first, d_mid))
        input_gradient = run_place(mine, input_blocks, FULL)
        output_blocks = tensor_blocks(low(residual_mid + ring_sum(y_parts)))
        wholes = []
        for _, keep, send in backs:
            half = keep + full(pair(send))
            half = laid_z(spread(low(total_of(sends_z(half)))))
            wholes.append(joined(half, pair(half)))
        sums = sum_everywhere(jnp.concatenate([small, grad_gain_first[None]]))

    span = cut + 2 * HEAD_WIDTH
    turned = lambda a, b: full(jnp.concatenate([w[a:b] for w in wholes])).T
    return (
        run_place(mine, output_blocks, LOW),
        input_gradient,
        sums[-1],
        turned(0, cut),
        turned(cut, cut + HEAD_WIDTH),
        turned(cut + HEAD_WIDTH, span),
        full(jnp.concatenate([w[span:] for w in wholes])),
        sums[0],
        sums[1:-1].T,
        grad_gate,
        grad_up,
        grad_down.reshape(local, hidden, width),
    )


def solution(mesh):
    in_specs = (
        P("expert", None),
        P("expert", None),
        P("expert", None),
        P("expert", None),
        P("expert", None),
        P(),
        P(None, "tensor"),
        P(None, "tensor"),
        P(None, "tensor"),
        P("tensor", None),
        P(),
        P(),
        P("expert", None, "tensor"),
        P("expert", None, "tensor"),
        P("expert", "tensor", None),
    )
    out_specs = (
        P("expert", None),
        P("expert", None),
        P(),
        P(None, "tensor"),
        P(None, "tensor"),
        P(None, "tensor"),
        P("tensor", None),
        P(),
        P(),
        P("expert", None, "tensor"),
        P("expert", None, "tensor"),
        P("expert", "tensor", None),
    )
    return jax.shard_map(shards, mesh=mesh, in_specs=in_specs, out_specs=out_specs, check_vma=False)
```

time: 888 us -> 563 us (0.63)
  waiting for transfers between devices: 404 us -> 133 us
  Pallas kernels: 65.3 us -> 203 us
  matrix products: 108 us -> 5.68 us
  other arithmetic: 97.4 us -> 45.3 us
  local copies, waits for them, and re-layouts: 140 us -> 104 us
  starting transfers between devices: 45.3 us -> 58.9 us
  between operations: 16 us -> 2.66 us
    ppermute x27 -> x12, waiting for transfers between devices: 172 us -> 11.9 us  [ring(): lax.ppermute(values, 'expert', [(i, (i + 2) % count) for i in range(count)])]
    pallas_call x2 -> x21, Pallas kernels: 65.3 us -> 203 us  [the longest x6 87.7 us: run_experts(): pl.pallas_call(functools.partial(expert_body, tuple(places), blocks, loca...]
    psum x1 -> x0, waiting for transfers between devices: 97.8 us -> none  [shards(): lax.psum(jnp.concatenate([grad_gain_first[None], grad_gain_second[None],...]
    dot_general x14 -> x0, matrix products: 56.6 us -> none  [the longest x2 14.2 us: one_block(): jnp.einsum('qkgd,skd->kgqs', part_grads, values_low, preferred_element_ty...]
    unnamed x170 -> x330, local copies, waits for them, and re-layouts: 28.2 us -> 76.2 us
    dot_general x11 -> x5, matrix products: 51.4 us -> 5.68 us  [mul(): return lax.dot_general(left, right, dims, preferred_element_type=FULL)]
    dynamic_update_slice x15 -> x0, local copies, waits for them, and re-layouts: 36.4 us -> none  [the longest x4 31.4 us: attention_backward(): lax.scan(one_block, (zeros_kv, zeros_kv), (jnp.arange(block_count, dtype=...]
    all_to_all x1 -> x0, waiting for transfers between devices: 24.9 us -> none  [shards(): lax.all_to_all(dgb_sends.reshape(expert_count, rows, num_experts), 'exper...]
  transfers between devices with their start and end apart: 59 -> 72, of which waited for: 26 -> 24; matrix products, arithmetic and copies ran while one was open for 26% -> 11% of each run, Pallas kernels for 0% -> 35%
where the time goes in v2:
time: 563 us; the launch traced here: 553 us
  Pallas kernels  203 us (36%)
  waiting for transfers between devices  133 us (24%)
  local copies, waits for them, and re-layouts  104 us (18%)
  starting transfers between devices  58.9 us (10%)
  other arithmetic  45.3 us (8%)
  matrix products  5.68 us (1%)
    ppermute x60, waiting for transfers between devices, swap(): return lax.ppermute(values, axis, [(i, i ^ bit) for i in range(count)])  121 us
    pallas_call x6, Pallas kernels, run_experts(): pl.pallas_call(functools.partial(expert_body, tuple(places), blocks, loca...  87.7 us
    unnamed x330, local copies, waits for them, and re-layouts  76.2 us
    ppermute x60, starting transfers between devices, swap(): return lax.ppermute(values, axis, [(i, i ^ bit) for i in range(count)])  45.3 us
    pallas_call x2, Pallas kernels, run_back(): pl.pallas_call(functools.partial(back_body, count, group, size, rows, min...  40.7 us
    pallas_call x2, Pallas kernels, run_weights(): pl.pallas_call(functools.partial(weight_body, plan, rows, wide), out_shap...  30.4 us
    pallas_call x1, Pallas kernels, run_attention(): pl.pallas_call(functools.partial(attention_body, heads, groups, rows, min...  22.3 us
    ppermute x12, starting transfers between devices, ring(): lax.ppermute(values, 'expert', [(i, (i + 2) % count) for i in range(count)])  13.6 us
  transfers between devices with their start and end apart: 72, of which 24 were waited for; matrix products, arithmetic and copies ran while one was open for 11% of the time, Pallas kernels for 35%

profile of v2, /device:TPU:0, one launch (start us, length us, event | category | flops | bytes accessed | tf_op | source)
XLA Modules:
  0.0 552.7 jit_solution(3757376781851329446)
XLA Ops:
  11.0 3.1 collective-permute-start.2
  17.2 6.0 %front.1 = (bf16[1024,1536]{1,0:T(8,128)(2,1)S(1)}, bf16[6,1024,64]{2,1,0:T(8,128)(2,1)S(1)}, bf16[2,1024,64]{2,1,0:T(8,128)(2,1)S(1)}, bf16[2,1024,64]{2,1,0:T(8,128)(2,1)S(1)}) custom-call(bf16[1024,1536]{1,0:T(8,128)(2,1)S(1)} %copy-done.1, f32[1,1536]{1,0:T(1,128)S(1)} %broadcast_in_dim.131.gain_ref, bf16[1536,384]{1,0:T(8,128)(2,1)S(1)} %copy-done.44, ...), custom_call_target="tpu_custom_call" | custom-call | flops 301989888 | bytes 294912 | tf_op jit(solution)/shard_map/front/pallas_call | solution.py:91
  28.5 5.6 %collective-permute-done.rest_10_ = bf16[256,1536]{1,0:T(8,128)(2,1)} collective-permute-done((bf16[256,1536]{1,0:T(8,128)(2,1)S(1)}, bf16[256,1536]{1,0:T(8,128)(2,1)}, u32[]{:S(2)}, u32[]{:S(2)}) %collective-permute-start) | collective-permute-done | bytes 786464 | tf_op jit(solution)/shard_map/ppermute | solution.py:604
  45.6 22.3 %attention.1 = (bf16[1024,384]{1,0:T(8,128)(2,1)S(1)}, f32[6,1,1024]{2,1,0:T(1,128)S(1)}, f32[256,1536]{1,0:T(8,128)S(1)}, bf16[256,1536]{1,0:T(8,128)(2,1)S(1)}...) custom-call(s32[2]{0:T(128)S(1)} %pad_add_fusion.mine_ref, bf16[6,1024,64]{2,1,0:T(8,128)(2,1)S(1)} %copy-done.7, ...), custom_call_target="tpu_custom_call" | custom-call | flops 452984832 | bytes 294912 | tf_op jit(solution)/shard_map/attention/pallas_call | solution.py:177
  76.5 16.8 %collective-permute-done.12 = bf16[256,1536]{1,0:T(8,128)(2,1)S(1)} collective-permute-done((bf16[256,1536]{1,0:T(8,128)(2,1)S(1)}, bf16[256,1536]{1,0:T(8,128)(2,1)S(1)}, u32[]{:S(2)}, u32[]{:S(2)}) %collective-permute-start.12) | collective-permute-done | bytes 786464 | tf_op jit(solution)/shard_map/ppermute | solution.py:604
  112.2 10.8 %experts.6 = (bf16[256,1536]{1,0:T(8,128)(2,1)S(1)}, bf16[256,1664]{1,0:T(8,128)(2,1)S(1)}, f32[256,128]{1,0:T(8,128)S(1)}, bf16[256,3072]{1,0:T(8,128)(2,1)S(1)}) custom-call(s32[4]{0:T(128)S(1)} %pad_add_fusion.1.columns_ref, bf16[1536,128]{1,0:T(8,128)(2,1)S(1)} %pad.8.router_ref, bf16[256,1536]{1,0:T(8,128)(2,1)S(1)} %multiply_convert_fusion.rest_0_, ...), custom_call_target="tpu_custom_call" | custom-call | flops 75497472 | bytes 147456 | tf_op jit(solution)/shard_map/experts/pallas_call | solution.py:466
  128.0 11.0 %experts.7 = (bf16[256,1536]{1,0:T(8,128)(2,1)S(1)}, bf16[256,1664]{1,0:T(8,128)(2,1)S(1)}, f32[256,128]{1,0:T(8,128)S(1)}, bf16[256,3072]{1,0:T(8,128)(2,1)S(1)}) custom-call(s32[4]{0:T(128)S(1)} %pad_add_fusion.1.columns_ref, bf16[1536,128]{1,0:T(8,128)(2,1)S(1)} %pad.8.router_ref, bf16[256,1536]{1,0:T(8,128)(2,1)S(1)} %collective-permute-done.19.rest_0_.rest_1_, ...), custom_call_target="tpu_custom_call" | custom-call | flops 75497472 | bytes 147456 | tf_op jit(solution)/shard_map/experts/pallas_call | solution.py:466
  140.2 12.0 %experts.8 = (bf16[256,1536]{1,0:T(8,128)(2,1)S(1)}, bf16[256,1536]{1,0:T(8,128)(2,1)S(1)}, bf16[256,1664]{1,0:T(8,128)(2,1)S(1)}, bf16[256,1664]{1,0:T(8,128)(2...) custom-call(s32[4]{0:T(128)S(1)} %pad_add_fusion.1.columns_ref, ...), custom_call_target="tpu_custom_call" | custom-call | flops 75497472 | bytes 73728 | tf_op jit(solution)/shard_map/experts/pallas_call | solution.py:466
  157.6 14.6 %experts.9 = (bf16[256,1536]{1,0:T(8,128)(2,1)S(1)}, bf16[256,1664]{1,0:T(8,128)(2,1)}, f32[256,128]{1,0:T(8,128)S(1)}, bf16[256,4608]{1,0:T(8,128)(2,1)}) custom-call(s32[4]{0:T(128)S(1)} %pad_add_fusion.1.columns_ref, bf16[1536,128]{1,0:T(8,128)(2,1)S(1)} %pad.8.router_ref, bf16[256,1536]{1,0:T(8,128)(2,1)S(1)} %collective-permute-done.22.rest_0_.rest_2_, ...), custom_call_target="tpu_custom_call" | custom-call | flops 113246208 | bytes 221184 | tf_op jit(solution)/shard_map/experts/pallas_call | solution.py:466
  176.2 15.6 %experts.10 = (bf16[256,1536]{1,0:T(8,128)(2,1)S(1)}, bf16[256,1536]{1,0:T(8,128)(2,1)S(1)}, bf16[256,1536]{1,0:T(8,128)(2,1)S(1)}, bf16[256,1664]{1,0:T(8,128)(...) custom-call(s32[4]{0:T(128)S(1)} %pad_add_fusion.1.columns_ref, ...), custom_call_target="tpu_custom_call" | custom-call | flops 113246208 | bytes 73728 | tf_op jit(solution)/shard_map/experts/pallas_call | solution.py:466
  198.0 23.8 %experts.11 = (bf16[256,1536]{1,0:T(8,128)(2,1)S(1)}, bf16[256,1664]{1,0:T(8,128)(2,1)}, f32[256,128]{1,0:T(8,128)}, bf16[256,6144]{1,0:T(8,128)(2,1)}) custom-call(s32[4]{0:T(128)S(1)} %pad_add_fusion.1.columns_ref, bf16[1536,128]{1,0:T(8,128)(2,1)S(1)} %pad.8.router_ref, bf16[256,1536]{1,0:T(8,128)(2,1)} %collective-permute-done.27.rest_0_.rest_3_, ...), custom_call_target="tpu_custom_call" | custom-call | flops 150994944 | bytes 294912 | tf_op jit(solution)/shard_map/experts/pallas_call | solution.py:466
  223.2 15.2 %weight_gradients.2 = (bf16[256,1536]{1,0:T(8,128)(2,1)S(1)}, bf16[256,1536]{1,0:T(8,128)(2,1)S(1)}, bf16[256,1536]{1,0:T(8,128)(2,1)S(1)}, bf16[256,1536]{1,0:T...) custom-call(bf16[256,1536]{1,0:T(8,128)(2,1)S(1)} %multiply_convert_fusio, ...), custom_call_target="tpu_custom_call" | custom-call | flops 150994944 | bytes 98304 | tf_op jit(solution)/shard_map/weight_gradients/pallas_call | solution.py:581
  241.9 3.5 collective-permute-done.31.refs_0_
  246.5 15.3 %weight_gradients.3 = (bf16[256,1536]{1,0:T(8,128)(2,1)S(1)}, bf16[256,1536]{1,0:T(8,128)(2,1)S(1)}, bf16[256,1536]{1,0:T(8,128)(2,1)S(1)}, bf16[256,1536]{1,0:T...) custom-call(bf16[256,1536]{1,0:T(8,128)(2,1)S(1)} %multiply_convert_fusio, ...), custom_call_target="tpu_custom_call" | custom-call | flops 150994944 | bytes 98304 | tf_op jit(solution)/shard_map/weight_gradients/pallas_call | solution.py:581
  263.6 5.4 collective-permute-done.32
  279.3 15.6 %collective-permute-done.36.rest_2_ = bf16[256,1536]{1,0:T(8,128)(2,1)S(1)} collective-permute-done((bf16[256,1536]{1,0:T(8,128)(2,1)S(1)}, bf16[256,1536]{1,0:T(8,128)(2,1)S(1)}, u32[]{:S(2)}, u32[]{:S(2)}) %collective-permute-start.36) | collective-permute-done | bytes 786464 | tf_op jit(solution)/shard_map/ppermute | solution.py:604
  320.0 20.3 %back.2 = (bf16[1024,320]{1,0:T(8,128)(2,1)S(1)}, f32[256,1536]{1,0:T(8,128)}, bf16[256,1536]{1,0:T(8,128)(2,1)S(1)}) custom-call(s32[2]{0:T(128)S(1)} %pad_add_fusion.mine_ref, bf16[256,1536]{1,0:T(8,128)(2,1)S(1)} %get-tuple-element.570.rest_0_, bf16[256,1536]{1,0:T(8,128)(2,1)S(1)} %copy-done.77, bf16[256,1536]{1,0:T(8,128)(2,1)S(1)} %copy-done.74, ...), custom_call_target="tpu_custom_call" | custom-call | flops 301989888 | bytes 294912 | tf_op jit(solution)/shard_map/back/pallas_call | solution.py:274
  345.3 3.7 adds.13
  352.1 20.4 %back.3 = (bf16[1024,320]{1,0:T(8,128)(2,1)S(1)}, f32[256,1536]{1,0:T(8,128)}, bf16[256,1536]{1,0:T(8,128)(2,1)S(1)}) custom-call(s32[2]{0:T(128)S(1)} %pad_add_fusion.mine_ref, bf16[256,1536]{1,0:T(8,128)(2,1)S(1)} %get-tuple-element.570.rest_0_, bf16[256,1536]{1,0:T(8,128)(2,1)S(1)} %copy-done.78, bf16[256,1536]{1,0:T(8,128)(2,1)S(1)} %copy-done.75, ...), custom_call_target="tpu_custom_call" | custom-call | flops 301989888 | bytes 294912 | tf_op jit(solution)/shard_map/back/pallas_call | solution.py:274
  392.5 12.8 %collective-permute-done.49 = bf16[288,1536]{1,0:T(8,128)(2,1)} collective-permute-done((bf16[288,1536]{1,0:T(8,128)(2,1)}, bf16[288,1536]{1,0:T(8,128)(2,1)}, u32[]{:S(2)}, u32[]{:S(2)}) %collective-permute-start.49) | collective-permute-done | bytes 884768 | tf_op jit(solution)/shard_map/ppermute | solution.py:604
  405.4 4.2 collective-permute-done.48
  418.1 3.7 collective-permute-start.53
  422.8 10.7 %collective-permute-done.53 = bf16[64,1536]{1,0:T(8,128)(2,1)S(1)} collective-permute-done((bf16[64,1536]{1,0:T(8,128)(2,1)S(1)}, bf16[64,1536]{1,0:T(8,128)(2,1)S(1)}, u32[]{:S(2)}, u32[]{:S(2)}) %collective-permute-start.53) | collective-permute-done | bytes 196640 | tf_op jit(solution)/shard_map/ppermute | solution.py:604
  437.6 3.7 collective-permute-start.57
  442.7 10.2 %collective-permute-done.59 = bf16[256,1536]{1,0:T(8,128)(2,1)} collective-permute-done((bf16[256,1536]{1,0:T(8,128)(2,1)}, bf16[256,1536]{1,0:T(8,128)(2,1)}, u32[]{:S(2)}, u32[]{:S(2)}) %collective-permute-start.59) | collective-permute-done | bytes 786464 | tf_op jit(solution)/shard_map/ppermute | solution.py:604
  453.4 10.6 %collective-permute-done.56 = bf16[64,1536]{1,0:T(8,128)(2,1)} collective-permute-done((bf16[64,1536]{1,0:T(8,128)(2,1)}, bf16[64,1536]{1,0:T(8,128)(2,1)}, u32[]{:S(2)}, u32[]{:S(2)}) %collective-permute-start.56) | collective-permute-done | bytes 196640 | tf_op jit(solution)/shard_map/ppermute | solution.py:604
  469.1 3.4 collective-permute-start.62
  472.5 4.3 place.2
  476.7 5.2 collective-permute-done.62
  497.6 3.1 copy.45
  505.3 6.9 %collective-permute-done.67 = bf16[128,1536]{1,0:T(8,128)(2,1)S(1)} collective-permute-done((bf16[128,1536]{1,0:T(8,128)(2,1)S(1)}, bf16[128,1536]{1,0:T(8,128)(2,1)S(1)}, u32[]{:S(2)}, u32[]{:S(2)}) %collective-permute-start.67) | collective-permute-done | bytes 393248 | tf_op jit(solution)/shard_map/ppermute | solution.py:604
  520.6 12.2 %collective-permute-done.71 = bf16[256,1536]{1,0:T(8,128)(2,1)S(1)} collective-permute-done((bf16[256,1536]{1,0:T(8,128)(2,1)S(1)}, bf16[256,1536]{1,0:T(8,128)(2,1)S(1)}, u32[]{:S(2)}, u32[]{:S(2)}) %collective-permute-start.71) | collective-permute-done | bytes 786464 | tf_op jit(solution)/shard_map/ppermute | solution.py:604
  (565 shorter events, 218.2 us)
Async XLA Ops:
  11.0 25.3 %collective-permute-start.2 = (bf16[256,1664]{1,0:T(8,128)(2,1)S(1)}, bf16[256,1664]{1,0:T(8,128)(2,1)}, u32[]{:S(2)}, u32[]{:S(2)}) collective-permute-start(bf16[256,1664]{1,0:T(8,128)(2,1)S(1)} %pad_maximum_fusion.2.rest_1_.rest_2_.rest_3_.rest_4_), channel_id=1, source_target_pairs={{0,8},{4,12},{8,16},{12,20},{16,24},{20,28},{24,0},{28,4},{1,9},{5... | collective-permute-start | bytes 2555912 | tf_op jit(solution)/shard_map/ppermute | solution.py:613
  36.3 31.7 %collective-permute-start.7 = (bf16[256,1664]{1,0:T(8,128)(2,1)}, bf16[256,1664]{1,0:T(8,128)(2,1)S(1)}, u32[]{:S(2)}, u32[]{:S(2)}) collective-permute-start(bf16[256,1664]{1,0:T(8,128)(2,1)} %collective-permute-done.2.rest_1_.rest_3_.rest_4_.rest_5_), channel_id=1, source_target_pairs={{0,8},{4,12},{8,16},{12,20},{16,24},{20,28},{24,0},{28,4},{1,9},{5... | collective-permute-start | bytes 2555912 | tf_op jit(solution)/shard_map/ppermute | solution.py:613
  37.8 30.1 %collective-permute-start.5 = (bf16[256,1536]{1,0:T(8,128)(2,1)}, bf16[256,1536]{1,0:T(8,128)(2,1)}, u32[]{:S(2)}, u32[]{:S(2)}) collective-permute-start(bf16[256,1536]{1,0:T(8,128)(2,1)} %bitcast.3.rest_2_), channel_id=1, source_target_pairs={{0,4},{4,0},{8,12},{12,8},{16,20},{20,16},{24,28},{28,24},{1,5},{5... | collective-permute-start | bytes 2359304 | tf_op jit(solution)/shard_map/ppermute | solution.py:604
  38.4 29.6 %collective-permute-start.6 = (bf16[256,1536]{1,0:T(8,128)(2,1)}, bf16[256,1536]{1,0:T(8,128)(2,1)}, u32[]{:S(2)}, u32[]{:S(2)}) collective-permute-start(bf16[256,1536]{1,0:T(8,128)(2,1)} %bitcast.3.rest_2_), channel_id=1, source_target_pairs={{0,2},{1,3},{2,0},{3,1},{4,6},{5,7},{6,4},{7,5},{8,10},{9,11},{10,... | collective-permute-start | bytes 2359304 | tf_op jit(solution)/shard_map/ppermute | solution.py:604
  39.9 28.1 %collective-permute-start.8 = (bf16[256,1536]{1,0:T(8,128)(2,1)}, bf16[256,1536]{1,0:T(8,128)(2,1)S(1)}, u32[]{:S(2)}, u32[]{:S(2)}) collective-permute-start(bf16[256,1536]{1,0:T(8,128)(2,1)} %collective-permute-done.rest_10_), channel_id=1, source_target_pairs={{0,1},{1,0},{2,3},{3,2},{4,5},{5,4},{6,7},{7,6},{8,9},{9,8},{10,11... | collective-permute-start | bytes 2359304 | tf_op jit(solution)/shard_map/ppermute | solution.py:604
  39.9 28.1 %collective-permute-start.9 = (bf16[256,1536]{1,0:T(8,128)(2,1)}, bf16[256,1536]{1,0:T(8,128)(2,1)S(1)}, u32[]{:S(2)}, u32[]{:S(2)}) collective-permute-start(bf16[256,1536]{1,0:T(8,128)(2,1)} %bitcast.5.rest_3_), channel_id=1, source_target_pairs={{0,1},{1,0},{2,3},{3,2},{4,5},{5,4},{6,7},{7,6},{8,9},{9,8},{10,11... | collective-permute-start | bytes 2359304 | tf_op jit(solution)/shard_map/ppermute | solution.py:604
  71.9 25.3 %collective-permute-start.14 = (bf16[256,1664]{1,0:T(8,128)(2,1)S(1)}, bf16[256,1664]{1,0:T(8,128)(2,1)S(1)}, u32[]{:S(2)}, u32[]{:S(2)}) collective-permute-start(bf16[256,1664]{1,0:T(8,128)(2,1)S(1)} %collective-permute-done.7.rest_1_.rest_5_.rest_6_), channel_id=1, source_target_pairs={{0,8},{4,12},{8,16},{12,20},{16,24},{20,28},{24,0},{28,4},{1,9},{5... | collective-permute-start | bytes 2555912 | tf_op jit(solution)/shard_map/ppermute | solution.py:613
  93.3 30.8 %collective-permute-start.20 = (bf16[256,1536]{1,0:T(8,128)(2,1)}, bf16[256,1536]{1,0:T(8,128)(2,1)}, u32[]{:S(2)}, u32[]{:S(2)}) collective-permute-start(bf16[256,1536]{1,0:T(8,128)(2,1)} %bitcast.5.rest_3_), channel_id=1, source_target_pairs={{0,2},{1,3},{2,0},{3,1},{4,6},{5,7},{6,4},{7,5},{8,10},{9,11},{10,... | collective-permute-start | bytes 2359304 | tf_op jit(solution)/shard_map/ppermute | solution.py:604
  93.8 30.3 %collective-permute-start.21 = (bf16[256,1536]{1,0:T(8,128)(2,1)}, bf16[256,1536]{1,0:T(8,128)(2,1)}, u32[]{:S(2)}, u32[]{:S(2)}) collective-permute-start(bf16[256,1536]{1,0:T(8,128)(2,1)} %collective-permute-done.1.rest_6_.rest_16_), channel_id=1, source_target_pairs={{0,4},{4,0},{8,12},{12,8},{16,20},{20,16},{24,28},{28,24},{1,5},{5... | collective-permute-start | bytes 2359304 | tf_op jit(solution)/shard_map/ppermute | solution.py:604
  124.2 30.9 %collective-permute-start.23 = (bf16[256,1536]{1,0:T(8,128)(2,1)}, bf16[256,1536]{1,0:T(8,128)(2,1)S(1)}, u32[]{:S(2)}, u32[]{:S(2)}) collective-permute-start(bf16[256,1536]{1,0:T(8,128)(2,1)} %collective-permute-done.5.rest_8_), channel_id=1, source_target_pairs={{0,2},{1,3},{2,0},{3,1},{4,6},{5,7},{6,4},{7,5},{8,10},{9,11},{10,... | collective-permute-start | bytes 2359304 | tf_op jit(solution)/shard_map/ppermute | solution.py:604
  125.9 29.3 %collective-permute-start.24 = (bf16[256,1536]{1,0:T(8,128)(2,1)}, bf16[256,1536]{1,0:T(8,128)(2,1)S(1)}, u32[]{:S(2)}, u32[]{:S(2)}) collective-permute-start(bf16[256,1536]{1,0:T(8,128)(2,1)} %collective-permute-done.20.rest_5_.rest_15_), channel_id=1, source_target_pairs={{0,4},{4,0},{8,12},{12,8},{16,20},{20,16},{24,28},{28,24},{1,5},{5... | collective-permute-start | bytes 2359304 | tf_op jit(solution)/shard_map/ppermute | solution.py:604
  126.4 28.8 %collective-permute-start.22 = (bf16[256,1536]{1,0:T(8,128)(2,1)S(1)}, bf16[256,1536]{1,0:T(8,128)(2,1)S(1)}, u32[]{:S(2)}, u32[]{:S(2)}) collective-permute-start(bf16[256,1536]{1,0:T(8,128)(2,1)S(1)} %collective-permute-done.19.rest_0_.rest_1_), channel_id=1, source_target_pairs={{0,8},{4,12},{8,16},{12,20},{16,24},{20,28},{24,0},{28,4},{1,9},{5... | collective-permute-start | bytes 2359304 | tf_op jit(solution)/shard_map/ppermute | solution.py:613
  128.0 27.2 %collective-permute-start.26 = (bf16[256,1536]{1,0:T(8,128)(2,1)}, bf16[256,1536]{1,0:T(8,128)(2,1)S(1)}, u32[]{:S(2)}, u32[]{:S(2)}) collective-permute-start(bf16[256,1536]{1,0:T(8,128)(2,1)} %collective-permute-done.21.rest_8_.rest_22_), channel_id=1, source_target_pairs={{0,1},{1,0},{2,3},{3,2},{4,5},{5,4},{6,7},{7,6},{8,9},{9,8},{10,11... | collective-permute-start | bytes 2359304 | tf_op jit(solution)/shard_map/ppermute | solution.py:604
  155.9 40.2 %collective-permute-start.27 = (bf16[256,1536]{1,0:T(8,128)(2,1)S(1)}, bf16[256,1536]{1,0:T(8,128)(2,1)}, u32[]{:S(2)}, u32[]{:S(2)}) collective-permute-start(bf16[256,1536]{1,0:T(8,128)(2,1)S(1)} %collective-permute-done.22.rest_0_.rest_2_), channel_id=1, source_target_pairs={{0,8},{4,12},{8,16},{12,20},{16,24},{20,28},{24,0},{28,4},{1,9},{5... | collective-permute-start | bytes 2359304 | tf_op jit(solution)/shard_map/ppermute | solution.py:613
  196.0 25.7 %collective-permute-start.30 = (bf16[256,1664]{1,0:T(8,128)(2,1)S(1)}, bf16[256,1664]{1,0:T(8,128)(2,1)S(1)}, u32[]{:S(2)}, u32[]{:S(2)}) collective-permute-start(bf16[256,1664]{1,0:T(8,128)(2,1)S(1)} %get-tuple-element.437), channel_id=1, source_target_pairs={{0,8},{4,12},{8,16},{12,20},{16,24},{20,28},{24,0},{28,4},{1,9},{5... | collective-permute-start | bytes 2555912 | tf_op jit(solution)/shard_map/ppermute | solution.py:613
  245.3 23.7 %collective-permute-start.33 = (bf16[1536,1536]{1,0:T(8,128)(2,1)}, bf16[1536,1536]{1,0:T(8,128)(2,1)S(1)}, u32[]{:S(2)}, u32[]{:S(2)}) collective-permute-start(bf16[1536,1536]{1,0:T(8,128)(2,1)} %get-tuple-element.485), channel_id=1, source_target_pairs={{0,1},{1,0},{2,3},{3,2},{4,5},{5,4},{6,7},{7,6},{8,9},{9,8},{10,11... | collective-permute-start | bytes 14155784 | tf_op jit(solution)/shard_map/ppermute | solution.py:604
  245.6 23.4 %collective-permute-start.32 = (bf16[256,1664]{1,0:T(8,128)(2,1)S(1)}, bf16[256,1664]{1,0:T(8,128)(2,1)S(1)}, u32[]{:S(2)}, u32[]{:S(2)}) collective-permute-start(bf16[256,1664]{1,0:T(8,128)(2,1)S(1)} %adds.8), channel_id=1, source_target_pairs={{0,8},{4,12},{8,16},{12,20},{16,24},{20,28},{24,0},{28,4},{1,9},{5... | collective-permute-start | bytes 2555912 | tf_op jit(solution)/shard_map/ppermute | solution.py:613
  274.9 24.1 %collective-permute-start.40 = (bf16[1536,1536]{1,0:T(8,128)(2,1)}, bf16[1536,1536]{1,0:T(8,128)(2,1)S(1)}, u32[]{:S(2)}, u32[]{:S(2)}) collective-permute-start(bf16[1536,1536]{1,0:T(8,128)(2,1)} %get-tuple-element.509), channel_id=1, source_target_pairs={{0,1},{1,0},{2,3},{3,2},{4,5},{5,4},{6,7},{7,6},{8,9},{9,8},{10,11... | collective-permute-start | bytes 14155784 | tf_op jit(solution)/shard_map/ppermute | solution.py:604
  302.1 43.1 %collective-permute-start.34 = (bf16[256,1536]{1,0:T(8,128)(2,1)}, bf16[256,1536]{1,0:T(8,128)(2,1)}, u32[]{:S(2)}, u32[]{:S(2)}) collective-permute-start(bf16[256,1536]{1,0:T(8,128)(2,1)} %get-tuple-element.504), channel_id=1, source_target_pairs={{0,2},{1,3},{2,0},{3,1},{4,6},{5,7},{6,4},{7,5},{8,10},{9,11},{10,... | collective-permute-start | bytes 2359304 | tf_op jit(solution)/shard_map/ppermute | solution.py:604
  303.7 41.6 %collective-permute-start.35 = (bf16[256,1536]{1,0:T(8,128)(2,1)}, bf16[256,1536]{1,0:T(8,128)(2,1)}, u32[]{:S(2)}, u32[]{:S(2)}) collective-permute-start(bf16[256,1536]{1,0:T(8,128)(2,1)} %get-tuple-element.505), channel_id=1, source_target_pairs={{0,4},{4,0},{8,12},{12,8},{16,20},{20,16},{24,28},{28,24},{1,5},{5... | collective-permute-start | bytes 2359304 | tf_op jit(solution)/shard_map/ppermute | solution.py:604
  307.0 38.2 %collective-permute-start.42 = (bf16[256,1536]{1,0:T(8,128)(2,1)}, bf16[256,1536]{1,0:T(8,128)(2,1)}, u32[]{:S(2)}, u32[]{:S(2)}) collective-permute-start(bf16[256,1536]{1,0:T(8,128)(2,1)} %get-tuple-element.524), channel_id=1, source_target_pairs={{0,8},{4,12},{8,16},{12,20},{16,24},{20,28},{24,0},{28,4},{1,9},{5... | collective-permute-start | bytes 2359304 | tf_op jit(solution)/shard_map/ppermute | solution.py:613
  349.1 23.4 %collective-permute-start.43 = (bf16[256,1536]{1,0:T(8,128)(2,1)S(1)}, bf16[256,1536]{1,0:T(8,128)(2,1)S(1)}, u32[]{:S(2)}, u32[]{:S(2)}) collective-permute-start(bf16[256,1536]{1,0:T(8,128)(2,1)S(1)} %copy-done.128), channel_id=1, source_target_pairs={{0,2},{1,3},{2,0},{3,1},{4,6},{5,7},{6,4},{7,5},{8,10},{9,11},{10,... | collective-permute-start | bytes 2359304 | tf_op jit(solution)/shard_map/ppermute | solution.py:604
  349.7 22.8 %collective-permute-start.45 = (bf16[256,1536]{1,0:T(8,128)(2,1)S(1)}, bf16[256,1536]{1,0:T(8,128)(2,1)S(1)}, u32[]{:S(2)}, u32[]{:S(2)}) collective-permute-start(bf16[256,1536]{1,0:T(8,128)(2,1)S(1)} %get-tuple-element.569), channel_id=1, source_target_pairs={{0,8},{4,12},{8,16},{12,20},{16,24},{20,28},{24,0},{28,4},{1,9},{5... | collective-permute-start | bytes 2359304 | tf_op jit(solution)/shard_map/ppermute | solution.py:613
  349.7 22.9 %collective-permute-start.44 = (bf16[256,1536]{1,0:T(8,128)(2,1)S(1)}, bf16[256,1536]{1,0:T(8,128)(2,1)S(1)}, u32[]{:S(2)}, u32[]{:S(2)}) collective-permute-start(bf16[256,1536]{1,0:T(8,128)(2,1)S(1)} %get-tuple-element.568), channel_id=1, source_target_pairs={{0,4},{4,0},{8,12},{12,8},{16,20},{20,16},{24,28},{28,24},{1,5},{5... | collective-permute-start | bytes 2359304 | tf_op jit(solution)/shard_map/ppermute | solution.py:604
  382.5 22.8 %collective-permute-start.49 = (bf16[288,1536]{1,0:T(8,128)(2,1)}, bf16[288,1536]{1,0:T(8,128)(2,1)}, u32[]{:S(2)}, u32[]{:S(2)}) collective-permute-start(bf16[288,1536]{1,0:T(8,128)(2,1)} %pad_maximum_fusion), channel_id=1, source_target_pairs={{0,4},{4,0},{8,12},{12,8},{16,20},{20,16},{24,28},{28,24},{1,5},{5... | collective-permute-start | bytes 2654216 | tf_op jit(solution)/shard_map/ppermute | solution.py:604
  392.0 30.2 %collective-permute-start.55 = (bf16[256,1536]{1,0:T(8,128)(2,1)}, bf16[256,1536]{1,0:T(8,128)(2,1)S(1)}, u32[]{:S(2)}, u32[]{:S(2)}) collective-permute-start(bf16[256,1536]{1,0:T(8,128)(2,1)} %get-tuple-element.602), channel_id=1, source_target_pairs={{0,4},{4,0},{8,12},{12,8},{16,20},{20,16},{24,28},{28,24},{1,5},{5... | collective-permute-start | bytes 2359304 | tf_op jit(solution)/shard_map/ppermute | solution.py:604
  437.6 26.5 %collective-permute-start.60 = (bf16[256,1536]{1,0:T(8,128)(2,1)S(1)}, bf16[256,1536]{1,0:T(8,128)(2,1)}, u32[]{:S(2)}, u32[]{:S(2)}) collective-permute-start(bf16[256,1536]{1,0:T(8,128)(2,1)S(1)} %collective-permute-done.51.refs_2_), channel_id=1, source_target_pairs={{0,1},{1,0},{2,3},{3,2},{4,5},{5,4},{6,7},{7,6},{8,9},{9,8},{10,11... | collective-permute-start | bytes 2359304 | tf_op jit(solution)/shard_map/ppermute | solution.py:604
  437.6 26.5 %collective-permute-start.57 = (bf16[96,1536]{1,0:T(8,128)(2,1)}, bf16[96,1536]{1,0:T(8,128)(2,1)}, u32[]{:S(2)}, u32[]{:S(2)}) collective-permute-start(bf16[96,1536]{1,0:T(8,128)(2,1)} %pad_maximum_fusion.8), channel_id=1, source_target_pairs={{0,16},{4,20},{8,24},{12,28},{16,0},{20,4},{24,8},{28,12},{1,17},{... | collective-permute-start | bytes 884744 | tf_op jit(solution)/shard_map/ppermute | solution.py:604
  441.3 22.7 %collective-permute-start.56 = (bf16[64,1536]{1,0:T(8,128)(2,1)}, bf16[64,1536]{1,0:T(8,128)(2,1)}, u32[]{:S(2)}, u32[]{:S(2)}) collective-permute-start(bf16[64,1536]{1,0:T(8,128)(2,1)} %add_convert_fusion.4), channel_id=1, source_target_pairs={{0,16},{4,20},{8,24},{12,28},{16,0},{20,4},{24,8},{28,12},{1,17},{... | collective-permute-start | bytes 589832 | tf_op jit(solution)/shard_map/ppermute | solution.py:604
  442.2 34.6 %collective-permute-start.63 = (bf16[256,1536]{1,0:T(8,128)(2,1)}, bf16[256,1536]{1,0:T(8,128)(2,1)}, u32[]{:S(2)}, u32[]{:S(2)}) collective-permute-start(bf16[256,1536]{1,0:T(8,128)(2,1)} %copy-done.126), channel_id=1, source_target_pairs={{0,4},{4,0},{8,12},{12,8},{16,20},{20,16},{24,28},{28,24},{1,5},{5... | collective-permute-start | bytes 2359304 | tf_op jit(solution)/shard_map/ppermute | solution.py:604
  452.9 23.8 %collective-permute-start.64 = (bf16[256,1536]{1,0:T(8,128)(2,1)}, bf16[256,1536]{1,0:T(8,128)(2,1)}, u32[]{:S(2)}, u32[]{:S(2)}) collective-permute-start(bf16[256,1536]{1,0:T(8,128)(2,1)} %copy-done.125), channel_id=1, source_target_pairs={{0,2},{1,3},{2,0},{3,1},{4,6},{5,7},{6,4},{7,5},{8,10},{9,11},{10,... | collective-permute-start | bytes 2359304 | tf_op jit(solution)/shard_map/ppermute | solution.py:604
  519.4 30.8 %collective-permute-start.70 = (bf16[256,1536]{1,0:T(8,128)(2,1)S(1)}, bf16[256,1536]{1,0:T(8,128)(2,1)S(1)}, u32[]{:S(2)}, u32[]{:S(2)}) collective-permute-start(bf16[256,1536]{1,0:T(8,128)(2,1)S(1)} %slice.176.refs_2_), channel_id=1, source_target_pairs={{0,1},{1,0},{2,3},{3,2},{4,5},{5,4},{6,7},{7,6},{8,9},{9,8},{10,11... | collective-permute-start | bytes 2359304 | tf_op jit(solution)/shard_map/ppermute | solution.py:604
  (203 other events, 1633.6 us)

commit v3 on v2

--- a/solution.py
+++ b/solution.py
@@ -20,6 +20,9 @@
 TN = (((0,), (0,)), ((), ()))
 BLOCK = 256
 EXTRA = 32
+AHEAD = 2
+TILE = 512
+VMEM_GRANT = 58 * 1024 * 1024
 
 
 def cost_of(flops, size):
@@ -45,6 +48,10 @@
         jnp.asarray(np.concatenate([cosine, cosine], axis=1)),
         jnp.asarray(np.concatenate([-sine, sine], axis=1)),
     )
+
+
+def entire(shape):
+    return pl.BlockSpec(shape, lambda i: (0,) * len(shape))
 
 
 def normalized(values):
@@ -101,7 +108,7 @@
         + [fixed(w) for w in weights]
         + [strip(HEAD_WIDTH), strip(HEAD_WIDTH)],
         out_specs=[strip(width), of_heads(heads), of_heads(groups), of_heads(groups)],
-        compiler_params=pltpu.CompilerParams(vmem_limit_bytes=32 * 1024 * 1024),
+        compiler_params=pltpu.CompilerParams(vmem_limit_bytes=VMEM_GRANT),
         cost_estimate=cost_of(8 * length * width * width, 12 * length * width),
         name="front",
     )(x, gain, *weights, cosine, sine)
@@ -130,7 +137,7 @@
             out_shape=[jax.ShapeDtypeStruct((rows, width), LOW)] * count,
             in_specs=specs,
             out_specs=[block] * count,
-            compiler_params=pltpu.CompilerParams(vmem_limit_bytes=40 * 1024 * 1024),
+            compiler_params=pltpu.CompilerParams(vmem_limit_bytes=VMEM_GRANT),
             cost_estimate=cost_of(1000, 6 * count * rows * width),
             name="adds",
         )(*values)
@@ -172,32 +179,34 @@
     groups = k.shape[0]
     width = output_weight.shape[1]
     rows = length // count
-    whole = pl.BlockSpec(memory_space=pltpu.VMEM)
     shape = jax.ShapeDtypeStruct
     results = pl.pallas_call(
-        functools.partial(attention_body, heads, groups, rows, min(256, length)),
+        functools.partial(attention_body, heads, groups, rows, min(2 * TILE, length)),
+        grid=(1,),
         out_shape=[
             shape((length, heads * HEAD_WIDTH), LOW),
             shape((heads, 1, length), FULL),
         ]
         + [shape((rows, width), LOW if r % 2 else FULL) for r in range(count)],
-        in_specs=[pl.BlockSpec(memory_space=pltpu.SMEM)] + [whole] * 6,
-        out_specs=[whole] * (2 + count),
+        in_specs=[pl.BlockSpec(memory_space=pltpu.SMEM)]
+        + [entire(v.shape) for v in (q, k, v, output_weight, column, row)],
+        out_specs=[entire((length, heads * HEAD_WIDTH)), entire((heads, 1, length))]
+        + [entire((rows, width))] * count,
         scratch_shapes=[
             pltpu.VMEM((groups, HEAD_WIDTH, length), LOW),
             pltpu.VMEM((heads, length, HEAD_WIDTH), LOW),
         ],
-        compiler_params=pltpu.CompilerParams(vmem_limit_bytes=40 * 1024 * 1024),
+        compiler_params=pltpu.CompilerParams(vmem_limit_bytes=VMEM_GRANT),
         cost_estimate=cost_of(12 * length * width * width, 12 * length * width),
         name="attention",
     )(mine, q, k, v, output_weight, column, row)
     return results[0], results[1], list(results[2:])
 
 
-def back_body(count, group, size, rows, tile, mine_ref, *rest):
+def back_body(count, group, size, rows, tile, split, mine_ref, *rest):
     da_refs = rest[:count]
     (h_in, wo_ref, mix_ref, q_ref, k_ref, v_ref, lse_ref, column_ref, row_ref, cos_ref, sin_ref,
-     d_ref, keep_ref, send_ref, da_ref, h_ref, do_ref, turned_ref, dk_ref, dv_ref, dq_ref,
+     d_ref, *outs, da_ref, h_ref, do_ref, turned_ref, dk_ref, dv_ref, dq_ref,
      square_ref, landed) = rest[count:]
     length = row_ref.shape[1]
     scale = HEAD_WIDTH ** (-0.5)
@@ -253,35 +262,52 @@
     depth = (size + 2) * HEAD_WIDTH
     square_ref[0:depth, :] = mul(d_ref[...], h_ref[...], TN)
     square_ref[depth:, :] = mul(mix_ref[:, span], da_ref[...], TN)
+    if not split:
+        outs[0][...] = square_ref[...].astype(LOW)
+        return
+    keep_ref, send_ref = outs
     half = keep_ref.shape[0]
     for side in range(2):
 
         @pl.when(mine_ref[1] == side)
         def _(side=side):
             keep_ref[...] = square_ref[side * half : (side + 1) * half, :]
-            send_ref[...] = square_ref[(1 - side) * half : (2 - side) * half, :].astype(LOW)
-
-
-def run_back(group, mine, da, hidden, output_weight, mixture, q, k, v, lse, column, row, cosine, sine):
+            send_ref[0:half, :] = square_ref[(1 - side) * half : (2 - side) * half, :].astype(LOW)
+
+    send_ref[half:, :] = jnp.zeros((EXTRA, send_ref.shape[1]), LOW)
+
+
+def run_back(group, split, mine, da, hidden, output_weight, mixture, q, k, v, lse, column, row, cosine, sine):
     heads, length, _ = q.shape
     groups = k.shape[0]
     size = heads // groups
     rows, width = da[0].shape
     count = len(da)
     half = (size + 1) * HEAD_WIDTH
-    whole = pl.BlockSpec(memory_space=pltpu.VMEM)
     shape = jax.ShapeDtypeStruct
     return pl.pallas_call(
-        functools.partial(back_body, count, group, size, rows, min(256, length)),
-        out_shape=(
+        functools.partial(back_body, count, group, size, rows, min(TILE, length), split),
+        grid=(1,),
+        out_shape=[
             shape((length, (size + 2) * HEAD_WIDTH), LOW),
-            shape((half, width), FULL),
-            shape((half, width), LOW),
+        ]
+        + (
+            [shape((half, width), FULL), shape((half + EXTRA, width), LOW)]
+            if split
+            else [shape((2 * half, width), LOW)]
         ),
         in_specs=[pl.BlockSpec(memory_space=pltpu.SMEM)]
         + [pl.BlockSpec(memory_space=pltpu.HBM)] * (count + 1)
-        + [whole] * 10,
-        out_specs=(whole, whole, whole),
+        + [
+            entire(v.shape)
+            for v in (output_weight, mixture, q, k, v, lse, column, row, cosine, sine)
+        ],
+        out_specs=[entire((length, (size + 2) * HEAD_WIDTH))]
+        + (
+            [entire((half, width)), entire((half + EXTRA, width))]
+            if split
+            else [entire((2 * half, width))]
+        ),
         scratch_shapes=[
             pltpu.VMEM((length, width), LOW),
             pltpu.VMEM((length, width), LOW),
@@ -293,16 +319,175 @@
             pltpu.VMEM((2 * half, width), FULL),
             pltpu.SemaphoreType.DMA((count + 1,)),
         ],
-        compiler_params=pltpu.CompilerParams(vmem_limit_bytes=44 * 1024 * 1024),
+        compiler_params=pltpu.CompilerParams(vmem_limit_bytes=VMEM_GRANT),
         cost_estimate=cost_of(8 * length * width * width, 12 * length * width),
         name="back",
     )(mine, *da, hidden, output_weight, mixture, q, k, v, lse, column, row, cosine, sine)
 
 
+def first_body(groups, count, x_ref, *rest):
+    d_refs, w_refs = rest[:groups], rest[groups : 2 * groups]
+    out_refs, gain_ref = rest[2 * groups : -1], rest[-1]
+    step = pl.program_id(0)
+    d_first = mul(d_refs[0][...], w_refs[0][...], NT)
+    for d_ref, w_ref in zip(d_refs[1:], w_refs[1:]):
+        d_first = d_first + mul(d_ref[...], w_ref[...], NT)
+    x = x_ref[...].astype(FULL)
+    part = jnp.sum(d_first * (x * normalized(x)), axis=0, keepdims=True)
+
+    @pl.when(step == 0)
+    def _():
+        gain_ref[...] = part
+
+    @pl.when(step != 0)
+    def _():
+        gain_ref[...] += part
+
+    for r in range(count):
+
+        @pl.when(step == r)
+        def _(r=r):
+            out_refs[r][...] = d_first.astype(out_refs[r].dtype)
+
+
+def run_first(mine, x, d_projected, weights, count):
+    length, width = x.shape
+    rows = length // count
+    groups = len(weights)
+    depth = weights[0].shape[1]
+    strip = lambda columns: pl.BlockSpec((rows, columns), lambda r, m: (m[0] ^ r, 0))
+    fixed = lambda shape: pl.BlockSpec(shape, lambda r, m: (0, 0))
+    results = pl.pallas_call(
+        lambda m, *refs: first_body(groups, count, *refs),
+        grid_spec=pltpu.PrefetchScalarGridSpec(
+            num_scalar_prefetch=1,
+            grid=(count,),
+            in_specs=[strip(width)]
+            + [strip(depth)] * groups
+            + [fixed((width, depth))] * groups,
+            out_specs=[fixed((rows, width))] * count + [fixed((1, width))],
+        ),
+        out_shape=[
+            jax.ShapeDtypeStruct((rows, width), LOW if r % 2 else FULL) for r in range(count)
+        ]
+        + [jax.ShapeDtypeStruct((1, width), FULL)],
+        compiler_params=pltpu.CompilerParams(vmem_limit_bytes=VMEM_GRANT),
+        cost_estimate=cost_of(1000, 1000),
+        name="first_gradients",
+    )(mine, x, *d_projected, *weights)
+    return list(results[:-1]), results[-1]
+
+
+def token_body(num_experts, came_ref, own_ref, h_ref, router_ref, code_ref, mid_ref, gain_ref,
+               g_ref, mid_out, low_out, gain_out, router_out):
+    width = h_ref.shape[1]
+    total = came_ref[...].astype(FULL) + own_ref[...].astype(FULL)
+    d_gates = jnp.zeros(code_ref.shape, FULL)
+    for n in range(3):
+        tile, turn = divmod(n * num_experts, LANES)
+        part = total[:, width + tile * LANES : width + (tile + 1) * LANES]
+        d_gates = d_gates + (pltpu.roll(part, LANES - turn, 1) if turn else part)
+    h = h_ref[...]
+    code = code_ref[...]
+    logits = mul(h, router_ref[...])
+    picked = code > 0.5
+    peak = jnp.max(jnp.where(picked, logits, NEGATIVE), axis=1, keepdims=True)
+    exponent = jnp.where(picked, jnp.exp(logits - peak), 0.0)
+    gates = exponent / jnp.sum(exponent, axis=1, keepdims=True)
+    d_gates = jnp.where(code > 1.5, d_gates, 0.0)
+    d_logits = gates * (d_gates - jnp.sum(gates * d_gates, axis=1, keepdims=True))
+    d_logits = d_logits.astype(LOW)
+    d_hidden = total[:, :width] + mul(d_logits, router_ref[...], NT)
+    router_out[...] = mul(d_logits, h, TN)[:num_experts]
+    mid = mid_ref[...]
+    inverse = normalized(mid)
+    normed = mid * inverse
+    gain_out[...] = jnp.sum(d_hidden * normed, axis=0, keepdims=True)
+    scaled = d_hidden * gain_ref[...]
+    d_mid = g_ref[...].astype(FULL) + inverse * (
+        scaled - normed * jnp.mean(scaled * normed, axis=1, keepdims=True)
+    )
+    mid_out[...] = d_mid
+    low_out[...] = d_mid.astype(LOW)
+
+
+def run_token(came, own, h, router, code, mid, gain, g, num_experts):
+    rows, width = h.shape
+    values = (came, own, h, router, code, mid, gain, g)
+    shape = jax.ShapeDtypeStruct
+    outs = ((rows, width), FULL), ((rows, width), LOW), ((1, width), FULL), ((num_experts, width), FULL)
+    return pl.pallas_call(
+        functools.partial(token_body, num_experts),
+        grid=(1,),
+        in_specs=[entire(v.shape) for v in values],
+        out_specs=[entire(size) for size, _ in outs],
+        out_shape=[shape(size, kind) for size, kind in outs],
+        compiler_params=pltpu.CompilerParams(vmem_limit_bytes=VMEM_GRANT),
+        cost_estimate=cost_of(1000, 1000),
+        name="token_gradients",
+    )(*values)
+
+
+def finish_body(size, groups, split, mine_ref, *refs):
+    count = 2 * groups if split else groups
+    q_ref, k_ref, v_ref, o_ref = refs[count : count + 4]
+    if split:
+        half = refs[0].shape[0]
+        wholes = refs[count + 4 :]
+        for n in range(groups):
+            for side in range(2):
+                near = slice(side * half, (side + 1) * half)
+                other = slice((1 - side) * half, (2 - side) * half)
+
+                @pl.when(mine_ref[1] == side)
+                def _(n=n, near=near, other=other):
+                    wholes[n][near, :] = refs[2 * n][...]
+                    wholes[n][other, :] = refs[2 * n + 1][...]
+
+    else:
+        wholes = refs[:groups]
+    cut = size * HEAD_WIDTH
+    spans = ((q_ref, 0, cut), (k_ref, cut, cut + HEAD_WIDTH), (v_ref, cut + HEAD_WIDTH, cut + 2 * HEAD_WIDTH))
+    for ref, start, end in spans:
+        ref[...] = jnp.concatenate([w[start:end, :].astype(FULL) for w in wholes]).T
+    end = cut + 2 * HEAD_WIDTH
+    for i, w in enumerate(wholes):
+        o_ref[i * cut : (i + 1) * cut, :] = w[end:, :].astype(FULL)
+
+
+def run_finish(mine, wholes, size, halves=None):
+    values = wholes if halves is None else [v for pair_of in halves for v in pair_of]
+    groups = len(wholes if halves is None else halves)
+    depth, width = values[0].shape
+    tile = 256
+    heads = size * groups * HEAD_WIDTH
+    down = lambda n: pl.BlockSpec((tile, n), lambda i: (i, 0))
+    along = lambda n: pl.BlockSpec((n, tile), lambda i: (0, i))
+    shape = jax.ShapeDtypeStruct
+    return pl.pallas_call(
+        functools.partial(finish_body, size, groups, halves is not None),
+        grid=(width // tile,),
+        in_specs=[pl.BlockSpec(memory_space=pltpu.SMEM)] + [along(depth)] * len(values),
+        out_specs=[down(heads), down(groups * HEAD_WIDTH), down(groups * HEAD_WIDTH), along(heads)],
+        out_shape=[
+            shape((width, heads), FULL),
+            shape((width, groups * HEAD_WIDTH), FULL),
+            shape((width, groups * HEAD_WIDTH), FULL),
+            shape((heads, width), FULL),
+        ],
+        scratch_shapes=[]
+        if halves is None
+        else [pltpu.VMEM((2 * depth, tile), LOW)] * groups,
+        compiler_params=pltpu.CompilerParams(vmem_limit_bytes=VMEM_GRANT),
+        cost_estimate=cost_of(1000, 1000),
+        name="finish",
+    )(mine, *values)
+
+
 def place_body(rows, mine_ref, *refs):
     for r, ref in enumerate(refs[:-1]):
         at = pl.ds(pl.multiple_of((mine_ref[0] ^ r) * rows, rows), rows)
-        refs[-1][at, :] = ref[...].astype(refs[-1].dtype)
+        refs[-1][at, :] = ref[0:rows, :].astype(refs[-1].dtype)
 
 
 def run_place(mine, blocks, kind):
@@ -360,13 +545,17 @@
                     begin(before[j * block_count + i], target.at[span[i]], landed.at[i, 3 + j])
                 )
     copies = []
-    for s in range(shard_count):
+
+    def fetch(s):
         targets = (
             first_buffer.at[pl.ds(s * first, wide)],
             first_buffer.at[pl.ds(s * first + wide, wide)],
             second_buffer.at[pl.ds(s * wide, wide)],
         )
         copies.append([begin(w_refs[s][j], targets[j], arrived.at[s, j]) for j in range(3)])
+
+    for s in range(min(AHEAD, shard_count)):
+        fetch(s)
     for load in loads:
         load.wait()
     code = code_ref[...].astype(FULL)
@@ -386,6 +575,8 @@
     for s in range(shard_count):
         for copy in copies[s]:
             copy.wait()
+        if s + AHEAD < shard_count:
+            fetch(s + AHEAD)
         place = local * places[s]
 
         @pl.loop(0, total // row_tile)
@@ -465,7 +656,7 @@
     extra = [] if before is None else before[0] + before[1] + before[2]
     results = pl.pallas_call(
         functools.partial(
-            expert_body, tuple(places), blocks, local, hidden, total // -(-total // 512), 512,
+            expert_body, tuple(places), blocks, local, hidden, total // -(-total // 512), width,
             num_experts, bool(extra),
         ),
         out_shape=[shape((rows, width), LOW)] * blocks
@@ -491,7 +682,7 @@
             pltpu.SemaphoreType.DMA((blocks + 1, 3)),
         ],
         compiler_params=pltpu.CompilerParams(
-            vmem_limit_bytes=min(56, 16 + total * count * 3 // 500 + count * 3) * 1024 * 1024
+            vmem_limit_bytes=VMEM_GRANT
         ),
         cost_estimate=cost_of(4 * total * width * depth * count, depth * width * count * 2),
         name="experts",
@@ -513,8 +704,9 @@
     hid_refs = take(plan[0][0])
     stay = len(shards_plan) // 2
     out_refs = [take(3) for _ in range(stay)]
-    (away_ref,) = take(1)
-    h_ref, g_ref, first_ref, second_ref, landed, arrived = rest
+    loose = plan[2]
+    away_refs = take(3 * loose + stay - loose)
+    h_ref, g_ref, first_ref, second_ref, out_buffer, landed, arrived, left = rest
     loads = []
     for i in range(blocks):
         at = pl.ds(i * rows, rows)
@@ -548,6 +740,7 @@
         return group
 
     waiting = fetch(0)
+    leaves = []
     for load in loads:
         load.wait()
     for s in range(len(shards_plan)):
@@ -561,42 +754,59 @@
             lambda: mul(second_ref[slot], g_ref[...], TN),
         )
         for j in range(3):
+            start = 3 * s + j
+            out_buffer[start * wide : (start + 1) * wide, :] = sums[j]().astype(LOW)
             if s < stay:
-                out_refs[s][j][...] = sums[j]().astype(LOW)
+                target = out_refs[s][j]
+            elif s - stay < loose:
+                target = away_refs[3 * (s - stay) + j]
             else:
-                start = (3 * (s - stay) + j) * wide
-                away_ref[start : start + wide, :] = sums[j]().astype(LOW)
+                target = away_refs[s - stay + 2 * loose].at[pl.ds(j * wide, wide)]
+            leave = pltpu.make_async_copy(
+                out_buffer.at[pl.ds(start * wide, wide)], target, left.at[start]
+            )
+            leave.start()
+            leaves.append(leave)
         waiting = following
-
-
-def run_weights(h, g, hids, shards_plan, wide):
+    for leave in leaves:
+        leave.wait()
+
+
+def run_weights(h, g, hids, shards_plan, wide, loose=0):
     blocks = len(h)
     rows, width = h[0].shape
     total = blocks * rows
     stay = len(shards_plan) // 2
     pieces = max(len(p) for p in shards_plan)
-    whole = pl.BlockSpec(memory_space=pltpu.VMEM)
     away = pl.BlockSpec(memory_space=pltpu.HBM)
-    plan = ((len(hids), blocks), tuple(tuple(p) for p in shards_plan))
+    plan = ((len(hids), blocks), tuple(tuple(p) for p in shards_plan), loose)
     results = pl.pallas_call(
         functools.partial(weight_body, plan, rows, wide),
         out_shape=[jax.ShapeDtypeStruct((wide, width), LOW)] * (3 * stay)
-        + [jax.ShapeDtypeStruct((3 * stay * wide, width), LOW)],
+        + [jax.ShapeDtypeStruct((wide, width), LOW)] * (3 * loose)
+        + [jax.ShapeDtypeStruct((3 * wide, width), LOW)] * (stay - loose),
         in_specs=[away] * (2 * blocks + len(hids)),
-        out_specs=[whole] * (3 * stay + 1),
+        out_specs=[away] * (4 * stay + 2 * loose),
         scratch_shapes=[
             pltpu.VMEM((total, width), LOW),
             pltpu.VMEM((total, width), LOW),
             pltpu.VMEM((2, total, 2 * wide), LOW),
             pltpu.VMEM((2, total, wide), LOW),
+            pltpu.VMEM((6 * stay * wide, width), LOW),
             pltpu.SemaphoreType.DMA((blocks, 2)),
             pltpu.SemaphoreType.DMA((2, pieces, 2)),
+            pltpu.SemaphoreType.DMA((6 * stay,)),
         ],
-        compiler_params=pltpu.CompilerParams(vmem_limit_bytes=44 * 1024 * 1024),
+        compiler_params=pltpu.CompilerParams(vmem_limit_bytes=VMEM_GRANT),
         cost_estimate=cost_of(12 * total * width * wide * stay, total * 6 * wide * stay * 2),
         name="weight_gradients",
     )(*h, *g, *hids)
-    return list(results[:-1]), results[-1]
+    chips = []
+    for i in range(stay):
+        start = 3 * (stay + i)
+        other = list(results[start : start + 3]) if i < loose else results[3 * stay + 2 * loose + i]
+        chips += [list(results[3 * i : 3 * i + 3]), other]
+    return chips
 
 
 def swap(values, axis, bit):
@@ -624,11 +834,17 @@
     return blocks
 
 
-def ring_sum(blocks, sent=LOW):
-    running = blocks[1 % len(blocks)].astype(FULL)
+def ring_partial(blocks):
+    running = blocks[1]
     for k in range(2, len(blocks) + 1):
-        running = ring(running.astype(sent)).astype(FULL) + blocks[k % len(blocks)].astype(FULL)
+        running = ring(running.astype(LOW))
+        if k < len(blocks):
+            running = running.astype(FULL) + blocks[k].astype(FULL)
     return running
+
+
+def ring_sum(blocks):
+    return ring_partial(blocks).astype(FULL) + blocks[0].astype(FULL)
 
 
 def bits_of(count):
@@ -651,16 +867,6 @@
         for r in range(0, count, 2 * bit):
             blocks[r + bit] = swap(blocks[r], "tensor", bit)
     return blocks
-
-
-def sends_z(values):
-    size = lax.axis_size("expert") // 2
-    place = lax.axis_index("expert") // 2
-    n, m = values.shape
-    cuts = values.reshape(size, n // size, m)
-    return [pick(cuts, place)] + [
-        shift(pick(cuts, (place + k) % size).astype(LOW), k) for k in range(1, size)
-    ]
 
 
 def total_of(parts):
@@ -798,14 +1004,16 @@
     x_own = own_rows(activations)
     core = lambda v: swap(v, "tensor", 1)
     if fine:
-        x_in, gate, up, sent, x_own, column = tie(activations, gate, up, sent, x_own, column)
-        moved = [pair(down), across(down), ring(sent), core(down), core(gate)]
+        sent = tie(sent)[0]
+        moved = [pair(down), across(down), ring(sent), core(down)]
     hidden_first, q, k, v = run_front(
         x_in, gain_first, (query_weight, key_matrix, value_matrix), cosine, sine, heads, groups
     )
     if fine:
-        moved, hidden_first, q, k, v, gate, up = tie(moved, hidden_first, q, k, v, gate, up)
-        down_x, down_y, g_1, down_c, gate_c = moved
+        moved, hidden_first, q, k, v, gate, up, x_own, column = tie(
+            moved, hidden_first, q, k, v, gate, up, x_own, column
+        )
+        down_x, down_y, g_1, down_c = moved
         moved = [pair(gate), across(gate), ring(g_1), core(down_x), core(up)]
     mixture, lse, parts = run_attention(mine, q, k, v, output_weight, column, row, tensor_count)
     if fine:
@@ -814,13 +1022,13 @@
         parts = tie(parts[0], parts[2], core(parts[3]), core(parts[1]))
         to_send = (parts[1] + parts[2].astype(FULL)).astype(LOW)
         attention_out = parts[0] + parts[3].astype(FULL)
-        to_send, attention_out, up, g_2, gate_x, down_y = tie(
-            to_send, attention_out, up, g_2, gate_x, down_y
-        )
-        moved = [across(to_send), pair(up), ring(g_2), core(gate_x), core(down_y)]
-        moved, gate_y = tie(moved, gate_y)
+        to_send, attention_out, up, g_2, gate_x, down_y, gate = tie(
+            to_send, attention_out, up, g_2, gate_x, down_y, gate
+        )
+        moved = [across(to_send), pair(up), ring(g_2), core(gate_x), core(gate)]
+        moved, gate_y, down_y = tie(moved, gate_y, down_y)
         attention_out = attention_out + moved[0].astype(FULL)
-        up_x, g_3, gate_xc, down_yc = moved[1:]
+        up_x, g_3, gate_xc, gate_c = moved[1:]
         g = [sent, g_1, g_2, g_3]
     else:
         attention_out = parts_sum(parts)
@@ -845,29 +1053,15 @@
     low = lambda v: v.astype(LOW)
     full = lambda v: v.astype(FULL)
 
-    def token_gradients(summed_rows):
-        d_hidden_moe = summed_rows[:, :width]
-        d_gates = sum(
-            summed_rows[:, width + n * num_experts : width + (n + 1) * num_experts]
-            for n in range(3)
-        )
-        logits = mul(hidden_second, router_weight)
-        picked = code[:, :num_experts] > 0.5
-        held = code[:, :num_experts] > 1.5
-        gates = jax.nn.softmax(jnp.where(picked, logits, NEGATIVE), axis=-1)
-        d_gates = jnp.where(held, d_gates, 0.0)
-        d_logits = low(gates * (d_gates - jnp.sum(gates * d_gates, axis=-1, keepdims=True)))
-        d_hidden_second = d_hidden_moe + mul(d_logits, router_weight, NT)
-        grad_router = mul(hidden_second, d_logits, TN)
-        grad_gain_second = jnp.sum(d_hidden_second * normed_second, axis=0)
-        scaled = d_hidden_second * gain_second
-        d_mid = full(cotangent_own) + inverse_second * (
-            scaled - normed_second * jnp.mean(scaled * normed_second, axis=-1, keepdims=True)
-        )
-        return d_mid, jnp.concatenate([grad_gain_second[None], grad_router.T])
-
-    back = lambda group, da: run_back(
-        group, mine, da, hidden_first, output_weight, mixture, q, k, v, lse, column, row, cosine, sine
+    def token_gradients(came, own):
+        d_mid, d_a, grad_gain, grad_router = run_token(
+            came, own, hidden_second, router_wide, code, residual_mid, gain_second[None],
+            cotangent_own, num_experts,
+        )
+        return d_mid, d_a, jnp.concatenate([grad_gain, grad_router])
+
+    back = lambda group, da, split=True: run_back(
+        group, split, mine, da, hidden_first, output_weight, mixture, q, k, v, lse, column, row, cosine, sine
     )
     size = heads // groups
     cut = size * HEAD_WIDTH
@@ -883,15 +1077,9 @@
         for i in range(groups)
     ]
 
-    def first_gradients(d_projected):
-        d_first = sum(mul(d, w, NT) for d, w in zip(d_projected, group_weights))
-        inverse = normalized(full(activations))
-        grad_gain = jnp.sum(d_first * (full(activations) * inverse), axis=0)
-        parts = [
-            lax.dynamic_slice_in_dim(d_first, (tensor_index ^ r) * rows, rows, 0)
-            for r in range(tensor_count)
-        ]
-        return [low(p) if r % 2 else p for r, p in enumerate(parts)], grad_gain
+    first_gradients = lambda d_projected: run_first(
+        mine, activations, d_projected, group_weights, tensor_count
+    )
 
     def input_rows(d_first, d_mid):
         values = full(x_own)
@@ -904,34 +1092,34 @@
         )
 
     if fine:
-        hidden_second, up_xc, gate_yc = tie(hidden_second, core(up_x), core(gate_y))
+        h = [hidden_second]
+        moved = [ring(h[0]), across(up), pair(down_y)]
+        up_xc, gate_yc = core(up_x), core(gate_y)
         side = [
             [gate, up, down], [gate_c, up_c, down_c],
             [gate_x, up_x, down_x], [gate_xc, up_xc, down_xc],
         ]
         side_places = [0, 0, 1, 1]
-        h = [hidden_second]
-        moved = [ring(h[0]), across(up), pair(down_y)]
         start = experts(h[:1], g[:1], side, side_places)
-        moved, start = tie(moved, start)
+        moved, start, group_weights, gate_yc = tie(moved, start, group_weights, gate_yc)
         y_0, dh_0, dgb_0, hid_0 = start
         h.append(moved[0])
         up_y, down_far = moved[1:]
 
         moved = [ring(h[1]), across(gate_x), pair(up_y)]
-        up_yc, down_farc = core(up_y), core(down_far)
+        up_yc, down_yc = core(up_y), core(down_y)
         y_1, dh_1, dgb_1, hid_1 = experts(h[1:2], g[1:2], side, side_places)
         beside = [[gate_y, up_y, down_y], [gate_yc, up_yc, down_yc]]
         second = experts(
             h[:2], g[:2], beside, [0, 0], (y_0 + y_1, dh_0 + dh_1, dgb_0 + dgb_1)
         )
-        moved, second, hid_1, down_farc = tie(moved, second, hid_1, down_farc)
+        moved, second, hid_1, down_far = tie(moved, second, hid_1, down_far)
         y_1, dh_1, dgb_1, hid_y = second
         h.append(moved[0])
         gate_far, up_far = moved[1:]
 
         moved = [ring(h[2])]
-        gate_farc, up_farc = core(gate_far), core(up_far)
+        gate_farc, up_farc, down_farc = core(gate_far), core(up_far), core(down_far)
         y_2, dh_2, dgb_2, hid_2 = experts(h[2:3], g[2:3], side + beside, side_places + [0, 0])
         distant = [[gate_far, up_far, down_far], [gate_farc, up_farc, down_farc]]
         third = experts(
@@ -961,140 +1149,121 @@
             else:
                 head = [(4, *place_of(2, s - 6), 0, 3 * rows)]
             plan.append(head + [(5, *place_of(8, s), 3 * rows, rows)])
-        weights_of = lambda which: run_weights(h, g, hids, [plan[s] for s in which], wide)
+        weights_of = lambda which, loose=0: run_weights(
+            h, g, hids, [plan[s] for s in which], wide, loose
+        )
+        take_all = lambda kept, other, start: [
+            (piece, other, (start + i) * wide) for i, piece in enumerate(kept)
+        ]
         running, hids = tie(running, hids)
+        far, far_other, beside_kept, beside_other = weights_of([6, 4, 7, 5], 1)
+        far_other = [core(v) for v in far_other]
         moved = ring(running)
-        ready = weights_of([6, 4, 7, 5])
-        moved, ready = tie(moved, ready)
+        moved, far, far_other, beside_kept, beside_other = tie(
+            moved, far, far_other, beside_kept, beside_other
+        )
 
         (running,) = run_adds([(moved, dh_parts[3])])
-        running, h = tie(running, h)
-        moved, others = ring(running), core(ready[1])
-        later = weights_of([2, 0, 3, 1])
-        moved, later, others = tie(moved, later, others)
-
-        take_all = lambda kept, other, start: run_adds(
-            [(piece, other, (start + i) * wide) for i, piece in enumerate(kept)]
-        )
-        far_sum = take_all(ready[0][:3], others, 0)
-        d_mid, small = token_gradients(full(moved) + full(dh_parts[0]))
-        d_a = low(d_mid)
-        d_a, d_mid, far_sum, y_run, others, later = tie(
-            d_a, d_mid, far_sum, y_parts[1], others, later
-        )
-
-        moved = [across(d_a), pair(far_sum[0]), ring(y_run), core(d_a), core(later[1])]
-        y_sum = take_all(ready[0][3:], others, 3)
-        moved, y_sum = tie(moved, y_sum)
+        running, far, far_other, h = tie(running, far, far_other, h)
+        far = run_adds(list(zip(far, far_other)))
+        moved = [ring(running), pair(far[0]), across(far[1]), core(beside_other)]
+        x_kept, x_other, own_kept, own_other = weights_of([2, 0, 3, 1])
+        moved, x_kept, x_other, own_kept, own_other, beside_kept = tie(
+            moved, x_kept, x_other, own_kept, own_other, beside_kept
+        )
+        running, moved_gate, moved_up, beside_other = moved
+        d_mid, d_a, small = token_gradients(running, dh_parts[0])
+        d_a, d_mid, small, y_run, moved_gate, moved_up, beside_other = tie(
+            d_a, d_mid, small, y_parts[1], moved_gate, moved_up, beside_other
+        )
+
+        moved = [across(d_a), pair(far[2]), ring(y_run), core(d_a), core(x_other)]
+        y_sum = run_adds(take_all(beside_kept, beside_other, 0))
+        (y_sum[0],) = run_adds([(y_sum[0], moved_gate)])
+        x_other = moved.pop()
+        x_sum = run_adds(take_all(x_kept, x_other, 0))
+        moved, y_sum, x_sum = tie(moved, y_sum, x_sum)
+        x_gate, x_up, x_down = x_sum
         da = [d_a, moved[3], moved[0]]
-        later_others = moved[4]
-        da_3, y_sum[0], y_run = tie(
-            core(da[2]), *run_adds([(y_sum[0], moved[1]), (moved[2], y_parts[2])])
+        moved_down, y_run = moved[1], moved[2]
+        own_other, y_run, da_3 = tie(
+            own_other, run_adds([(y_run, y_parts[2])])[0], core(da[2])
         )
         da.append(da_3)
 
-        moved = [across(far_sum[1]), pair(far_sum[2]), ring(y_run)]
+        moved = [across(y_sum[0]), pair(x_gate), ring(y_run), core(own_other)]
         d_one, keep_one, send_one = back(0, da)
-        kept, d_one = tie(later[0], d_one)
-        sums = take_all(kept, later_others, 0)
-        moved, d_one, keep_one, send_one, sums, da = tie(
-            moved, d_one, keep_one, send_one, sums, da
-        )
-        x_sum, own_sum = sums[:3], sums[3:]
-        y_sum[2], x_sum[1], y_run = run_adds(
-            [(y_sum[2], moved[1]), (x_sum[1], moved[0]), (moved[2], y_parts[3])]
-        )
-        y_sum, x_sum, y_run = tie(y_sum, x_sum, y_run)
-
-        moved = [across(y_sum[0]), pair(send_one), ring(y_run)]
+        moved, d_one, keep_one, send_one, da = tie(moved, d_one, keep_one, send_one, da)
+        arrived_y, arrived_x, own_other = [moved[0]], [moved[1]], moved[3]
+        y_down, x_up, y_run = run_adds(
+            [(y_sum[2], moved_down), (x_up, moved_up), (moved[2], y_parts[3])]
+        )
+        y_down, x_up, y_run = tie(y_down, x_up, y_run)
+
+        moved = [across(y_down), pair(send_one), ring(y_run), across(y_sum[1]), pair(x_up)]
         d_two, keep_two, send_two = back(1, da)
-        moved, d_two, keep_two, send_two = tie(moved, d_two, keep_two, send_two)
-        arrived_y, arrived_x = [moved[0]], []
-        summed = moved[2]
         d_parts, grad_gain_first = first_gradients([d_one, d_two])
-        half_one = keep_one + full(moved[1])
-        extra = jnp.pad(
-            jnp.concatenate([small, grad_gain_first[None]]),
-            ((0, EXTRA - 2 - num_experts), (0, 0)),
-        )
-        send_two = jnp.concatenate([send_two, low(extra)])
-        d_parts, half_one, extra, send_two = tie(d_parts, half_one, extra, send_two)
+        moved, d_parts, keep_two, send_two, grad_gain_first = tie(
+            moved, d_parts, keep_two, send_two, grad_gain_first
+        )
+        arrived_y += [moved[0], moved[3]]
+        arrived_x.append(moved[4])
+        summed, from_one = moved[2], moved[1]
+        extra = jnp.concatenate([small, grad_gain_first])
+        send_two = lax.dynamic_update_slice(send_two, low(extra), (keep_two.shape[0], 0))
+        d_parts, send_two, extra = tie(d_parts, send_two, extra)
         d_others = tie(core(d_parts[3]), core(d_parts[1]))
         to_send = low(d_parts[2] + full(d_others[0]))
         d_first = d_parts[0] + full(d_others[1])
-
+        n = keep_two.shape[0]
         place = expert_index // 2
-        bits = [place % 2, place // 2]
-        along = lambda v, bit: swap(v, "expert", 2 << bit)
-
-        def halved(v, bit, more=None):
-            parts = v.reshape(2, v.shape[0] // 2, v.shape[1])
-            goes = low(pick(parts, 1 - bits[bit]))
-            if more is not None:
-                goes = jnp.concatenate([goes, low(more)])
-            return pick(parts, bits[bit]), goes
-
-        def doubled(v, other, bit):
-            front = bits[bit] == 0
-            return jnp.concatenate([jnp.where(front, v, other), jnp.where(front, other, v)])
-
-        def apart(keep, came, more):
-            n = keep.shape[0]
-            return keep + full(came[:n]), more + full(came[n:])
-
-        stay_one, go_one = halved(half_one, 0)
-        to_send, d_first, stay_one, go_one = tie(to_send, d_first, stay_one, go_one)
-
-        moved = tie(across(to_send), pair(send_two), along(go_one, 0))
+
+        def quarters(half):
+            cuts = half.reshape(ring_size, n // ring_size, width)
+            goes = [low(pick(cuts, (place + k) % ring_size)) for k in range(1, ring_size)]
+            return pick(cuts, place), goes
+
+        stay_one, go_one = quarters(keep_one + full(from_one[:n]))
+        to_send, d_first, send_two, stay_one, go_one = tie(
+            to_send, d_first, send_two, stay_one, go_one
+        )
+
+        moved = tie(
+            across(to_send), pair(send_two), [shift(v, k + 1) for k, v in enumerate(go_one)]
+        )
         d_in = input_rows(d_first + full(moved[0]), d_mid)
-        half_two, extra = apart(keep_two, moved[1], extra)
-        stay_one, go_one = halved(stay_one + full(moved[2]), 1)
-        stay_two, go_two = halved(half_two, 0, extra)
-        d_in, stay_one, go_one, stay_two, go_two, extra = tie(
-            d_in, stay_one, go_one, stay_two, go_two, extra
-        )
-        moved = [
-            across(d_in), core(d_in), along(go_one, 1), along(go_two, 0), pair(x_sum[0]),
-        ]
+        stay_two, go_two = quarters(keep_two + full(moved[1][:n]))
+        count = extra.shape[0]
+        extra = extra + full(moved[1][n : n + count])
+        wider = jnp.pad(low(extra), ((0, EXTRA - count), (0, 0)))
+        go_two = [jnp.concatenate([v, wider]) for v in go_two]
+        from_one = moved[2]
+        d_in, go_two, stay_two, extra = tie(d_in, go_two, stay_two, extra)
+
+        moved = [across(d_in), pair(x_down), [shift(v, k + 1) for k, v in enumerate(go_two)]]
         out_own = low(residual_mid + full(summed) + full(y_parts[0]))
-        moved, out_own = tie(moved, out_own)
-        input_blocks = [d_in, moved[1], moved[0]]
-        arrived_x.append(moved[4])
-        one = low(stay_one + full(moved[2]))
-        stay_two, extra = apart(stay_two, moved[3], extra)
-        stay_two, go_two = halved(stay_two, 1, extra)
-        one, stay_two, go_two, extra, input_blocks, arrived_x = tie(
-            one, stay_two, go_two, extra, input_blocks, arrived_x
-        )
-        moved = [
-            along(one, 1), along(go_two, 1), pair(x_sum[1]), across(y_sum[2]),
-            core(input_blocks[2]),
-        ]
-        moved = tie(*moved)
-        arrived_x.append(moved[2])
-        arrived_y.append(moved[3])
-        input_blocks.append(moved[4])
-        one = doubled(one, moved[0], 1)
-        two, extra = apart(stay_two, moved[1], extra)
-        two = low(two)
-        one, two, extra, input_blocks, arrived_x, arrived_y = tie(
-            one, two, extra, input_blocks, arrived_x, arrived_y
-        )
+        own_sum = run_adds(take_all(own_kept, own_other, 0))
+        quarter_one = low(total_of([stay_one] + from_one))
+        moved, out_own, own_sum, quarter_one = tie(moved, out_own, own_sum, quarter_one)
+        arrived_x.append(moved[1])
+        q = stay_two.shape[0]
+        quarter_two = low(total_of([stay_two] + [v[:q] for v in moved[2]]))
+        extra = total_of([extra] + [v[q : q + count] for v in moved[2]])
+        out_more = jnp.concatenate([out_own, jnp.pad(low(extra), ((0, EXTRA - count), (0, 0)))])
+        input_blocks = [d_in, core(d_in), moved[0], core(moved[0])]
+        input_blocks, quarter_one, quarter_two, extra, out_more, arrived_x = tie(
+            input_blocks, quarter_one, quarter_two, extra, out_more, arrived_x
+        )
+
+        moved = [across(out_more), core(out_more)]
+        from_one = [shift(quarter_one, k) for k in range(1, ring_size)]
         input_gradient = run_place(mine, input_blocks, FULL)
-        moved = tie(
-            along(one, 0), along(two, 1), pair(x_sum[2]), across(y_sum[1]), core(extra),
-            input_gradient,
-        )
-        input_gradient = moved[5]
-        arrived_x.append(moved[2])
-        arrived_y.append(moved[3])
-        one = doubled(one, moved[0], 0)
-        two = doubled(two, moved[1], 1)
-        extra = extra + moved[4]
-        out_more = jnp.concatenate([out_own, low(extra)])
-        one, two, extra, out_more, out_own, arrived_x, arrived_y = tie(
-            one, two, extra, out_more, out_own, arrived_x, arrived_y
-        )
+        moved, from_one, input_gradient = tie(moved, from_one, input_gradient)
+        one = laid_z([quarter_one] + from_one)
+        one, quarter_two, arrived_x, arrived_y = tie(one, quarter_two, arrived_x, arrived_y)
+
+        from_two = [shift(quarter_two, k) for k in range(1, ring_size)]
+        one_other, out_3 = pair(one), core(moved[0])
         grads = [
             total_of([own_sum[0], arrived_y[0], arrived_x[0]]),
             total_of([own_sum[1], arrived_y[2], arrived_x[1]]),
@@ -1102,16 +1271,17 @@
         ]
         unturned = lambda v: v.reshape(local, hidden, width).transpose(0, 2, 1)
         grad_gate, grad_up, grad_down = unturned(grads[0]), unturned(grads[1]), grads[2]
-        moved = tie(pair(one), along(two, 0), across(out_more), core(out_own), grad_gate, grad_up)
-        grad_gate, grad_up = moved[4:]
-        two = doubled(two, moved[1], 0)
-        out_2 = moved[2][:rows]
-        sums = extra + full(moved[2][rows:])
-        sums = sums[: 2 + num_experts]
-        two, out_2 = tie(two, out_2)
-        whole_one = joined(one, moved[0])
-        output_blocks = [out_own, moved[3], out_2, core(out_2)]
-        wholes = [whole_one, joined(two, pair(two))]
+        from_two, one_other, out_3, grad_gate, grad_up, grad_down = tie(
+            from_two, one_other, out_3, grad_gate, grad_up, grad_down
+        )
+        two = laid_z([quarter_two] + from_two)
+
+        output = run_place(mine, [out_own, moved[1], moved[0], out_3], LOW)
+        sums = total_of(
+            [extra] + [v[rows : rows + count] for v in (moved[1], moved[0], out_3)]
+        )
+        two_other, output, sums = tie(pair(two), output, sums)
+        finished = run_finish(mine, None, size, [(one, one_other), (two, two_other)])
     else:
         g = spread(sent)
         h = ring_gather(hidden_second)
@@ -1130,40 +1300,41 @@
             hids.append(hid)
         grad_parts = []
         for i in range(0, len(weights), 4):
-            kept, other = run_weights(
+            chips = run_weights(
                 h, g, hids, [plan[i], plan[i + 2], plan[i + 1], plan[i + 3]], wide
             )
-            other = core(other)
-            sums = run_adds([(piece, other, j * wide) for j, piece in enumerate(kept)])
-            grad_parts += [sums[:3], sums[3:]]
+            for kept, other in ((chips[0], core(chips[1])), (chips[2], core(chips[3]))):
+                grad_parts.append(
+                    run_adds([(piece, other, j * wide) for j, piece in enumerate(kept)])
+                )
         grad_gate, grad_up, grad_down = scatter_weights(grad_parts)
         unturned = lambda v: v.reshape(local, hidden, width).transpose(0, 2, 1)
         grad_gate, grad_up = unturned(grad_gate), unturned(grad_up)
-        d_mid, small = token_gradients(ring_sum(dh_parts))
-        da = tensor_blocks(low(d_mid))
-        backs = [back(i, da) for i in range(groups)]
-        d_parts, grad_gain_first = first_gradients([d for d, _, _ in backs])
+        running = low(full(ring_partial(dh_parts)))
+        d_mid, d_a, small = token_gradients(running, dh_parts[0])
+        da = tensor_blocks(d_a)
+        backs = [back(i, da, False) for i in range(groups)]
+        d_parts, grad_gain_first = first_gradients([d for d, _ in backs])
         d_first = parts_sum(d_parts)
         input_blocks = tensor_blocks(input_rows(d_first, d_mid))
         input_gradient = run_place(mine, input_blocks, FULL)
-        output_blocks = tensor_blocks(low(residual_mid + ring_sum(y_parts)))
-        wholes = []
-        for _, keep, send in backs:
-            half = keep + full(pair(send))
-            half = laid_z(spread(low(total_of(sends_z(half)))))
-            wholes.append(joined(half, pair(half)))
-        sums = sum_everywhere(jnp.concatenate([small, grad_gain_first[None]]))
-
-    span = cut + 2 * HEAD_WIDTH
-    turned = lambda a, b: full(jnp.concatenate([w[a:b] for w in wholes])).T
+        output = run_place(
+            mine, tensor_blocks(low(residual_mid + ring_sum(y_parts))), LOW
+        )
+        finished = run_finish(
+            mine, [lax.psum(square, "expert") for _, square in backs], size
+        )
+        sums = sum_everywhere(jnp.concatenate([small, grad_gain_first]))
+
+    grad_query, grad_key, grad_value, grad_output = finished
     return (
-        run_place(mine, output_blocks, LOW),
+        output,
         input_gradient,
         sums[-1],
-        turned(0, cut),
-        turned(cut, cut + HEAD_WIDTH),
-        turned(cut + HEAD_WIDTH, span),
-        full(jnp.concatenate([w[span:] for w in wholes])),
+        grad_query,
+        grad_key,
+        grad_value,
+        grad_output,
         sums[0],
         sums[1:-1].T,
         grad_gate,

time: 563 us -> 501 us (0.89)
  local copies, waits for them, and re-layouts: 104 us -> 51.1 us
  waiting for transfers between devices: 133 us -> 88.6 us
  Pallas kernels: 203 us -> 244 us
  starting transfers between devices: 58.9 us -> 75.3 us
  other arithmetic: 45.3 us -> 29.1 us
  matrix products: 5.68 us -> 0 us
    ppermute x60 -> x55, waiting for transfers between devices: 121 us -> 54.2 us  [swap(): return lax.ppermute(values, axis, [(i, i ^ bit) for i in range(count)])]
    unnamed x330 -> x157, local copies, waits for them, and re-layouts: 76.2 us -> 18.7 us
    ppermute x0 -> x12, starting transfers between devices: none -> 29.3 us  [shift(): lax.ppermute(block, 'expert', [(i, (i + 2 * steps) % count) for i in rang...]
    ppermute x0 -> x12, waiting for transfers between devices: none -> 23.6 us  [shift(): lax.ppermute(block, 'expert', [(i, (i + 2 * steps) % count) for i in rang...]
    pallas_call x0 -> x3, Pallas kernels: none -> 22.3 us  [the longest x1 9.83 us: run_first(): pl.pallas_call(lambda m, *refs: first_body(groups, count, *refs), grid_sp...]
    pallas_call x7 -> x9, Pallas kernels: 8.94 us -> 26.7 us  [run_adds(): pl.pallas_call(functools.partial(add_body, count), grid=(rows // tile,),...]
    ppermute x60 -> x55, starting transfers between devices: 45.3 us -> 31.6 us  [swap(): return lax.ppermute(values, axis, [(i, i ^ bit) for i in range(count)])]
    dynamic_update_slice x0 -> x9, local copies, waits for them, and re-layouts: none -> 8.18 us  [the longest x8 6.57 us: laid_z(): whole = lax.dynamic_update_index_in_dim(whole, block, (place - k) % size, 0)]
  transfers between devices with their start and end apart: 72 -> 79, of which waited for: 24 -> 28; matrix products, arithmetic and copies ran while one was open for 11% -> 9% of each run, Pallas kernels for 35% -> 48%
where the time goes in v3:
time: 501 us; the launch traced here: 491 us
  Pallas kernels  244 us (49%)
  waiting for transfers between devices  88.6 us (18%)
  starting transfers between devices  75.3 us (15%)
  local copies, waits for them, and re-layouts  51.1 us (10%)
  other arithmetic  29.1 us (6%)
    pallas_call x6, Pallas kernels, run_experts(): pl.pallas_call(functools.partial(expert_body, tuple(places), blocks, loca...  89.2 us
    ppermute x55, waiting for transfers between devices, swap(): return lax.ppermute(values, axis, [(i, i ^ bit) for i in range(count)])  54.2 us
    pallas_call x2, Pallas kernels, run_back(): pl.pallas_call(functools.partial(back_body, count, group, size, rows, min...  43.6 us
    ppermute x55, starting transfers between devices, swap(): return lax.ppermute(values, axis, [(i, i ^ bit) for i in range(count)])  31.6 us
    pallas_call x2, Pallas kernels, run_weights(): pl.pallas_call(functools.partial(weight_body, plan, rows, wide), out_shap...  30.1 us
    ppermute x12, starting transfers between devices, shift(): lax.ppermute(block, 'expert', [(i, (i + 2 * steps) % count) for i in rang...  29.3 us
    pallas_call x9, Pallas kernels, run_adds(): pl.pallas_call(functools.partial(add_body, count), grid=(rows // tile,),...  26.7 us
    ppermute x12, waiting for transfers between devices, shift(): lax.ppermute(block, 'expert', [(i, (i + 2 * steps) % count) for i in rang...  23.6 us
  transfers between devices with their start and end apart: 79, of which 28 were waited for; matrix products, arithmetic and copies ran while one was open for 9% of the time, Pallas kernels for 48%

profile of v3, /device:TPU:0, one launch (start us, length us, event | category | flops | bytes accessed | tf_op | source)
XLA Modules:
  0.0 490.6 jit_solution(8680160232931601388)
XLA Ops:
  15.9 8.7 %front.1 = (bf16[1024,1536]{1,0:T(8,128)(2,1)}, bf16[6,1024,64]{2,1,0:T(8,128)(2,1)}, bf16[2,1024,64]{2,1,0:T(8,128)(2,1)}, bf16[2,1024,64]{2,1,0:T(8,128)(2,1)}) custom-call(bf16[1024,1536]{1,0:T(8,128)(2,1)} %refs_0_.1, f32[1,1536]{1,0:T(1,128)} %broadcast_in_dim.140.gain_ref, bf16[1536,384]{1,0:T(8,128)(2,1)} %wq_ref.1, bf16[1536,128]{1,0:T(8,128)(2,1)} %wk_ref.1, ...), custom_call_target="tpu_custom_call" | custom-call | flops 301989888 | bytes 294912 | tf_op jit(solution)/shard_map/front/pallas_call | solution.py:98
  34.2 17.1 %attention.1 = (bf16[1024,384]{1,0:T(8,128)(2,1)}, f32[6,1,1024]{2,1,0:T(1,128)}, f32[256,1536]{1,0:T(8,128)}, bf16[256,1536]{1,0:T(8,128)(2,1)}, f32[256,1536]{1,0:T(8,128)}, /*index=5*/bf16[256,1536]{1,0:T(8,128)(2,1)}) custom-call(s32[2]{0:T(128)} %pad_add_fusion.mine_ref.m, bf16[6,1024,64]{2,1,0:T(8,128)(2,1)} %get-tuple-element.354.q_ref.rest_7_, ...), custom_call_target="tpu_custom_call" | custom-call | flops 452984832 | bytes 294912 | tf_op jit(solution)/shard_map/attention/pallas_call | solution.py:183
  55.1 3.7 convert_add_fusion.7
  69.7 10.7 %collective-permute-done.11 = bf16[256,1536]{1,0:T(8,128)(2,1)} collective-permute-done((bf16[256,1536]{1,0:T(8,128)(2,1)}, bf16[256,1536]{1,0:T(8,128)(2,1)}, u32[]{:S(2)}, u32[]{:S(2)}) %collective-permute-start.11) | collective-permute-done | bytes 786464 | tf_op jit(solution)/shard_map/ppermute | solution.py:814
  89.9 12.5 %experts.6 = (bf16[256,1536]{1,0:T(8,128)(2,1)}, bf16[256,1664]{1,0:T(8,128)(2,1)}, f32[256,128]{1,0:T(8,128)}, bf16[256,3072]{1,0:T(8,128)(2,1)}) custom-call(s32[4]{0:T(128)} %pad_add_fusion.1.columns_ref, bf16[1536,128]{1,0:T(8,128)(2,1)} %pad.11.router_ref, bf16[256,1536]{1,0:T(8,128)(2,1)} %copy-done.9, bf16[256,1664]{1,0:T(8,128)(2,1)} %copy-done.10, ...), custom_call_target="tpu_custom_call" | custom-call | flops 75497472 | bytes 147456 | tf_op jit(solution)/shard_map/experts/pallas_call | solution.py:657
  102.3 3.9 collective-permute-done.16.rest_0_.rest_1_
  110.8 12.5 %experts.7 = (bf16[256,1536]{1,0:T(8,128)(2,1)}, bf16[256,1664]{1,0:T(8,128)(2,1)}, f32[256,128]{1,0:T(8,128)}, bf16[256,3072]{1,0:T(8,128)(2,1)}) custom-call(s32[4]{0:T(128)} %pad_add_fusion.1.columns_ref, bf16[1536,128]{1,0:T(8,128)(2,1)} %pad.11.router_ref, bf16[256,1536]{1,0:T(8,128)(2,1)} %copy-done.17, bf16[256,1664]{1,0:T(8,128)(2,1)} %copy-done.13, ...), custom_call_target="tpu_custom_call" | custom-call | flops 75497472 | bytes 147456 | tf_op jit(solution)/shard_map/experts/pallas_call | solution.py:657
  124.5 12.3 %experts.8 = (bf16[256,1536]{1,0:T(8,128)(2,1)}, bf16[256,1536]{1,0:T(8,128)(2,1)}, bf16[256,1664]{1,0:T(8,128)(2,1)}, bf16[256,1664]{1,0:T(8,128)(2,1)}, f32[25...) custom-call(s32[4]{0:T(128)} %pad_add_fusion.1.columns_ref, bf16[1536,128]{1,0:T(8,128)(2,1)} %pad.11.router_ref, ...), custom_call_target="tpu_custom_call" | custom-call | flops 75497472 | bytes 73728 | tf_op jit(solution)/shard_map/experts/pallas_call | solution.py:657
  138.8 16.0 %experts.9 = (bf16[256,1536]{1,0:T(8,128)(2,1)}, bf16[256,1664]{1,0:T(8,128)(2,1)}, f32[256,128]{1,0:T(8,128)}, bf16[256,4608]{1,0:T(8,128)(2,1)}) custom-call(s32[4]{0:T(128)} %pad_add_fusion.1.columns_ref, bf16[1536,128]{1,0:T(8,128)(2,1)} %pad.11.router_ref, bf16[256,1536]{1,0:T(8,128)(2,1)} %copy-done.20, bf16[256,1664]{1,0:T(8,128)(2,1)} %copy-done.19, ...), custom_call_target="tpu_custom_call" | custom-call | flops 113246208 | bytes 221184 | tf_op jit(solution)/shard_map/experts/pallas_call | solution.py:657
  156.2 16.4 %experts.10 = (bf16[256,1536]{1,0:T(8,128)(2,1)}, bf16[256,1536]{1,0:T(8,128)(2,1)}, bf16[256,1536]{1,0:T(8,128)(2,1)}, bf16[256,1664]{1,0:T(8,128)(2,1)}, bf16[...) custom-call(s32[4]{0:T(128)} %pad_add_fusion.1.columns_ref, ...), custom_call_target="tpu_custom_call" | custom-call | flops 113246208 | bytes 73728 | tf_op jit(solution)/shard_map/experts/pallas_call | solution.py:657
  174.5 19.6 %experts.11 = (bf16[256,1536]{1,0:T(8,128)(2,1)}, bf16[256,1664]{1,0:T(8,128)(2,1)}, f32[256,128]{1,0:T(8,128)}, bf16[256,6144]{1,0:T(8,128)(2,1)}) custom-call(s32[4]{0:T(128)} %pad_add_fusion.1.columns_ref, bf16[1536,128]{1,0:T(8,128)(2,1)} %pad.11.router_ref, bf16[256,1536]{1,0:T(8,128)(2,1)} %copy-done.28, ...), custom_call_target="tpu_custom_call" | custom-call | flops 150994944 | bytes 294912 | tf_op jit(solution)/shard_map/experts/pallas_call | solution.py:657
  199.5 15.0 %weight_gradients.2 = (bf16[256,1536]{1,0:T(8,128)(2,1)}, bf16[256,1536]{1,0:T(8,128)(2,1)}, bf16[256,1536]{1,0:T(8,128)(2,1)}, bf16[256,1536]{1,0:T(8,128)(2,1)...) custom-call(bf16[256,1536]{1,0:T(8,128)(2,1)} %copy-done.9, ...), custom_call_target="tpu_custom_call" | custom-call | flops 150994944 | bytes 98304 | tf_op jit(solution)/shard_map/weight_gradients/pallas_call | solution.py:783
  225.1 3.6 adds.11
  230.0 15.1 %weight_gradients.3 = (bf16[256,1536]{1,0:T(8,128)(2,1)}, bf16[256,1536]{1,0:T(8,128)(2,1)}, bf16[256,1536]{1,0:T(8,128)(2,1)}, bf16[256,1536]{1,0:T(8,128)(2,1)...) custom-call(bf16[256,1536]{1,0:T(8,128)(2,1)} %copy-done.9, ...), custom_call_target="tpu_custom_call" | custom-call | flops 150994944 | bytes 98304 | tf_op jit(solution)/shard_map/weight_gradients/pallas_call | solution.py:783
  251.6 5.6 %token_gradients.1 = (f32[256,1536]{1,0:T(8,128)}, bf16[256,1536]{1,0:T(8,128)(2,1)}, f32[1,1536]{1,0:T(1,128)}, f32[16,1536]{1,0:T(8,128)}) custom-call(bf16[256,1664]{1,0:T(8,128)(2,1)} %copy-done.54, bf16[256,1664]{1,0:T(8,128)(2,1)} %get-tuple-element.507.own_ref, bf16[256,1536]{1,0:T(8,128)(2,1)} %copy-done.9, bf16[1536,128]{1,0:T(8,128)(2,1)} %pad.11.router_ref, ...), custom_call_target="tpu_custom_call" | custom-call | flops 15 | bytes 15 | tf_op jit(solution)/shard_map/token_gradients/pallas_call | solution.py:419
  258.9 3.5 adds.12
  266.0 3.5 adds.14
  270.0 7.5 %collective-permute-done.39.rest_2_ = bf16[256,1536]{1,0:T(8,128)(2,1)S(1)} collective-permute-done((bf16[256,1536]{1,0:T(8,128)(2,1)}, bf16[256,1536]{1,0:T(8,128)(2,1)S(1)}, u32[]{:S(2)}, u32[]{:S(2)}) %collective-permute-start.39) | collective-permute-done | bytes 786464 | tf_op jit(solution)/shard_map/ppermute | solution.py:814
  285.3 21.8 %back.2 = (bf16[1024,320]{1,0:T(8,128)(2,1)}, f32[256,1536]{1,0:T(8,128)}, bf16[288,1536]{1,0:T(8,128)(2,1)}) custom-call(s32[2]{0:T(128)} %pad_add_fusion.mine_ref.m, bf16[256,1536]{1,0:T(8,128)(2,1)} %get-tuple-element.563.rest_0_, bf16[256,1536]{1,0:T(8,128)(2,1)} %copy-done.42, bf16[256,1536]{1,0:T(8,128)(2,1)} %copy-done.41, ...), custom_call_target="tpu_custom_call" | custom-call | flops 301989888 | bytes 294912 | tf_op jit(solution)/shard_map/back/pallas_call | solution.py:288
  309.3 3.5 adds.16
  316.3 21.8 %back.3 = (bf16[1024,320]{1,0:T(8,128)(2,1)}, f32[256,1536]{1,0:T(8,128)}, bf16[288,1536]{1,0:T(8,128)(2,1)}) custom-call(s32[2]{0:T(128)} %pad_add_fusion.mine_ref.m, bf16[256,1536]{1,0:T(8,128)(2,1)} %get-tuple-element.563.rest_0_, bf16[256,1536]{1,0:T(8,128)(2,1)} %copy-done.42, bf16[256,1536]{1,0:T(8,128)(2,1)} %copy-done.41, ...), custom_call_target="tpu_custom_call" | custom-call | flops 301989888 | bytes 294912 | tf_op jit(solution)/shard_map/back/pallas_call | solution.py:288
  338.2 9.8 %first_gradients.1 = (f32[256,1536]{1,0:T(8,128)}, bf16[256,1536]{1,0:T(8,128)(2,1)}, f32[256,1536]{1,0:T(8,128)}, bf16[256,1536]{1,0:T(8,128)(2,1)}, f32[1,1536]{1,0:T(1,128)}) custom-call(s32[2]{0:T(128)} %pad_add_fusion.mine_ref.m, bf16[1024,1536]{1,0:T(8,128)(2,1)} %refs_0_.1, bf16[1024,320]{1,0:T(8,128)(2,1)} %get-tuple-element.562.refs_1_, ...), custom_call_target="tpu_custom_call" | custom-call | flops 15 | bytes 15 | tf_op jit(solution)/shard_map/first_gradients/pallas_call | solution.py:360
  363.2 3.7 adds.17
  367.8 6.3 %collective-permute-done.59 = bf16[64,1536]{1,0:T(8,128)(2,1)} collective-permute-done((bf16[64,1536]{1,0:T(8,128)(2,1)}, bf16[64,1536]{1,0:T(8,128)(2,1)}, u32[]{:S(2)}, u32[]{:S(2)}) %collective-permute-start.59) | collective-permute-done | bytes 196640 | tf_op jit(solution)/shard_map/ppermute | solution.py:899
  395.7 9.8 %collective-permute-done.65 = bf16[96,1536]{1,0:T(8,128)(2,1)S(1)} collective-permute-done((bf16[96,1536]{1,0:T(8,128)(2,1)S(1)}, bf16[96,1536]{1,0:T(8,128)(2,1)S(1)}, u32[]{:S(2)}, u32[]{:S(2)}) %collective-permute-start.65) | collective-permute-done | bytes 294944 | tf_op jit(solution)/shard_map/ppermute | solution.py:899
  410.1 6.8 %collective-permute-start.70 = (bf16[64,1536]{1,0:T(8,128)(2,1)}, bf16[64,1536]{1,0:T(8,128)(2,1)S(1)}, u32[]{:S(2)}, u32[]{:S(2)}) collective-permute-start(bf16[64,1536]{1,0:T(8,128)(2,1)} %add_convert_fusion.4), channel_id=1, source_target_pairs={{0,8},{4,12},{8,16},{12,20},{16,24},{20,28},{24,0},{28,4},{1,9},{5... | collective-permute-start | bytes 589832 | tf_op jit(solution)/shard_map/ppermute | solution.py:899
  424.1 3.7 place.2
  427.7 5.1 %collective-permute-done.71 = bf16[64,1536]{1,0:T(8,128)(2,1)S(1)} collective-permute-done((bf16[64,1536]{1,0:T(8,128)(2,1)}, bf16[64,1536]{1,0:T(8,128)(2,1)S(1)}, u32[]{:S(2)}, u32[]{:S(2)}) %collective-permute-start.71) | collective-permute-done | bytes 196640 | tf_op jit(solution)/shard_map/ppermute | solution.py:899
  434.9 5.3 %collective-permute-start.73 = (bf16[64,1536]{1,0:T(8,128)(2,1)S(1)}, bf16[64,1536]{1,0:T(8,128)(2,1)}, u32[]{:S(2)}, u32[]{:S(2)}) collective-permute-start(bf16[64,1536]{1,0:T(8,128)(2,1)S(1)} %add_convert_fusion.3), channel_id=1, source_target_pairs={{0,8},{4,12},{8,16},{12,20},{16,24},{20,28},{24,0},{28,4},{1,9},{5... | collective-permute-start | bytes 589832 | tf_op jit(solution)/shard_map/ppermute | solution.py:899
  457.0 4.4 collective-permute-done.76.refs_1_
  469.8 12.2 %collective-permute-done.78.refs_3_ = bf16[256,1536]{1,0:T(8,128)(2,1)S(1)} collective-permute-done((bf16[256,1536]{1,0:T(8,128)(2,1)S(1)}, bf16[256,1536]{1,0:T(8,128)(2,1)S(1)}, u32[]{:S(2)}, u32[]{:S(2)}) %collective-permute-start.78) | collective-permute-done | bytes 786464 | tf_op jit(solution)/shard_map/ppermute | solution.py:814
  483.3 6.8 %finish.1 = (f32[1536,384]{1,0:T(8,128)}, f32[1536,128]{1,0:T(8,128)}, f32[1536,128]{1,0:T(8,128)}, f32[384,1536]{1,0:T(8,128)}) custom-call(s32[2]{0:T(128)} %pad_add_fusion.mine_ref.m, bf16[256,1536]{1,0:T(8,128)(2,1)} %bitcast.38.refs_0_, bf16[256,1536]{1,0:T(8,128)(2,1)} %collective-permute-done.76.refs_1_, bf16[256,1536]{1,0:T(8,128)(2,1)} %bitcast.81, ...), custom_call_target="tpu_custom_call" | custom-call | flops 15 | bytes 15 | tf_op jit(solution)/shard_map/finish/pallas_call | solution.py:467
  (375 shorter events, 180.2 us)
Async XLA Ops:
  5.2 24.0 %collective-permute-start.2 = (bf16[256,1664]{1,0:T(8,128)(2,1)S(1)}, bf16[256,1664]{1,0:T(8,128)(2,1)S(1)}, u32[]{:S(2)}, u32[]{:S(2)}) collective-permute-start(bf16[256,1664]{1,0:T(8,128)(2,1)S(1)} %pad_maximum_fusion.2.rest_1_.rest_2_.rest_3_.rest_4_), channel_id=1, source_target_pairs={{0,8},{4,12},{8,16},{12,20},{16,24},{20,28},{24,0},{28,4},{1,9},{5... | collective-permute-start | bytes 2555912 | tf_op jit(solution)/shard_map/ppermute | solution.py:823
  29.3 22.0 %collective-permute-start.6 = (bf16[256,1664]{1,0:T(8,128)(2,1)S(1)}, bf16[256,1664]{1,0:T(8,128)(2,1)S(1)}, u32[]{:S(2)}, u32[]{:S(2)}) collective-permute-start(bf16[256,1664]{1,0:T(8,128)(2,1)S(1)} %collective-permute-done.2.rest_1_.rest_3_.rest_4_.rest_5_), channel_id=1, source_target_pairs={{0,8},{4,12},{8,16},{12,20},{16,24},{20,28},{24,0},{28,4},{1,9},{5... | collective-permute-start | bytes 2555912 | tf_op jit(solution)/shard_map/ppermute | solution.py:823
  30.5 20.8 %collective-permute-start.4 = (bf16[256,1536]{1,0:T(8,128)(2,1)S(1)}, bf16[256,1536]{1,0:T(8,128)(2,1)}, u32[]{:S(2)}, u32[]{:S(2)}) collective-permute-start(bf16[256,1536]{1,0:T(8,128)(2,1)S(1)} %bitcast.67), channel_id=1, source_target_pairs={{0,4},{4,0},{8,12},{12,8},{16,20},{20,16},{24,28},{28,24},{1,5},{5... | collective-permute-start | bytes 2359304 | tf_op jit(solution)/shard_map/ppermute | solution.py:814
  58.9 23.3 %collective-permute-start.13 = (bf16[256,1664]{1,0:T(8,128)(2,1)S(1)}, bf16[256,1664]{1,0:T(8,128)(2,1)}, u32[]{:S(2)}, u32[]{:S(2)}) collective-permute-start(bf16[256,1664]{1,0:T(8,128)(2,1)S(1)} %collective-permute-done.6.rest_1_.rest_5_.rest_6_), channel_id=1, source_target_pairs={{0,8},{4,12},{8,16},{12,20},{16,24},{20,28},{24,0},{28,4},{1,9},{5... | collective-permute-start | bytes 2555912 | tf_op jit(solution)/shard_map/ppermute | solution.py:823
  80.4 21.9 %collective-permute-start.17 = (bf16[256,1536]{1,0:T(8,128)(2,1)}, bf16[256,1536]{1,0:T(8,128)(2,1)}, u32[]{:S(2)}, u32[]{:S(2)}) collective-permute-start(bf16[256,1536]{1,0:T(8,128)(2,1)} %bitcast.20.rest_3_), channel_id=1, source_target_pairs={{0,2},{1,3},{2,0},{3,1},{4,6},{5,7},{6,4},{7,5},{8,10},{9,11},{10,... | collective-permute-start | bytes 2359304 | tf_op jit(solution)/shard_map/ppermute | solution.py:814
  84.3 22.0 %collective-permute-start.16 = (bf16[256,1536]{1,0:T(8,128)(2,1)S(1)}, bf16[256,1536]{1,0:T(8,128)(2,1)S(1)}, u32[]{:S(2)}, u32[]{:S(2)}) collective-permute-start(bf16[256,1536]{1,0:T(8,128)(2,1)S(1)} %multiply_convert_fusion.rest_0_.h_ref), channel_id=1, source_target_pairs={{0,8},{4,12},{8,16},{12,20},{16,24},{20,28},{24,0},{28,4},{1,9},{5... | collective-permute-start | bytes 2359304 | tf_op jit(solution)/shard_map/ppermute | solution.py:823
  89.0 34.3 %collective-permute-start.25 = (bf16[256,1536]{1,0:T(8,128)(2,1)}, bf16[256,1536]{1,0:T(8,128)(2,1)S(1)}, u32[]{:S(2)}, u32[]{:S(2)}) collective-permute-start(bf16[256,1536]{1,0:T(8,128)(2,1)} %collective-permute-done.1.rest_6_.rest_16_), channel_id=1, source_target_pairs={{0,1},{1,0},{2,3},{3,2},{4,5},{5,4},{6,7},{7,6},{8,9},{9,8},{10,11... | collective-permute-start | bytes 2359304 | tf_op jit(solution)/shard_map/ppermute | solution.py:814
  107.2 29.6 %collective-permute-start.22 = (bf16[256,1536]{1,0:T(8,128)(2,1)}, bf16[256,1536]{1,0:T(8,128)(2,1)S(1)}, u32[]{:S(2)}, u32[]{:S(2)}) collective-permute-start(bf16[256,1536]{1,0:T(8,128)(2,1)} %collective-permute-done.4.rest_8_), channel_id=1, source_target_pairs={{0,2},{1,3},{2,0},{3,1},{4,6},{5,7},{6,4},{7,5},{8,10},{9,11},{10,... | collective-permute-start | bytes 2359304 | tf_op jit(solution)/shard_map/ppermute | solution.py:814
  108.6 28.2 %collective-permute-start.21 = (bf16[256,1536]{1,0:T(8,128)(2,1)S(1)}, bf16[256,1536]{1,0:T(8,128)(2,1)S(1)}, u32[]{:S(2)}, u32[]{:S(2)}) collective-permute-start(bf16[256,1536]{1,0:T(8,128)(2,1)S(1)} %collective-permute-done.16.rest_0_.rest_1_), channel_id=1, source_target_pairs={{0,8},{4,12},{8,16},{12,20},{16,24},{20,28},{24,0},{28,4},{1,9},{5... | collective-permute-start | bytes 2359304 | tf_op jit(solution)/shard_map/ppermute | solution.py:823
  110.3 26.5 %collective-permute-start.23 = (bf16[256,1536]{1,0:T(8,128)(2,1)}, bf16[256,1536]{1,0:T(8,128)(2,1)S(1)}, u32[]{:S(2)}, u32[]{:S(2)}) collective-permute-start(bf16[256,1536]{1,0:T(8,128)(2,1)} %collective-permute-done.17.rest_5_.rest_15_), channel_id=1, source_target_pairs={{0,4},{4,0},{8,12},{12,8},{16,20},{20,16},{24,28},{28,24},{1,5},{5... | collective-permute-start | bytes 2359304 | tf_op jit(solution)/shard_map/ppermute | solution.py:814
  137.5 35.1 %collective-permute-start.26 = (bf16[256,1536]{1,0:T(8,128)(2,1)S(1)}, bf16[256,1536]{1,0:T(8,128)(2,1)S(1)}, u32[]{:S(2)}, u32[]{:S(2)}) collective-permute-start(bf16[256,1536]{1,0:T(8,128)(2,1)S(1)} %collective-permute-done.21.rest_0_.rest_2_), channel_id=1, source_target_pairs={{0,8},{4,12},{8,16},{12,20},{16,24},{20,28},{24,0},{28,4},{1,9},{5... | collective-permute-start | bytes 2359304 | tf_op jit(solution)/shard_map/ppermute | solution.py:823
  172.6 23.3 %collective-permute-start.30 = (bf16[256,1664]{1,0:T(8,128)(2,1)}, bf16[256,1664]{1,0:T(8,128)(2,1)S(1)}, u32[]{:S(2)}, u32[]{:S(2)}) collective-permute-start(bf16[256,1664]{1,0:T(8,128)(2,1)} %get-tuple-element.436), channel_id=1, source_target_pairs={{0,8},{4,12},{8,16},{12,20},{16,24},{20,28},{24,0},{28,4},{1,9},{5... | collective-permute-start | bytes 2555912 | tf_op jit(solution)/shard_map/ppermute | solution.py:823
  199.1 22.6 %collective-permute-start.31 = (bf16[256,1664]{1,0:T(8,128)(2,1)}, bf16[256,1664]{1,0:T(8,128)(2,1)S(1)}, u32[]{:S(2)}, u32[]{:S(2)}) collective-permute-start(bf16[256,1664]{1,0:T(8,128)(2,1)} %adds.9), channel_id=1, source_target_pairs={{0,8},{4,12},{8,16},{12,20},{16,24},{20,28},{24,0},{28,4},{1,9},{5... | collective-permute-start | bytes 2555912 | tf_op jit(solution)/shard_map/ppermute | solution.py:823
  221.7 26.6 %collective-permute-start.38 = (bf16[768,1536]{1,0:T(8,128)(2,1)}, bf16[768,1536]{1,0:T(8,128)(2,1)S(1)}, u32[]{:S(2)}, u32[]{:S(2)}) collective-permute-start(bf16[768,1536]{1,0:T(8,128)(2,1)} %get-tuple-element.490), channel_id=1, source_target_pairs={{0,1},{1,0},{2,3},{3,2},{4,5},{5,4},{6,7},{7,6},{8,9},{9,8},{10,11... | collective-permute-start | bytes 7077896 | tf_op jit(solution)/shard_map/ppermute | solution.py:814
  224.9 23.4 %collective-permute-start.35 = (bf16[256,1664]{1,0:T(8,128)(2,1)}, bf16[256,1664]{1,0:T(8,128)(2,1)S(1)}, u32[]{:S(2)}, u32[]{:S(2)}) collective-permute-start(bf16[256,1664]{1,0:T(8,128)(2,1)} %adds.10), channel_id=1, source_target_pairs={{0,8},{4,12},{8,16},{12,20},{16,24},{20,28},{24,0},{28,4},{1,9},{5... | collective-permute-start | bytes 2555912 | tf_op jit(solution)/shard_map/ppermute | solution.py:823
  258.9 21.0 %collective-permute-start.41 = (bf16[256,1536]{1,0:T(8,128)(2,1)}, bf16[256,1536]{1,0:T(8,128)(2,1)S(1)}, u32[]{:S(2)}, u32[]{:S(2)}) collective-permute-start(bf16[256,1536]{1,0:T(8,128)(2,1)} %get-tuple-element.519), channel_id=1, source_target_pairs={{0,8},{4,12},{8,16},{12,20},{16,24},{20,28},{24,0},{28,4},{1,9},{5... | collective-permute-start | bytes 2359304 | tf_op jit(solution)/shard_map/ppermute | solution.py:823
  258.9 21.0 %collective-permute-start.42 = (bf16[256,1536]{1,0:T(8,128)(2,1)}, bf16[256,1536]{1,0:T(8,128)(2,1)S(1)}, u32[]{:S(2)}, u32[]{:S(2)}) collective-permute-start(bf16[256,1536]{1,0:T(8,128)(2,1)} %get-tuple-element.563.rest_0_), channel_id=1, source_target_pairs={{0,1},{1,0},{2,3},{3,2},{4,5},{5,4},{6,7},{7,6},{8,9},{9,8},{10,11... | collective-permute-start | bytes 2359304 | tf_op jit(solution)/shard_map/ppermute | solution.py:814
  282.9 24.2 %collective-permute-start.48 = (bf16[768,1536]{1,0:T(8,128)(2,1)}, bf16[768,1536]{1,0:T(8,128)(2,1)S(1)}, u32[]{:S(2)}, u32[]{:S(2)}) collective-permute-start(bf16[768,1536]{1,0:T(8,128)(2,1)} %get-tuple-element.546), channel_id=1, source_target_pairs={{0,1},{1,0},{2,3},{3,2},{4,5},{5,4},{6,7},{7,6},{8,9},{9,8},{10,11... | collective-permute-start | bytes 7077896 | tf_op jit(solution)/shard_map/ppermute | solution.py:814
  283.0 24.1 %collective-permute-start.44 = (bf16[256,1536]{1,0:T(8,128)(2,1)}, bf16[256,1536]{1,0:T(8,128)(2,1)}, u32[]{:S(2)}, u32[]{:S(2)}) collective-permute-start(bf16[256,1536]{1,0:T(8,128)(2,1)} %adds.13), channel_id=1, source_target_pairs={{0,2},{1,3},{2,0},{3,1},{4,6},{5,7},{6,4},{7,5},{8,10},{9,11},{10,... | collective-permute-start | bytes 2359304 | tf_op jit(solution)/shard_map/ppermute | solution.py:814
  284.4 22.8 %collective-permute-start.45 = (bf16[256,1536]{1,0:T(8,128)(2,1)}, bf16[256,1536]{1,0:T(8,128)(2,1)}, u32[]{:S(2)}, u32[]{:S(2)}) collective-permute-start(bf16[256,1536]{1,0:T(8,128)(2,1)} %get-tuple-element.540), channel_id=1, source_target_pairs={{0,4},{4,0},{8,12},{12,8},{16,20},{20,16},{24,28},{28,24},{1,5},{5... | collective-permute-start | bytes 2359304 | tf_op jit(solution)/shard_map/ppermute | solution.py:814
  285.0 22.1 %collective-permute-start.47 = (bf16[256,1536]{1,0:T(8,128)(2,1)}, bf16[256,1536]{1,0:T(8,128)(2,1)S(1)}, u32[]{:S(2)}, u32[]{:S(2)}) collective-permute-start(bf16[256,1536]{1,0:T(8,128)(2,1)} %adds.15), channel_id=1, source_target_pairs={{0,8},{4,12},{8,16},{12,20},{16,24},{20,28},{24,0},{28,4},{1,9},{5... | collective-permute-start | bytes 2359304 | tf_op jit(solution)/shard_map/ppermute | solution.py:823
  307.2 40.9 %collective-permute-start.50 = (bf16[288,1536]{1,0:T(8,128)(2,1)}, bf16[288,1536]{1,0:T(8,128)(2,1)}, u32[]{:S(2)}, u32[]{:S(2)}) collective-permute-start(bf16[288,1536]{1,0:T(8,128)(2,1)} %get-tuple-element.558), channel_id=1, source_target_pairs={{0,4},{4,0},{8,12},{12,8},{16,20},{20,16},{24,28},{28,24},{1,5},{5... | collective-permute-start | bytes 2654216 | tf_op jit(solution)/shard_map/ppermute | solution.py:814
  308.6 39.4 %collective-permute-start.52 = (bf16[256,1536]{1,0:T(8,128)(2,1)}, bf16[256,1536]{1,0:T(8,128)(2,1)S(1)}, u32[]{:S(2)}, u32[]{:S(2)}) collective-permute-start(bf16[256,1536]{1,0:T(8,128)(2,1)} %get-tuple-element.560), channel_id=1, source_target_pairs={{0,2},{1,3},{2,0},{3,1},{4,6},{5,7},{6,4},{7,5},{8,10},{9,11},{10,... | collective-permute-start | bytes 2359304 | tf_op jit(solution)/shard_map/ppermute | solution.py:814
  312.9 35.1 %collective-permute-start.49 = (bf16[256,1536]{1,0:T(8,128)(2,1)}, bf16[256,1536]{1,0:T(8,128)(2,1)S(1)}, u32[]{:S(2)}, u32[]{:S(2)}) collective-permute-start(bf16[256,1536]{1,0:T(8,128)(2,1)} %get-tuple-element.557), channel_id=1, source_target_pairs={{0,2},{1,3},{2,0},{3,1},{4,6},{5,7},{6,4},{7,5},{8,10},{9,11},{10,... | collective-permute-start | bytes 2359304 | tf_op jit(solution)/shard_map/ppermute | solution.py:814
  314.2 33.8 %collective-permute-start.51 = (bf16[256,1536]{1,0:T(8,128)(2,1)}, bf16[256,1536]{1,0:T(8,128)(2,1)}, u32[]{:S(2)}, u32[]{:S(2)}) collective-permute-start(bf16[256,1536]{1,0:T(8,128)(2,1)} %get-tuple-element.559), channel_id=1, source_target_pairs={{0,8},{4,12},{8,16},{12,20},{16,24},{20,28},{24,0},{28,4},{1,9},{5... | collective-permute-start | bytes 2359304 | tf_op jit(solution)/shard_map/ppermute | solution.py:823
  315.7 32.4 %collective-permute-start.53 = (bf16[256,1536]{1,0:T(8,128)(2,1)}, bf16[256,1536]{1,0:T(8,128)(2,1)}, u32[]{:S(2)}, u32[]{:S(2)}) collective-permute-start(bf16[256,1536]{1,0:T(8,128)(2,1)} %get-tuple-element.561), channel_id=1, source_target_pairs={{0,4},{4,0},{8,12},{12,8},{16,20},{20,16},{24,28},{28,24},{1,5},{5... | collective-permute-start | bytes 2359304 | tf_op jit(solution)/shard_map/ppermute | solution.py:814
  354.9 22.8 %collective-permute-start.57 = (bf16[288,1536]{1,0:T(8,128)(2,1)}, bf16[288,1536]{1,0:T(8,128)(2,1)S(1)}, u32[]{:S(2)}, u32[]{:S(2)}) collective-permute-start(bf16[288,1536]{1,0:T(8,128)(2,1)} %dynamic_update_slice.28), channel_id=1, source_target_pairs={{0,4},{4,0},{8,12},{12,8},{16,20},{20,16},{24,28},{28,24},{1,5},{5... | collective-permute-start | bytes 2654216 | tf_op jit(solution)/shard_map/ppermute | solution.py:814
  367.2 26.4 %collective-permute-start.63 = (bf16[256,1536]{1,0:T(8,128)(2,1)}, bf16[256,1536]{1,0:T(8,128)(2,1)S(1)}, u32[]{:S(2)}, u32[]{:S(2)}) collective-permute-start(bf16[256,1536]{1,0:T(8,128)(2,1)} %get-tuple-element.604), channel_id=1, source_target_pairs={{0,4},{4,0},{8,12},{12,8},{16,20},{20,16},{24,28},{28,24},{1,5},{5... | collective-permute-start | bytes 2359304 | tf_op jit(solution)/shard_map/ppermute | solution.py:814
  381.1 24.4 %collective-permute-start.62 = (bf16[256,1536]{1,0:T(8,128)(2,1)S(1)}, bf16[256,1536]{1,0:T(8,128)(2,1)S(1)}, u32[]{:S(2)}, u32[]{:S(2)}) collective-permute-start(bf16[256,1536]{1,0:T(8,128)(2,1)S(1)} %fusion.7.refs_0_), channel_id=1, source_target_pairs={{0,2},{1,3},{2,0},{3,1},{4,6},{5,7},{6,4},{7,5},{8,10},{9,11},{10,... | collective-permute-start | bytes 2359304 | tf_op jit(solution)/shard_map/ppermute | solution.py:814
  409.3 23.5 %collective-permute-start.68 = (bf16[288,1536]{1,0:T(8,128)(2,1)}, bf16[288,1536]{1,0:T(8,128)(2,1)S(1)}, u32[]{:S(2)}, u32[]{:S(2)}) collective-permute-start(bf16[288,1536]{1,0:T(8,128)(2,1)} %fusion.9), channel_id=1, source_target_pairs={{0,2},{1,3},{2,0},{3,1},{4,6},{5,7},{6,4},{7,5},{8,10},{9,11},{10,... | collective-permute-start | bytes 2654216 | tf_op jit(solution)/shard_map/ppermute | solution.py:814
  410.0 22.8 %collective-permute-start.69 = (bf16[288,1536]{1,0:T(8,128)(2,1)}, bf16[288,1536]{1,0:T(8,128)(2,1)S(1)}, u32[]{:S(2)}, u32[]{:S(2)}) collective-permute-start(bf16[288,1536]{1,0:T(8,128)(2,1)} %fusion.9), channel_id=1, source_target_pairs={{0,1},{1,0},{2,3},{3,2},{4,5},{5,4},{6,7},{7,6},{8,9},{9,8},{10,11... | collective-permute-start | bytes 2654216 | tf_op jit(solution)/shard_map/ppermute | solution.py:814
  434.9 22.1 %collective-permute-start.73 = (bf16[64,1536]{1,0:T(8,128)(2,1)S(1)}, bf16[64,1536]{1,0:T(8,128)(2,1)}, u32[]{:S(2)}, u32[]{:S(2)}) collective-permute-start(bf16[64,1536]{1,0:T(8,128)(2,1)S(1)} %add_convert_fusion.3), channel_id=1, source_target_pairs={{0,8},{4,12},{8,16},{12,20},{16,24},{20,28},{24,0},{28,4},{1,9},{5... | collective-permute-start | bytes 589832 | tf_op jit(solution)/shard_map/ppermute | solution.py:899
  (125 other events, 1191.9 us)
